TPU v7x, 256 devices: a whole 4x4x8 slice. The times are simulated.
256 devices in a mesh: sy: 16 (over y, z_lo), sx: 8 (over x, core), fr: 2 (over z_hi).
Axes of the slice: x: 4, y: 4, z: 8 (z_hi: 2, z_lo: 4; z = z_hi * 4 + z_lo), core: 2. Of those that a mesh axis runs over, the one named last changes fastest.
Arguments:
- object_field: float32 [2048, 4096], P('sy', 'sx'), may hold values from 0.5 to 15
- frames_data: float32 [2, 2048, 4096], P('fr', 'sy', 'sx'), may hold values from 0.4 to 16
- patch_psfs: float32 [2, 16, 32, 128, 128], P('fr', 'sy', 'sx'), may hold values from 0 to 0.80009155
Outputs:
- gradient: float32 [2048, 4096], P('sy', 'sx')
- residual: float32 [2, 2048, 4096], P('fr', 'sy', 'sx')
All inputs are finite; a program needn't handle non-finite values.
Results may differ from a plain program's by a relative error of at most 0.0003.
Values sent between devices are 32-bit elements; how exact they have to be, the bound alone decides.
No kernel may reach another device: no remote copies, remote signals or barrier semaphores. Data moves between devices by JAX's collectives and lax.ppermute only.
A program may use at most 128 MiB of HBM per device.

v0:
```python
import math

import jax
import jax.numpy as jnp
from jax import lax
from jax.sharding import PartitionSpec as P


def passed_along(value, axis, steps):
    count = lax.axis_size(axis)
    leading, last = (max(0, -steps), min(count, count - steps))
    return lax.ppermute(value, axis, [(source, source + steps) for source in range(leading, last)])


def padded_2(block, sides, width):
    for axis, dim in sides:
        count = lax.axis_size(axis)
        forward = [(i, i + 1) for i in range(count - 1)]
        backward = [(target, source) for source, target in forward]
        low = lax.ppermute(
            lax.slice_in_dim(block, block.shape[dim] - width, None, axis=dim), axis, forward
        )
        high = lax.ppermute(lax.slice_in_dim(block, 0, width, axis=dim), axis, backward)
        block = jnp.concatenate([low, block, high], axis=dim)
    return block


def window_table(patch_size):
    position = lax.broadcasted_iota(jnp.float32, (patch_size,), 0)
    edge = jnp.sin(jnp.pi * (position + 0.5) / patch_size) ** 2
    return edge[:, None] * edge[None, :]


def cut_windows(field, stride, count_y, count_x, span_blocks):
    blocks = field.reshape(count_y + span_blocks - 1, stride, count_x + span_blocks - 1, stride)
    stacked = jnp.stack([blocks[a : a + count_y] for a in range(span_blocks)], axis=1)
    both = jnp.stack([stacked[:, :, :, b : b + count_x] for b in range(span_blocks)], axis=4)
    side = span_blocks * stride
    return both.transpose(0, 3, 1, 2, 4, 5).reshape(count_y, count_x, side, side)


def spread(pieces, stride):
    count_y, count_x = (pieces.shape[0], pieces.shape[1])
    blocks = pieces.reshape(count_y, count_x, 3, stride, 3, stride)
    summed = jnp.zeros((count_y + 2, stride, count_x + 2, stride), pieces.dtype)
    for a in range(3):
        for b in range(3):
            placed = blocks[:, :, a, :, b, :].transpose(0, 2, 1, 3)
            summed = summed + jnp.pad(placed, ((a, 2 - a), (0, 0), (b, 2 - b), (0, 0)))
    return summed.reshape((count_y + 2) * stride, (count_x + 2) * stride)


def angle_tables(length, out_size):
    frequency = lax.broadcasted_iota(jnp.int32, (length, out_size), 0)
    position = lax.broadcasted_iota(jnp.int32, (length, out_size), 1)
    phases = (frequency * position % length).astype(jnp.float32) * (2.0 * math.pi / length)
    return (jnp.cos(phases), jnp.sin(phases))


def contract(pattern, first_op, second_op):
    return jnp.einsum(pattern, first_op, second_op, precision=lax.Precision.HIGHEST)


def forward_transform(values, length):
    cos_in, sin_in = angle_tables(length, values.shape[-1])
    half_re = contract("pab,kb->pak", values, cos_in)
    half_im = -contract("pab,kb->pak", values, sin_in)
    cos_out, sin_out = angle_tables(length, values.shape[-2])
    real_part = contract("ka,pal->pkl", cos_out, half_re) + contract(
        "ka,pal->pkl", sin_out, half_im
    )
    imag_part = contract("ka,pal->pkl", cos_out, half_im) - contract(
        "ka,pal->pkl", sin_out, half_re
    )
    return (real_part, imag_part)


def inverse_transform(real_part, imag_part, out_size):
    length = real_part.shape[-1]
    cos_t, sin_t = angle_tables(length, out_size)
    mid_re = contract("pkl,lv->pkv", real_part, cos_t) - contract("pkl,lv->pkv", imag_part, sin_t)
    mid_im = contract("pkl,lv->pkv", real_part, sin_t) + contract("pkl,lv->pkv", imag_part, cos_t)
    result = contract("ku,pkv->puv", cos_t, mid_re) - contract("ku,pkv->puv", sin_t, mid_im)
    return result / (length * length)


def fold_rows(spilled, stride):
    from_above = passed_along(spilled[-stride:], "sy", 1)
    from_below = passed_along(spilled[:stride], "sy", -1)
    middle = spilled[stride:-stride]
    return middle + from_above + from_below


def fold_columns(spilled, stride):
    from_left = passed_along(spilled[:, -stride:], "sx", 1)
    from_right = passed_along(spilled[:, :stride], "sx", -1)
    middle = spilled[:, stride:-stride]
    width = middle.shape[1]
    return (
        middle
        + jnp.pad(from_left, ((0, 0), (0, width - stride)))
        + jnp.pad(from_right, ((0, 0), (width - stride, 0)))
    )


def fold(spilled, stride):
    return fold_columns(fold_rows(spilled, stride), stride)


def flux_totals(data_sum, model_sum):
    return lax.psum((data_sum, model_sum), ("sy", "sx"))


def per_device(object_field, frames_data, patch_psfs):
    stride = patch_psfs.shape[-1]
    half = stride // 2
    length = 3 * stride
    patch_size = 2 * stride
    tile_rows, tile_columns = object_field.shape
    count_y, count_x = (tile_rows // stride, tile_columns // stride)
    patches = count_y * count_x
    window = window_table(patch_size)
    padded = padded_2(object_field, (("sy", 0), ("sx", 1)), half)
    pieces = cut_windows(padded, stride, count_y, count_x, 2) * window
    piece_re, piece_im = forward_transform(pieces.reshape(patches, patch_size, patch_size), length)
    psf_re, psf_im = forward_transform(patch_psfs.reshape(patches, stride, stride), length)
    blurred = inverse_transform(
        piece_re * psf_re - piece_im * psf_im, piece_re * psf_im + piece_im * psf_re, length
    )
    spilled = spread(blurred.reshape(count_y, count_x, length, length), stride)
    observed = frames_data[0]
    data_sum = jnp.sum(observed)
    model_tile = fold(spilled, stride)
    data_total, model_total = flux_totals(data_sum, jnp.sum(model_tile))
    frame_gain = data_total / model_total
    residual = frame_gain * model_tile - observed
    beside_all = padded_2(residual, (("sy", 0), ("sx", 1)), stride)
    windows = cut_windows(beside_all, stride, count_y, count_x, 3).reshape(patches, length, length)
    res_re, res_im = forward_transform(windows, length)
    adjoint = inverse_transform(
        res_re * psf_re + res_im * psf_im, res_im * psf_re - res_re * psf_im, patch_size
    )
    shares = frame_gain * window * adjoint.reshape(count_y, count_x, patch_size, patch_size)
    shares = jnp.pad(shares, ((0, 0), (0, 0), (half, half), (half, half)))
    frame_grad = fold(spread(shares, stride), stride)
    gradient = lax.psum(frame_grad, "fr")
    return (gradient, residual[None])


def solution(mesh):
    placed = (P("sy", "sx"), P("fr", "sy", "sx"), P("fr", "sy", "sx", None, None))
    return jax.shard_map(
        per_device,
        mesh=mesh,
        in_specs=placed,
        out_specs=(P("sy", "sx"), P("fr", "sy", "sx")),
        check_vma=False,
    )
```

profile of v0, /device:TPU:1, one launch (start us, length us, event | category | flops | bytes accessed | tf_op | source)
XLA Modules:
  0.0 687.6 jit_solution(3198152524753815777)
XLA Ops:
  8.5 4.4 collective-permute-start
  25.6 4.8 convolution_subtract_fusion
  47.9 4.3 fusion.50
  55.6 4.2 fusion.107
  59.8 6.8 fusion.105
  66.6 6.9 %convolution_add_fusion.1 = f32[4,384,384]{2,1,0:T(8,128)S(1)} fusion(f32[4,384,384]{2,1,0:T(8,128)S(1)} %fusion.107, f32[4,256,384]{2,1,0:T(8,128)S(1)} %convolution_negate_fusion), kind=kOutput, calls=%fused_computation.35 | convolution fusion | flops 1813413888 | bytes 6291456 | tf_op jit(solution)/shard_map/ka,pal->pkl/dot_general | solution.py:61
  73.5 4.6 multiply_add_fusion.1
  78.1 7.5 %fusion.8 = f32[4,384,384]{2,1,0:T(8,128)S(1)} fusion(f32[4,384,384]{2,1,0:T(8,128)S(1)} %get-tuple-element.10), kind=kOutput, calls=%fused_computation.9 | convolution fusion | flops 2719236096 | bytes 4718592 | tf_op jit(solution)/shard_map/pkl,lv->pkv/dot_general | solution.py:61
  85.6 7.1 %fusion.10 = f32[4,384,384]{2,1,0:T(8,128)S(1)} fusion(f32[4,384,384]{2,1,0:T(8,128)S(1)} %get-tuple-element.10), kind=kOutput, calls=%fused_computation.11 | convolution fusion | flops 2719236096 | bytes 4718592 | tf_op jit(solution)/shard_map/pkl,lv->pkv/dot_general | solution.py:61
  92.7 7.3 %fusion.12 = f32[4,384,384]{2,1,0:T(8,128)S(1)} fusion(f32[4,384,384]{2,1,0:T(8,128)S(1)} %get-tuple-element.11), kind=kOutput, calls=%fused_computation.13 | convolution fusion | flops 2719236096 | bytes 4718592 | tf_op jit(solution)/shard_map/pkl,lv->pkv/dot_general | solution.py:61
  100.0 6.7 fusion.14
  106.6 7.5 %fusion.16 = f32[4,384,384]{2,1,0:T(8,128)S(1)} fusion(f32[4,384,384]{2,1,0:T(8,128)S(1)} %fusion.12, f32[4,384,384]{2,1,0:T(8,128)S(1)} %fusion.8), kind=kOutput, calls=%fused_computation.20 | convolution fusion | flops 2719825920 | bytes 7077888 | tf_op jit(solution)/shard_map/ku,pkv->puv/dot_general | solution.py:61
  114.2 6.9 multiply_bitcast_fusion
  128.7 4.3 collective-permute-start.4
  134.7 5.3 collective-permute-done.4
  140.0 12.7 %collective-permute-done.5 = f32[128,768]{0,1:T(8,128)S(1)} collective-permute-done((f32[128,768]{0,1:T(8,128)S(1)}, f32[128,768]{0,1:T(8,128)S(1)}, u32[]{:S(2)}, u32[]{:S(2)}) %collective-permute-start.5) | collective-permute-done | bytes 393248 | tf_op jit(solution)/shard_map/ppermute | solution.py:12
  152.8 4.3 collective-permute-start.6
  163.5 330.8 %all-reduce.23 = (f32[]{:T(128)}, f32[]{:T(128)}) all-reduce(f32[]{:T(128)} %reduce_sum.18, f32[]{:T(128)} %fusion.224), channel_id=1, replica_groups=mesh['sy'=16,'sx'=8,'fr'=2] {'sy','sx'}, use_global_device_ids=true, to_apply=%region_1.2 | all-reduce | flops 2 | bytes 16 | tf_op jit(solution)/shard_map/psum | solution.py:111
  506.0 6.1 collective-permute-start.11
  520.8 6.2 fusion.65
  527.0 7.3 %fusion.57 = f32[4,384,384]{2,1,0:T(8,128)S(1)} fusion(f32[4,384,384]{2,1,0:T(8,128)S(1)} %reshape_reshape.7), kind=kOutput, calls=%fused_computation.69 | convolution fusion | flops 2719236096 | bytes 4718592 | tf_op jit(solution)/shard_map/pab,kb->pak/dot_general | solution.py:61
  534.2 7.1 %fusion.54 = f32[4,384,384]{2,1,0:T(8,128)S(1)} fusion(f32[4,384,384]{1,2,0:T(8,128)S(1)} %fusion.65), kind=kOutput, calls=%fused_computation.66 | convolution fusion | flops 2719236096 | bytes 4718592 | tf_op jit(solution)/shard_map/ka,pal->pkl/dot_general | solution.py:61
  541.3 7.5 %fusion.63 = f32[4,384,384]{2,1,0:T(8,128)S(1)} fusion(f32[4,384,384]{1,2,0:T(8,128)S(1)} %fusion.65), kind=kOutput, calls=%fused_computation.75 | convolution fusion | flops 2719236096 | bytes 4718592 | tf_op jit(solution)/shard_map/ka,pal->pkl/dot_general | solution.py:61
  548.8 10.1 %fusion.27 = f32[4,384,384]{2,1,0:T(8,128)S(1)} fusion(f32[4,384,384]{2,1,0:T(8,128)S(1)} %fusion.54, f32[4,384,384]{2,1,0:T(8,128)S(1)} %fusion.57), kind=kOutput, calls=%fused_computation.31 | convolution fusion | flops 2720415744 | bytes 7077888 | tf_op jit(solution)/shard_map/ka,pal->pkl/dot_general | solution.py:61
  558.9 10.4 %multiply_subtract_fusion = (f32[4,384,384]{2,1,0:T(8,128)S(1)}, f32[4,384,384]{2,1,0:T(8,128)S(1)}) fusion(f32[4,384,384]{2,1,0:T(8,128)S(1)} %copy-done.5, f32[4,384,384]{2,1,0:T(8,128)S(1)} %fusion.27, f32[4,384,384]{2,1,0:T(8,128)S(1)} %copy-done.3, f32[4,384,384]{2,1,0:T(8,128)S(1)} %fusion.63, f32[4,384,384]{2,1,0:T(8,128)S(1)} %fusion.57), kind=kOutput, calls=%fused_computation.17 | convolution fusion | flops 2723954688 | bytes 16515072 | tf_op jit(solution)/shard_map/ka,pal->pkl/dot_general | solution.py:61
  569.3 5.6 fusion
  574.9 5.5 fusion.2
  580.4 5.9 fusion.4
  586.3 5.4 fusion.6
  591.7 4.2 fusion.32
  611.1 6.6 collective-permute-done.12
  630.9 47.9 %all-reduce.26.cloned.1.call-done = f32[128,512]{0,1:T(8,128)} async-done(((f32[128,512]{0,1:T(8,128)}), f32[128,512]{0,1:T(8,128)}) %all-reduce.26.cloned.1.call-update) | async-done | bytes 262160 | tf_op jit(solution)/shard_map/psum | solution.py:146
  (103 shorter events, 99.4 us)
Async XLA Ops:
  7.2 7.0 %copy-start = (f32[1,1,4,128,128]{4,3,2,1,0:T(8,128)S(1)}, f32[1,1,4,128,128]{4,3,2,1,0:T(8,128)}, u32[]{:S(2)}) copy-start(f32[1,1,4,128,128]{4,3,2,1,0:T(8,128)} %param.5) | copy-start | bytes 786436
  7.2 671.6 %all-reduce.26.cloned.1.call-start = ((), (), s32[]{:S(2)}) async-start(), calls=%async_computation | async-start | bytes 524288 | tf_op jit(solution)/shard_map/psum | solution.py:146
  8.5 21.9 %collective-permute-start = (f32[64,512]{0,1:T(8,128)S(1)}, f32[64,512]{0,1:T(8,128)S(1)}, u32[]{:S(2)}, u32[]{:S(2)}) collective-permute-start(f32[64,512]{0,1:T(8,128)S(1)} %get-tuple-element.54), channel_id=1, source_target_pairs={{0,16},{16,32},{32,48},{48,64},{64,80},{80,96},{96,112},{112,128},... | collective-permute-start | bytes 393224 | tf_op jit(solution)/shard_map/ppermute | solution.py:20
  12.9 17.6 %collective-permute-start.1 = (f32[64,512]{0,1:T(8,128)S(1)}, f32[64,512]{0,1:T(8,128)S(1)}, u32[]{:S(2)}, u32[]{:S(2)}) collective-permute-start(f32[64,512]{0,1:T(8,128)S(1)} %get-tuple-element.55), channel_id=1, source_target_pairs={{16,0},{32,16},{48,32},{64,48},{80,64},{96,80},{112,96},{128,112},... | collective-permute-start | bytes 393224 | tf_op jit(solution)/shard_map/ppermute | solution.py:23
  25.6 47.9 %copy-start.2 = (f32[4,384,384]{2,1,0:T(8,128)}, f32[4,384,384]{2,1,0:T(8,128)S(1)}, u32[]{:S(2)}) copy-start(f32[4,384,384]{2,1,0:T(8,128)S(1)} %convolution_add_fusion) | copy-start | bytes 7077892
  30.6 7.8 %collective-permute-start.2 = (f32[256,64]{0,1:T(8,128)S(1)}, f32[256,64]{0,1:T(8,128)}, u32[]{:S(2)}, u32[]{:S(2)}) collective-permute-start(f32[256,64]{0,1:T(8,128)S(1)} %get-tuple-element.44), channel_id=1, source_target_pairs={{0,2},{2,4},{4,6},{6,8},{8,10},{10,12},{12,14},{1,3},{3,5},{5,7},{... | collective-permute-start | bytes 196616 | tf_op jit(solution)/shard_map/ppermute | solution.py:20
  34.5 5.7 collective-permute-start.3
  47.9 4.3 copy-start.6
  66.6 6.9 %copy-start.4 = (f32[4,384,384]{2,1,0:T(8,128)S(1)}, f32[4,384,384]{2,1,0:T(8,128)}, u32[]{:S(2)}) copy-start(f32[4,384,384]{2,1,0:T(8,128)} %convolution_subtract_fusion) | copy-start | bytes 7077892
  128.5 30.5 %copy-start.9 = (f32[1,128,512]{2,1,0:T(8,128)S(1)}, f32[1,128,512]{2,1,0:T(8,128)}, u32[]{:S(2)}) copy-start(f32[1,128,512]{2,1,0:T(8,128)} %param.4) | copy-start | bytes 786436
  128.7 11.2 %collective-permute-start.4 = (f32[128,768]{0,1:T(8,128)S(1)}, f32[128,768]{0,1:T(8,128)S(1)}, u32[]{:S(2)}, u32[]{:S(2)}) collective-permute-start(f32[128,768]{0,1:T(8,128)S(1)} %bitcast.267), channel_id=1, source_target_pairs={{0,16},{16,32},{32,48},{48,64},{64,80},{80,96},{96,112},{112,128},... | collective-permute-start | bytes 1179656 | tf_op jit(solution)/shard_map/ppermute | solution.py:12
  133.2 19.5 %collective-permute-start.5 = (f32[128,768]{0,1:T(8,128)S(1)}, f32[128,768]{0,1:T(8,128)S(1)}, u32[]{:S(2)}, u32[]{:S(2)}) collective-permute-start(f32[128,768]{0,1:T(8,128)S(1)} %bitcast.269), channel_id=1, source_target_pairs={{16,0},{32,16},{48,32},{64,48},{80,64},{96,80},{112,96},{128,112},... | collective-permute-start | bytes 1179656 | tf_op jit(solution)/shard_map/ppermute | solution.py:12
  152.8 6.9 %collective-permute-start.6 = (f32[128,128]{0,1:T(8,128)S(1)}, f32[128,128]{0,1:T(8,128)S(1)}, u32[]{:S(2)}, u32[]{:S(2)}) collective-permute-start(f32[128,128]{0,1:T(8,128)S(1)} %get-tuple-element.52), channel_id=1, source_target_pairs={{0,2},{2,4},{4,6},{6,8},{8,10},{10,12},{12,14},{1,3},{3,5},{5,7},{... | collective-permute-start | bytes 196616 | tf_op jit(solution)/shard_map/ppermute | solution.py:12
  157.1 5.6 collective-permute-start.7
  495.6 17.8 %copy-start.7 = (f32[128,512]{0,1:T(8,128)}, f32[128,512]{0,1:T(8,128)S(1)}, u32[]{:S(2)}) copy-start(f32[128,512]{0,1:T(8,128)S(1)} %bitcast_subtract_fusion) | copy-start | bytes 786436
  495.6 4.6 collective-permute-start.8
  496.9 7.1 %collective-permute-start.9 = (f32[128,512]{0,1:T(8,128)S(1)}, f32[128,512]{0,1:T(8,128)S(1)}, u32[]{:S(2)}, u32[]{:S(2)}) collective-permute-start(f32[128,512]{0,1:T(8,128)S(1)} %bitcast_subtract_fusion), channel_id=1, source_target_pairs={{16,0},{32,16},{48,32},{64,48},{80,64},{96,80},{112,96},{128,112},... | collective-permute-start | bytes 786440 | tf_op jit(solution)/shard_map/ppermute | solution.py:23
  504.1 8.2 %collective-permute-start.10 = (f32[384,128]{0,1:T(8,128)S(1)}, f32[384,128]{0,1:T(8,128)S(1)}, u32[]{:S(2)}, u32[]{:S(2)}) collective-permute-start(f32[384,128]{0,1:T(8,128)S(1)} %get-tuple-element.42), channel_id=1, source_target_pairs={{0,2},{2,4},{4,6},{6,8},{8,10},{10,12},{12,14},{1,3},{3,5},{5,7},{... | collective-permute-start | bytes 589832 | tf_op jit(solution)/shard_map/ppermute | solution.py:20
  506.0 7.2 %collective-permute-start.11 = (f32[384,128]{0,1:T(8,128)S(1)}, f32[384,128]{0,1:T(8,128)S(1)}, u32[]{:S(2)}, u32[]{:S(2)}) collective-permute-start(f32[384,128]{0,1:T(8,128)S(1)} %get-tuple-element.43), channel_id=1, source_target_pairs={{2,0},{4,2},{6,4},{8,6},{10,8},{12,10},{14,12},{3,1},{5,3},{7,5},{... | collective-permute-start | bytes 589832 | tf_op jit(solution)/shard_map/ppermute | solution.py:23
  548.8 10.1 %copy-start.3 = (f32[4,384,384]{2,1,0:T(8,128)S(1)}, f32[4,384,384]{2,1,0:T(8,128)}, u32[]{:S(2)}) copy-start(f32[4,384,384]{2,1,0:T(8,128)} %copy-done.2) | copy-start | bytes 7077892
  548.8 10.1 %copy-start.5 = (f32[4,384,384]{2,1,0:T(8,128)S(1)}, f32[4,384,384]{2,1,0:T(8,128)}, u32[]{:S(2)}) copy-start(f32[4,384,384]{2,1,0:T(8,128)} %convolution_subtract_fusion) | copy-start | bytes 7077892
  608.0 22.0 %copy-start.8 = (f32[128,512]{0,1:T(8,128)S(1)}, f32[128,512]{0,1:T(8,128)}, u32[]{:S(2)}) copy-start(f32[128,512]{0,1:T(8,128)} %copy-done.7) | copy-start | bytes 786436
  608.0 9.7 %collective-permute-start.12 = (f32[128,768]{0,1:T(8,128)S(1)}, f32[128,768]{0,1:T(8,128)S(1)}, u32[]{:S(2)}, u32[]{:S(2)}) collective-permute-start(f32[128,768]{0,1:T(8,128)S(1)} %bitcast.268), channel_id=1, source_target_pairs={{0,16},{16,32},{32,48},{48,64},{64,80},{80,96},{96,112},{112,128},... | collective-permute-start | bytes 1179656 | tf_op jit(solution)/shard_map/ppermute | solution.py:12
  609.5 71.1 %copy-start.1 = (f32[1,1,4,128,128]{4,3,2,1,0:T(8,128)S(1)}, f32[1,1,4,128,128]{4,3,2,1,0:T(8,128)}, u32[]{:S(2)}) copy-start(f32[1,1,4,128,128]{4,3,2,1,0:T(8,128)} %param.5) | copy-start | bytes 786436
  609.6 12.0 %collective-permute-start.13 = (f32[128,768]{0,1:T(8,128)S(1)}, f32[128,768]{0,1:T(8,128)S(1)}, u32[]{:S(2)}, u32[]{:S(2)}) collective-permute-start(f32[128,768]{0,1:T(8,128)S(1)} %bitcast.270), channel_id=1, source_target_pairs={{16,0},{32,16},{48,32},{64,48},{80,64},{96,80},{112,96},{128,112},... | collective-permute-start | bytes 1179656 | tf_op jit(solution)/shard_map/ppermute | solution.py:12
  621.8 4.6 collective-permute-start.14
  623.7 5.6 collective-permute-start.15
Sparse Core Ops, SparseCore 0:
  630.2 48.5 all-reduce.25
where the time goes:
time: 697 us; the launch traced here: 688 us
  blocking collectives  331 us (47%)
  matrix products  168 us (24%)
  waiting for transfers between devices  91 us (13%)
  starting transfers between devices  41.4 us (6%)
  local copies, waits for them, and re-layouts  33.5 us (5%)
  between operations  16.3 us (2%)
    psum x1, blocking collectives, flux_totals(): return lax.psum((data_sum, model_sum), ('sy', 'sx'))  331 us
    dot_general x30, matrix products, contract(): jnp.einsum(pattern, first_op, second_op, precision=lax.Precision.HIGHEST)  168 us
    psum x1, waiting for transfers between devices, per_device(): gradient = lax.psum(frame_grad, 'fr')  47.9 us
    ppermute x8, waiting for transfers between devices, passed_along(): lax.ppermute(value, axis, [(source, source + steps) for source in range(l...  34.5 us
    ppermute x8, starting transfers between devices, passed_along(): lax.ppermute(value, axis, [(source, source + steps) for source in range(l...  19.1 us
  transfers between devices with their start and end apart: 17, of which 11 were waited for; matrix products, arithmetic and copies ran while one was open for 3% of the time, Pallas kernels for 0%

commit v1 on v0

v1 whole, which is shorter than its diff:
```python
import functools
import math

import jax
import jax.numpy as jnp
import numpy as np
from jax import lax
from jax.experimental import pallas as pl
from jax.experimental.pallas import tpu as pltpu
from jax.sharding import PartitionSpec as P

S = 128
L = 256
H = 64
F32 = jnp.float32
BF16 = jnp.bfloat16


def half_windows():
    n = np.arange(L, dtype=np.float64)
    s = np.sin(np.pi * (n + 0.5) / L) ** 2
    return s[:S], s[S:]


def phases(freqs, positions):
    product = (2 * np.arange(freqs)[:, None] + 1) * positions[None, :] % (2 * L)
    angle = product.astype(np.float64) * (math.pi / L)
    return np.cos(angle), np.sin(angle)


def forward_left(positions):
    c, s = phases(L, positions)
    return np.block([[c, s], [-s, c]])


def inverse_left(positions):
    c, s = phases(L, positions)
    return np.block([[c.T, -s.T], [s.T, c.T]]) / L


def forward_right(positions):
    c, s = phases(S, positions)
    return np.concatenate([c.T, -s.T], axis=1)


def inverse_right(positions):
    c, s = phases(S, positions)
    return np.concatenate([c, -s], axis=0) * (2.0 / L)


def bf16_parts(table):
    hi = table.astype(np.float32).astype(BF16)
    lo = (table - hi.astype(np.float64)).astype(np.float32).astype(BF16)
    return hi, lo


def left_table(table):
    hi, lo = bf16_parts(table)
    return np.concatenate([hi, hi, lo], axis=-1)


def right_table(table):
    hi, lo = bf16_parts(table)
    return np.concatenate([hi, hi, lo], axis=-2)


@functools.lru_cache(maxsize=1)
def tables():
    near, far = np.arange(S), np.arange(S, L)
    up, down = half_windows()
    first_half = near < H
    t = {}
    t["psf_right"] = right_table(forward_right(near))
    t["psf_left"] = left_table(forward_left(near))
    t["obj_right"] = right_table(
        np.concatenate([up[:, None] * forward_right(near), down[:, None] * forward_right(near)], axis=1)
    )
    rows_forward, rows_inverse = [], []
    for first in (False, True):
        row_up = np.where(first_half & first, 0.0, up)
        row_down = np.where(~first_half & first, 0.0, down)
        base, back = forward_left(near), inverse_left(near)
        rows_forward.append(
            np.concatenate([base * np.tile(w, 2)[None, :] for w in (row_up, row_down)], axis=0)
        )
        rows_inverse.append(
            np.concatenate([np.tile(w, 2)[:, None] * back for w in (row_up, row_down)], axis=1)
        )
    t["obj_left"] = left_table(np.stack(rows_forward))
    t["grad_left"] = left_table(np.stack(rows_inverse))
    t["top_inverse"] = left_table(inverse_left(near))
    t["bottom_inverse"] = left_table(inverse_left(far))
    t["out_right"] = right_table(inverse_right(np.arange(L)))
    t["res_right"] = right_table(forward_right(np.arange(L)))
    t["top_forward"] = left_table(forward_left(near))
    t["bottom_forward"] = left_table(forward_left(far))
    t["grad_right"] = right_table(
        np.concatenate([inverse_right(near) * up[None, :], inverse_right(near) * down[None, :]], axis=0)
    )
    return t


def split(value):
    hi = value.astype(BF16)
    return hi, (value - hi.astype(F32)).astype(BF16)


def times_right(value, table):
    hi, lo = split(value)
    return jnp.dot(jnp.concatenate([hi, lo, hi], axis=1), table, preferred_element_type=F32)


def times_left(table, value):
    hi, lo = split(value)
    return jnp.dot(table, jnp.concatenate([hi, lo, hi], axis=0), preferred_element_type=F32)


def stacked_parts(value):
    return jnp.concatenate([value[:, :S], value[:, S:]], axis=0)


def side_by_side(value):
    half = value.shape[0] // 2
    return jnp.concatenate([value[:half], value[half:]], axis=1)


def psf_spectra(psf_ref, right_ref, left_ref, out_ref):
    right, left = right_ref[...], left_ref[...]
    for j in range(psf_ref.shape[0]):
        lanes = times_right(psf_ref[j], right)
        out_ref[:, j * S : (j + 1) * S] = times_left(left, stacked_parts(lanes))


def units(q, count):
    return [(w, j) for w, j in ((0, q), (1, q - 1)) if 0 <= j < count]


def psf_kernel(psf_ref, frame_ref, right_ref, left_ref, spec_ref, total_ref):
    psf_spectra(psf_ref, right_ref, left_ref, spec_ref)
    total_ref[...] = jnp.full(total_ref.shape, jnp.sum(frame_ref[...]), F32)


def model_kernel(
    flags, above_ref, own_ref, left_ref, right_ref, psf_ref, spec_ref, total_ref,
    psf_right, psf_left, obj_right, obj_left, top_inverse, bottom_inverse, out_right,
    spec_above, spill_left, middle, spill_right, flux_ref, x_ref, spill,
):
    count = psf_ref.shape[0]
    width = own_ref.shape[1]
    alpha = 1.0 - flags[0].astype(F32)
    psf_spectra(psf_ref, psf_right, psf_left, spec_above)
    x_ref[:H] = above_ref[...]
    x_ref[H:] = jnp.concatenate([left_ref[:H], own_ref[:H], right_ref[:H]], axis=1)
    spill[...] = jnp.zeros(spill.shape, F32)
    specs = (spec_ref, spec_above)
    for q in range(count + 1):
        lanes = times_right(x_ref[:, q * S : (q + 1) * S], obj_right[...])
        pieces = jnp.concatenate(
            [stacked_parts(lanes[:, w * L : (w + 1) * L]) for w, _ in units(q, count)], axis=1
        )
        x_spec = times_left(obj_left[...], pieces)
        rows = []
        for r in range(2):
            re, im = 0.0, 0.0
            for u, (_, j) in enumerate(units(q, count)):
                x_re = x_spec[2 * r * L : (2 * r + 1) * L, u * S : (u + 1) * S]
                x_im = x_spec[(2 * r + 1) * L : (2 * r + 2) * L, u * S : (u + 1) * S]
                h_re = specs[r][:L, j * S : (j + 1) * S]
                h_im = specs[r][L:, j * S : (j + 1) * S]
                re = re + (x_re * h_re - x_im * h_im)
                im = im + (x_re * h_im + x_im * h_re)
            rows.append(jnp.concatenate([re, im], axis=0))
        top = times_left(top_inverse[...], rows[1] + alpha * rows[0])
        bottom = times_left(bottom_inverse[...], rows[0] + alpha * rows[1])
        both = jnp.concatenate([side_by_side(top), side_by_side(bottom)], axis=0)
        spill[:, q * S : (q + 2) * S] += times_right(both, out_right[...])
    spill_left[...] = spill[:, :S]
    middle[...] = spill[:, S : S + width]
    spill_right[...] = spill[:, S + width :]
    in_left, in_right = (1.0 - flags[1].astype(F32), 1.0 - flags[2].astype(F32))
    flux = (
        jnp.sum(spill[:, S : S + width])
        + in_left * jnp.sum(spill[:, :S])
        + in_right * jnp.sum(spill[:, S + width :])
    )
    row = lax.broadcasted_iota(jnp.int32, flux_ref.shape, 0)
    flux_ref[...] = jnp.where(row < 4, flux, total_ref[...])


def gradient_kernel(
    flags, top_left, top_middle, top_right, own_left, own_ref, own_right, gain_ref, spec_ref, spec_above,
    res_right, top_forward, bottom_forward, grad_left, grad_right,
    out_left, out_top, out_bottom, out_right, r_ref, grad,
):
    width = own_ref.shape[1]
    count = width // S
    alpha = 1.0 - flags[0].astype(F32)
    r_ref[:S] = jnp.concatenate([top_left[...], top_middle[...], top_right[...]], axis=1)
    r_ref[S:] = jnp.concatenate([own_left[...], own_ref[...], own_right[...]], axis=1)
    specs = (spec_ref, spec_above)
    gain = gain_ref[0, 0]
    for q in range(count + 1):
        lanes = times_right(r_ref[:, q * S : (q + 2) * S], res_right[...])
        top = times_left(top_forward[...], stacked_parts(lanes[:S]))
        bottom = times_left(bottom_forward[...], stacked_parts(lanes[S:]))
        seen = (bottom + alpha * top, top + alpha * bottom)
        columns = []
        for _, j in units(q, count):
            parts = []
            for r in range(2):
                h_re = specs[r][:L, j * S : (j + 1) * S]
                h_im = specs[r][L:, j * S : (j + 1) * S]
                r_re, r_im = seen[r][:L], seen[r][L:]
                parts += [r_re * h_re + r_im * h_im, r_im * h_re - r_re * h_im]
            columns.append(jnp.concatenate(parts, axis=0))
        rows = times_left(grad_left[...], jnp.concatenate(columns, axis=1))
        total = 0.0
        for u, (w, _) in enumerate(units(q, count)):
            table = grad_right[w]
            total = total + times_right(side_by_side(rows[:, u * S : (u + 1) * S]), table)
        grad[:, q * S : (q + 1) * S] = total * gain
    out_left[...] = grad[:, :H]
    out_top[...] = grad[:H, H : H + width]
    out_bottom[...] = grad[H:, H : H + width]
    out_right[...] = grad[:, H + width :]


WHOLE = pl.BlockSpec(memory_space=pltpu.VMEM)
SCALARS = pl.BlockSpec(memory_space=pltpu.SMEM)


def picked(table):
    block = (None,) + table.shape[1:]
    return pl.BlockSpec(block, lambda i, flags: (flags[0], 0, 0))


def params():
    return pltpu.CompilerParams(vmem_limit_bytes=44 * 2**20)


def f32(*shape):
    return jax.ShapeDtypeStruct(shape, F32)


def call(kernel, flags, operands, outs, scratch, chosen=(), flops=10**9):
    def spec(shape):
        return pl.BlockSpec(shape, lambda i, flags, n=len(shape): (0,) * n)

    in_specs = [picked(x) if n in chosen else spec(x.shape) for n, x in enumerate(operands)]
    size = sum(math.prod(x.shape) * x.dtype.itemsize for x in operands)
    return pl.pallas_call(
        kernel,
        out_shape=outs,
        grid_spec=pltpu.PrefetchScalarGridSpec(
            num_scalar_prefetch=1,
            grid=(1,),
            in_specs=in_specs,
            out_specs=[spec(o.shape) for o in outs],
            scratch_shapes=scratch,
        ),
        compiler_params=params(),
        cost_estimate=pl.CostEstimate(flops=flops, bytes_accessed=size, transcendentals=0),
    )(flags, *operands)


def cyclic(value, axis, steps):
    count = lax.axis_size(axis)
    return lax.ppermute(value, axis, [(s, (s + steps) % count) for s in range(count)])


def shifted(value, axis, steps):
    count = lax.axis_size(axis)
    pairs = [(s, s + steps) for s in range(count) if 0 <= s + steps < count]
    return lax.ppermute(value, axis, pairs)


def mirrored(value, axis, bits):
    count = lax.axis_size(axis)
    return lax.ppermute(value, axis, [(s, s ^ bits) for s in range(count)])


def summed(value, axis):
    count, step = lax.axis_size(axis), 1
    while step < count:
        radix = 4 if count // step % 4 == 0 else 2
        value = sum([mirrored(value, axis, step * k) for k in range(1, radix)], value)
        step *= radix
    return value


def per_device(object_field, frames_data, patch_psfs):
    rows, width = object_field.shape
    count = width // S
    psfs = patch_psfs.reshape(count, S, S)
    observed = frames_data[0]
    t = {name: jnp.asarray(value) for name, value in tables().items()}
    y, x = lax.axis_index("sy"), lax.axis_index("sx")
    flags = jnp.stack([y == 0, x == 0, x == lax.axis_size("sx") - 1]).astype(jnp.int32)

    psf_above = cyclic(psfs, "sy", 1)
    obj_left = shifted(object_field[:, -H:], "sx", 1)
    obj_right = shifted(object_field[:, :H], "sx", -1)
    obj_wide = jnp.concatenate([obj_left[H:], object_field[H:], obj_right[H:]], axis=1)
    obj_above = cyclic(obj_wide, "sy", 1)

    spec, total = call(
        lambda flags, *refs: psf_kernel(*refs),
        flags,
        (psfs, observed, t["psf_right"], t["psf_left"]),
        (f32(2 * L, width), f32(8, S)),
        [],
        flops=6 * 84 * 10**6,
    )
    spec_above, spill_left, middle, spill_right, flux = call(
        model_kernel,
        flags,
        (obj_above, object_field, obj_left, obj_right, psf_above, spec, total)
        + tuple(
            t[k]
            for k in (
                "psf_right", "psf_left", "obj_right", "obj_left",
                "top_inverse", "bottom_inverse", "out_right",
            )
        ),
        (f32(2 * L, width), f32(L, S), f32(L, width), f32(L, S), f32(8, S)),
        [pltpu.VMEM((S, width + S), F32), pltpu.VMEM((L, width + 2 * S), F32)],
        chosen=(10,),
        flops=6 * 600 * 10**6,
    )
    from_right = shifted(spill_left, "sx", -1)
    from_left = shifted(spill_right, "sx", 1)
    folded = jnp.concatenate(
        [middle[:, :S] + from_left, middle[:, S:-S], middle[:, -S:] + from_right], axis=1
    )
    from_below = cyclic(folded[:S], "sy", -1)
    flux = summed(summed(flux, "sx"), "sy")
    gain = flux[4, 0] / flux[0, 0]
    residual = gain * (folded[S:] + from_below) - observed

    own_left = shifted(residual[:, -S:], "sx", 1)
    own_right = shifted(residual[:, :S], "sx", -1)
    top_middle = cyclic(residual, "sy", 1)
    top_left = shifted(top_middle[:, -S:], "sx", 1)
    top_right = shifted(top_middle[:, :S], "sx", -1)
    grad_right = t["grad_right"].reshape(3, 2, L, S).transpose(1, 0, 2, 3).reshape(2, 3 * L, S)
    g_left, g_top, g_bottom, g_right = call(
        gradient_kernel,
        flags,
        (top_left, top_middle, top_right, own_left, residual, own_right,
         jnp.full((8, S), gain), spec, spec_above)
        + tuple(t[k] for k in ("res_right", "top_forward", "bottom_forward", "grad_left"))
        + (grad_right,),
        (f32(S, H), f32(H, width), f32(H, width), f32(S, H)),
        [pltpu.VMEM((L, width + 2 * S), F32), pltpu.VMEM((S, width + S), F32)],
        chosen=(12,),
        flops=6 * 500 * 10**6,
    )
    g_from_right = shifted(g_left, "sx", -1)
    g_from_left = shifted(g_right, "sx", 1)

    def joined(part, lo, hi):
        return jnp.concatenate(
            [part[:, :H] + g_from_left[lo:hi], part[:, H:-H], part[:, -H:] + g_from_right[lo:hi]], axis=1
        )

    g_top, g_bottom = joined(g_top, 0, H), joined(g_bottom, H, S)
    top_same = cyclic(g_top, "sy", -1)
    top_other = mirrored_up(g_top)
    bottom_other = mirrored(g_bottom, "fr", 1)
    gradient = jnp.concatenate([g_bottom + bottom_other, top_same + top_other], axis=0)
    return gradient, residual[None]


def mirrored_up(value):
    count_y, count_f = lax.axis_size("sy"), lax.axis_size("fr")
    pairs = [
        (y * count_f + f, (y - 1) % count_y * count_f + (f ^ 1))
        for y in range(count_y)
        for f in range(count_f)
    ]
    return lax.ppermute(value, ("sy", "fr"), pairs)


def solution(mesh):
    placed = (P("sy", "sx"), P("fr", "sy", "sx"), P("fr", "sy", "sx", None, None))
    return jax.shard_map(
        per_device,
        mesh=mesh,
        in_specs=placed,
        out_specs=(P("sy", "sx"), P("fr", "sy", "sx")),
        check_vma=False,
    )
```

time: 697 us -> 138 us (0.20); the launches traced: 688 us -> 138 us
  blocking collectives: 331 us -> 0 us
  matrix products: 168 us -> 0 us
  waiting for transfers between devices: 91 us -> 33.8 us
  Pallas kernels: 0 us -> 24.7 us
  starting transfers between devices: 41.4 us -> 59.5 us
  local copies, waits for them, and re-layouts: 33.5 us -> 15.8 us
  between operations: 16.3 us -> 2.35 us
    psum x1 -> x0, blocking collectives: 331 us -> none  [flux_totals(): return lax.psum((data_sum, model_sum), ('sy', 'sx'))]
    dot_general x30 -> x0, matrix products: 168 us -> none  [contract(): jnp.einsum(pattern, first_op, second_op, precision=lax.Precision.HIGHEST)]
    psum x1 -> x0, waiting for transfers between devices: 47.9 us -> none  [per_device(): gradient = lax.psum(frame_grad, 'fr')]
    pallas_call x0 -> x3, Pallas kernels: none -> 24.7 us  [call(): pl.pallas_call(kernel, out_shape=outs, grid_spec=pltpu.PrefetchScalarGrid...]
    ppermute x16 -> x27, starting transfers between devices: 41.3 us -> 59.5 us  [the longest x10 33.5 us: shifted(): return lax.ppermute(value, axis, pairs)]
    ppermute x16 -> x27, waiting for transfers between devices: 43.1 us -> 33.8 us  [the longest x5 10.3 us: cyclic(): lax.ppermute(value, axis, [(s, (s + steps) % count) for s in range(count)])]
    unnamed x25 -> x38, local copies, waits for them, and re-layouts: 4.24 us -> 13.2 us
    another operation x3 -> x0, local copies, waits for them, and re-layouts: 7.71 us -> none  [the longest x1 3.98 us: per_device(): cut_windows(beside_all, stride, count_y, count_x, 3)]
  transfers between devices with their start and end apart: 17 -> 27, of which waited for: 11 -> 12; matrix products, arithmetic and copies ran while one was open for 3% -> 2% of each run, Pallas kernels for 0% -> 1%
where the time goes in v1:
time: 138 us
  starting transfers between devices  59.5 us (43%)
  waiting for transfers between devices  33.8 us (24%)
  Pallas kernels  24.7 us (18%)
  local copies, waits for them, and re-layouts  15.8 us (11%)
  between operations  2.35 us (2%)
  other arithmetic  1.49 us (1%)
    ppermute x10, starting transfers between devices, shifted(): return lax.ppermute(value, axis, pairs)  33.5 us
    pallas_call x3, Pallas kernels, call(): pl.pallas_call(kernel, out_shape=outs, grid_spec=pltpu.PrefetchScalarGrid...  24.7 us
    ppermute x11, starting transfers between devices, mirrored(): return lax.ppermute(value, axis, [(s, s ^ bits) for s in range(count)])  18.1 us
    unnamed x38, local copies, waits for them, and re-layouts  13.2 us
    ppermute x5, waiting for transfers between devices, cyclic(): lax.ppermute(value, axis, [(s, (s + steps) % count) for s in range(count)])  10.3 us
    ppermute x11, waiting for transfers between devices, mirrored(): return lax.ppermute(value, axis, [(s, s ^ bits) for s in range(count)])  10.2 us
    ppermute x5, starting transfers between devices, cyclic(): lax.ppermute(value, axis, [(s, (s + steps) % count) for s in range(count)])  7.81 us
    ppermute x1, waiting for transfers between devices, mirrored_up(): return lax.ppermute(value, ('sy', 'fr'), pairs)  6.71 us
  transfers between devices with their start and end apart: 27, of which 12 were waited for; matrix products, arithmetic and copies ran while one was open for 2% of the time, Pallas kernels for 1%

profile of v1, /device:TPU:1, one launch (start us, length us, event | category | flops | bytes accessed | tf_op | source)
XLA Modules:
  0.0 137.6 jit_solution(12204437955860967216)
XLA Ops:
  1.6 4.5 %collective-permute-start = (f32[128,64]{1,0:T(8,128)S(1)}, f32[128,64]{1,0:T(8,128)S(1)}, u32[]{:S(2)}, u32[]{:S(2)}) collective-permute-start(f32[128,64]{1,0:T(8,128)S(1)} %get-tuple-element.30), channel_id=1, source_target_pairs={{0,2},{2,4},{4,6},{6,8},{8,10},{10,12},{12,14},{1,3},{3,5},{5,7},{... | collective-permute-start | bytes 98312 | tf_op jit(solution)/shard_map/ppermute | solution.py:274
  6.1 1.9 %collective-permute-start.1 = (f32[128,64]{1,0:T(8,128)S(1)}, f32[128,64]{1,0:T(8,128)S(1)}, u32[]{:S(2)}, u32[]{:S(2)}) collective-permute-start(f32[128,64]{1,0:T(8,128)S(1)} %get-tuple-element.31), channel_id=1, source_target_pairs={{2,0},{4,2},{6,4},{8,6},{10,8},{12,10},{14,12},{3,1},{5,3},{7,5},{... | collective-permute-start | bytes 98312 | tf_op jit(solution)/shard_map/ppermute | solution.py:274
  8.0 1.7 %collective-permute-start.3 = (f32[4,128,128]{2,1,0:T(8,128)}, f32[4,128,128]{2,1,0:T(8,128)S(1)}, u32[]{:S(2)}, u32[]{:S(2)}) collective-permute-start(f32[4,128,128]{2,1,0:T(8,128)} %bitcast.10), channel_id=1, source_target_pairs={{0,16},{16,32},{32,48},{48,64},{64,80},{80,96},{96,112},{112,128},... | collective-permute-start | bytes 786440 | tf_op jit(solution)/shard_map/ppermute | solution.py:268
  11.8 2.0 %collective-permute-start.2 = (f32[64,640]{1,0:T(8,128)S(1)}, f32[64,640]{1,0:T(8,128)S(1)}, u32[]{:S(2)}, u32[]{:S(2)}) collective-permute-start(f32[64,640]{1,0:T(8,128)S(1)} %pad_maximum_fusion.2), channel_id=1, source_target_pairs={{0,16},{16,32},{32,48},{48,64},{64,80},{80,96},{96,112},{112,128},... | collective-permute-start | bytes 491528 | tf_op jit(solution)/shard_map/ppermute | solution.py:268
  15.8 1.1 copy-done.7
  17.9 2.0 %shard_map.158 = (f32[512,512]{1,0:T(8,128)S(1)}, f32[8,128]{1,0:T(8,128)S(1)}) custom-call(s32[3]{0:T(128)S(1)} %add_convert_fusion.flags, f32[4,128,128]{2,1,0:T(8,128)S(1)} %bitcast.11, f32[128,512]{1,0:T(8,128)S(1)} %bitcast.9, bf16[384,256]{1,0:T(8,128)(2,1)S(1)} %copy-done.17, bf16[512,768]{1,0:T(8,128)(2,1)S(1)} %copy-done.7), custom_call_target="tpu_custom_call" | custom-call | flops 504000000 | bytes 1507328 | tf_op jit(solution)/shard_map/pallas_call | solution.py:251
  19.8 3.8 %collective-permute-done.2.above_ref = f32[64,640]{1,0:T(8,128)S(1)} collective-permute-done((f32[64,640]{1,0:T(8,128)S(1)}, f32[64,640]{1,0:T(8,128)S(1)}, u32[]{:S(2)}, u32[]{:S(2)}) %collective-permute-start.2) | collective-permute-done | bytes 163872 | tf_op jit(solution)/shard_map/ppermute | solution.py:268
  24.6 1.9 %copy-done.6 = bf16[2,1024,768]{2,1,0:T(8,128)(2,1)S(1)} copy-done((bf16[2,1024,768]{2,1,0:T(8,128)(2,1)S(1)}, bf16[2,1024,768]{2,1,0:T(8,128)(2,1)}, u32[]{:S(2)}) %copy-start.6) | copy-done | bytes 3145752
  32.8 12.5 %shard_map.159 = (f32[512,512]{1,0:T(8,128)S(1)}, f32[256,128]{1,0:T(8,128)S(1)}, f32[256,512]{1,0:T(8,128)S(1)}, f32[256,128]{1,0:T(8,128)S(1)}, f32[8,128]{1,0:T(8,128)S(1)}) custom-call(s32[3]{0:T(128)S(1)} %add_convert_fusion.flags, f32[64,640]{1,0:T(8,128)S(1)} %collective-permute-done.2.above_ref, f32[128,512]{1,0:T(8,128)S(1)} %copy-done.1, ...), custom_call_target="tpu_custom_call" | custom-call | flops 3600000000 | bytes 8294400 | tf_op jit(solution)/shard_map/pallas_call | solution.py:251
  45.4 3.4 %collective-permute-start.6 = (f32[8,128]{1,0:T(8,128)S(1)}, f32[8,128]{1,0:T(8,128)S(1)}, u32[]{:S(2)}, u32[]{:S(2)}) collective-permute-start(f32[8,128]{1,0:T(8,128)S(1)} %get-tuple-element.15), channel_id=1, source_target_pairs={{0,6},{2,4},{4,2},{6,0},{8,14},{10,12},{12,10},{14,8},{1,7},{3,5},... | collective-permute-start | bytes 12296 | tf_op jit(solution)/shard_map/ppermute | solution.py:279
  50.1 1.2 collective-permute-done.5
  51.4 1.5 %collective-permute-start.7 = (f32[8,128]{1,0:T(8,128)S(1)}, f32[8,128]{1,0:T(8,128)S(1)}, u32[]{:S(2)}, u32[]{:S(2)}) collective-permute-start(f32[8,128]{1,0:T(8,128)S(1)} %add_add_fusion.2), channel_id=1, source_target_pairs={{0,8},{2,10},{4,12},{6,14},{8,0},{10,2},{12,4},{14,6},{1,9},{3,11}... | collective-permute-start | bytes 12296 | tf_op jit(solution)/shard_map/ppermute | solution.py:279
  52.9 2.5 %collective-permute-done.7 = f32[8,128]{1,0:T(8,128)S(1)} collective-permute-done((f32[8,128]{1,0:T(8,128)S(1)}, f32[8,128]{1,0:T(8,128)S(1)}, u32[]{:S(2)}, u32[]{:S(2)}) %collective-permute-start.7) | collective-permute-done | bytes 4128 | tf_op jit(solution)/shard_map/ppermute | solution.py:279
  55.4 3.5 %collective-permute-start.8 = (f32[8,128]{1,0:T(8,128)S(1)}, f32[8,128]{1,0:T(8,128)S(1)}, u32[]{:S(2)}, u32[]{:S(2)}) collective-permute-start(f32[8,128]{1,0:T(8,128)S(1)} %add.60), channel_id=1, source_target_pairs={{0,16},{16,0},{32,48},{48,32},{64,80},{80,64},{96,112},{112,96},{1... | collective-permute-start | bytes 12296 | tf_op jit(solution)/shard_map/ppermute | solution.py:279
  59.0 5.2 %collective-permute-start.14 = (f32[256,128]{1,0:T(8,128)S(1)}, f32[256,128]{1,0:T(8,128)S(1)}, u32[]{:S(2)}, u32[]{:S(2)}) collective-permute-start(f32[256,128]{1,0:T(8,128)S(1)} %get-tuple-element.17), channel_id=1, source_target_pairs={{0,2},{2,4},{4,6},{6,8},{8,10},{10,12},{12,14},{1,3},{3,5},{5,7},{... | collective-permute-start | bytes 393224 | tf_op jit(solution)/shard_map/ppermute | solution.py:274
  64.2 1.9 %collective-permute-start.15 = (f32[256,128]{1,0:T(8,128)S(1)}, f32[256,128]{1,0:T(8,128)S(1)}, u32[]{:S(2)}, u32[]{:S(2)}) collective-permute-start(f32[256,128]{1,0:T(8,128)S(1)} %get-tuple-element.18), channel_id=1, source_target_pairs={{2,0},{4,2},{6,4},{8,6},{10,8},{12,10},{14,12},{3,1},{5,3},{7,5},{... | collective-permute-start | bytes 393224 | tf_op jit(solution)/shard_map/ppermute | solution.py:274
  66.8 2.7 %collective-permute-start.11 = (f32[8,128]{1,0:T(8,128)S(1)}, f32[8,128]{1,0:T(8,128)S(1)}, u32[]{:S(2)}, u32[]{:S(2)}) collective-permute-start(f32[8,128]{1,0:T(8,128)S(1)} %add_add_fusion.1), channel_id=1, source_target_pairs={{0,64},{16,80},{32,96},{48,112},{64,0},{80,16},{96,32},{112,48},{1... | collective-permute-start | bytes 12296 | tf_op jit(solution)/shard_map/ppermute | solution.py:279
  70.6 1.8 %collective-permute-start.16 = (f32[128,512]{1,0:T(8,128)S(1)}, f32[128,512]{1,0:T(8,128)S(1)}, u32[]{:S(2)}, u32[]{:S(2)}) collective-permute-start(f32[128,512]{1,0:T(8,128)S(1)} %slice.107), channel_id=1, source_target_pairs={{0,240},{16,0},{32,16},{48,32},{64,48},{80,64},{96,80},{112,96},{1... | collective-permute-start | bytes 786440 | tf_op jit(solution)/shard_map/ppermute | solution.py:268
  74.3 2.6 %collective-permute-done.16 = f32[128,512]{1,0:T(8,128)S(1)} collective-permute-done((f32[128,512]{1,0:T(8,128)S(1)}, f32[128,512]{1,0:T(8,128)S(1)}, u32[]{:S(2)}, u32[]{:S(2)}) %collective-permute-start.16) | collective-permute-done | bytes 262176 | tf_op jit(solution)/shard_map/ppermute | solution.py:268
  77.6 1.9 %collective-permute-start.21 = (f32[128,128]{1,0:T(8,128)S(1)}, f32[128,128]{1,0:T(8,128)S(1)}, u32[]{:S(2)}, u32[]{:S(2)}) collective-permute-start(f32[128,128]{1,0:T(8,128)S(1)} %get-tuple-element.26), channel_id=1, source_target_pairs={{2,0},{4,2},{6,4},{8,6},{10,8},{12,10},{14,12},{3,1},{5,3},{7,5},{... | collective-permute-start | bytes 196616 | tf_op jit(solution)/shard_map/ppermute | solution.py:274
  79.6 4.7 %collective-permute-start.20 = (f32[128,128]{1,0:T(8,128)S(1)}, f32[128,128]{1,0:T(8,128)S(1)}, u32[]{:S(2)}, u32[]{:S(2)}) collective-permute-start(f32[128,128]{1,0:T(8,128)S(1)} %get-tuple-element.27), channel_id=1, source_target_pairs={{0,2},{2,4},{4,6},{6,8},{8,10},{10,12},{12,14},{1,3},{3,5},{5,7},{... | collective-permute-start | bytes 196616 | tf_op jit(solution)/shard_map/ppermute | solution.py:274
  84.2 4.0 %collective-permute-done.17.top_middle = f32[128,512]{1,0:T(8,128)S(1)} collective-permute-done((f32[128,512]{1,0:T(8,128)S(1)}, f32[128,512]{1,0:T(8,128)S(1)}, u32[]{:S(2)}, u32[]{:S(2)}) %collective-permute-start.17) | collective-permute-done | bytes 262176 | tf_op jit(solution)/shard_map/ppermute | solution.py:268
  88.2 1.9 %collective-permute-start.19 = (f32[128,128]{1,0:T(8,128)S(1)}, f32[128,128]{1,0:T(8,128)S(1)}, u32[]{:S(2)}, u32[]{:S(2)}) collective-permute-start(f32[128,128]{1,0:T(8,128)S(1)} %get-tuple-element.28), channel_id=1, source_target_pairs={{2,0},{4,2},{6,4},{8,6},{10,8},{12,10},{14,12},{3,1},{5,3},{7,5},{... | collective-permute-start | bytes 196616 | tf_op jit(solution)/shard_map/ppermute | solution.py:274
  90.2 5.2 %collective-permute-start.18 = (f32[128,128]{1,0:T(8,128)S(1)}, f32[128,128]{1,0:T(8,128)S(1)}, u32[]{:S(2)}, u32[]{:S(2)}) collective-permute-start(f32[128,128]{1,0:T(8,128)S(1)} %get-tuple-element.29), channel_id=1, source_target_pairs={{0,2},{2,4},{4,6},{6,8},{8,10},{10,12},{12,14},{1,3},{3,5},{5,7},{... | collective-permute-start | bytes 196616 | tf_op jit(solution)/shard_map/ppermute | solution.py:274
  96.5 10.2 %shard_map.160 = (f32[128,64]{1,0:T(8,128)S(1)}, f32[64,512]{1,0:T(8,128)S(1)}, f32[64,512]{1,0:T(8,128)S(1)}, f32[128,64]{1,0:T(8,128)S(1)}) custom-call(s32[3]{0:T(128)S(1)} %add_convert_fusion.flags, f32[128,128]{1,0:T(8,128)S(1)} %collective-permute-done.18.top_left, f32[128,512]{1,0:T(8,128)S(1)} %collective-permute-done.17.top_middle, ...), custom_call_target="tpu_custom_call" | custom-call | flops 3000000000 | bytes 8392704 | tf_op jit(solution)/shard_map/pallas_call | solution.py:251
  106.7 4.3 %collective-permute-start.22 = (f32[128,64]{1,0:T(8,128)S(1)}, f32[128,64]{1,0:T(8,128)S(1)}, u32[]{:S(2)}, u32[]{:S(2)}) collective-permute-start(f32[128,64]{1,0:T(8,128)S(1)} %get-tuple-element.21), channel_id=1, source_target_pairs={{0,2},{2,4},{4,6},{6,8},{8,10},{10,12},{12,14},{1,3},{3,5},{5,7},{... | collective-permute-start | bytes 98312 | tf_op jit(solution)/shard_map/ppermute | solution.py:274
  110.9 1.9 %collective-permute-start.23 = (f32[128,64]{1,0:T(8,128)S(1)}, f32[128,64]{1,0:T(8,128)S(1)}, u32[]{:S(2)}, u32[]{:S(2)}) collective-permute-start(f32[128,64]{1,0:T(8,128)S(1)} %get-tuple-element.22), channel_id=1, source_target_pairs={{2,0},{4,2},{6,4},{8,6},{10,8},{12,10},{14,12},{3,1},{5,3},{7,5},{... | collective-permute-start | bytes 98312 | tf_op jit(solution)/shard_map/ppermute | solution.py:274
  113.0 3.6 %collective-permute-done.23 = f32[128,64]{1,0:T(8,128)S(1)} collective-permute-done((f32[128,64]{1,0:T(8,128)S(1)}, f32[128,64]{1,0:T(8,128)S(1)}, u32[]{:S(2)}, u32[]{:S(2)}) %collective-permute-start.23) | collective-permute-done | bytes 32800 | tf_op jit(solution)/shard_map/ppermute | solution.py:274
  116.7 5.6 %collective-permute-start.24 = (f32[64,512]{1,0:T(8,128)S(1)}, f32[64,512]{1,0:T(8,128)S(1)}, u32[]{:S(2)}, u32[]{:S(2)}) collective-permute-start(f32[64,512]{1,0:T(8,128)S(1)} %pad_maximum_fusion.3), channel_id=1, source_target_pairs={{0,1},{1,0},{2,3},{3,2},{4,5},{5,4},{6,7},{7,6},{8,9},{9,8},{10,11... | collective-permute-start | bytes 393224 | tf_op jit(solution)/shard_map/ppermute | solution.py:279
  122.6 1.6 %collective-permute-start.25 = (f32[64,512]{1,0:T(8,128)S(1)}, f32[64,512]{1,0:T(8,128)S(1)}, u32[]{:S(2)}, u32[]{:S(2)}) collective-permute-start(f32[64,512]{1,0:T(8,128)S(1)} %pad_maximum_fusion.4), channel_id=1, source_target_pairs={{0,240},{16,0},{32,16},{48,32},{64,48},{80,64},{96,80},{112,96},{1... | collective-permute-start | bytes 393224 | tf_op jit(solution)/shard_map/ppermute | solution.py:268
  124.2 5.8 %collective-permute-done.24 = f32[64,512]{1,0:T(8,128)S(1)} collective-permute-done((f32[64,512]{1,0:T(8,128)S(1)}, f32[64,512]{1,0:T(8,128)S(1)}, u32[]{:S(2)}, u32[]{:S(2)}) %collective-permute-start.24) | collective-permute-done | bytes 131104 | tf_op jit(solution)/shard_map/ppermute | solution.py:279
  130.1 6.7 %collective-permute-done.26 = f32[64,512]{1,0:T(8,128)S(1)} collective-permute-done((f32[64,512]{1,0:T(8,128)S(1)}, f32[64,512]{1,0:T(8,128)S(1)}, u32[]{:S(2)}, u32[]{:S(2)}) %collective-permute-start.26) | collective-permute-done | bytes 131104 | tf_op jit(solution)/shard_map/ppermute | solution.py:381
  (90 shorter events, 19.9 us)
Async XLA Ops:
  1.6 9.1 %collective-permute-start = (f32[128,64]{1,0:T(8,128)S(1)}, f32[128,64]{1,0:T(8,128)S(1)}, u32[]{:S(2)}, u32[]{:S(2)}) collective-permute-start(f32[128,64]{1,0:T(8,128)S(1)} %get-tuple-element.30), channel_id=1, source_target_pairs={{0,2},{2,4},{4,6},{6,8},{8,10},{10,12},{12,14},{1,3},{3,5},{5,7},{... | collective-permute-start | bytes 98312 | tf_op jit(solution)/shard_map/ppermute | solution.py:274
  6.1 5.6 %collective-permute-start.1 = (f32[128,64]{1,0:T(8,128)S(1)}, f32[128,64]{1,0:T(8,128)S(1)}, u32[]{:S(2)}, u32[]{:S(2)}) collective-permute-start(f32[128,64]{1,0:T(8,128)S(1)} %get-tuple-element.31), channel_id=1, source_target_pairs={{2,0},{4,2},{6,4},{8,6},{10,8},{12,10},{14,12},{3,1},{5,3},{7,5},{... | collective-permute-start | bytes 98312 | tf_op jit(solution)/shard_map/ppermute | solution.py:274
  8.0 15.6 %collective-permute-start.3 = (f32[4,128,128]{2,1,0:T(8,128)}, f32[4,128,128]{2,1,0:T(8,128)S(1)}, u32[]{:S(2)}, u32[]{:S(2)}) collective-permute-start(f32[4,128,128]{2,1,0:T(8,128)} %bitcast.10), channel_id=1, source_target_pairs={{0,16},{16,32},{32,48},{48,64},{64,80},{80,96},{96,112},{112,128},... | collective-permute-start | bytes 786440 | tf_op jit(solution)/shard_map/ppermute | solution.py:268
  11.8 11.8 %collective-permute-start.2 = (f32[64,640]{1,0:T(8,128)S(1)}, f32[64,640]{1,0:T(8,128)S(1)}, u32[]{:S(2)}, u32[]{:S(2)}) collective-permute-start(f32[64,640]{1,0:T(8,128)S(1)} %pad_maximum_fusion.2), channel_id=1, source_target_pairs={{0,16},{16,32},{32,48},{48,64},{64,80},{80,96},{96,112},{112,128},... | collective-permute-start | bytes 491528 | tf_op jit(solution)/shard_map/ppermute | solution.py:268
  32.8 63.6 %copy-start.10 = (bf16[512,768]{1,0:T(8,128)(2,1)S(1)}, bf16[512,768]{1,0:T(8,128)(2,1)}, u32[]{:S(2)}) copy-start(bf16[512,768]{1,0:T(8,128)(2,1)} %constant.46.clone.bottom_forward) | copy-start | bytes 2359300
  32.8 63.6 %copy-start.13 = (bf16[2,768,128]{2,1,0:T(8,128)(2,1)S(1)}, bf16[2,768,128]{2,1,0:T(8,128)(2,1)}, u32[]{:S(2)}) copy-start(bf16[2,768,128]{2,1,0:T(8,128)(2,1)} %constant.52.grad_right) | copy-start | bytes 1179652
  32.8 63.6 %copy-start.14 = (bf16[768,256]{1,0:T(8,128)(2,1)S(1)}, bf16[768,256]{1,0:T(8,128)(2,1)}, u32[]{:S(2)}) copy-start(bf16[768,256]{1,0:T(8,128)(2,1)} %constant.45.clone.res_right) | copy-start | bytes 1179652
  45.3 51.1 %copy-start.5 = (bf16[2,256,3072]{2,1,0:T(8,128)(2,1)S(1)}, bf16[2,256,3072]{2,1,0:T(8,128)(2,1)}, u32[]{:S(2)}) copy-start(bf16[2,256,3072]{2,1,0:T(8,128)(2,1)} %constant.41.clone.grad_left) | copy-start | bytes 9437188
  45.4 51.1 %copy-start.9 = (bf16[512,768]{1,0:T(8,128)(2,1)S(1)}, bf16[512,768]{1,0:T(8,128)(2,1)}, u32[]{:S(2)}) copy-start(bf16[512,768]{1,0:T(8,128)(2,1)} %constant.38.clone.refs_3_.psf_left.top_forward) | copy-start | bytes 2359300
  45.4 4.7 %collective-permute-start.6 = (f32[8,128]{1,0:T(8,128)S(1)}, f32[8,128]{1,0:T(8,128)S(1)}, u32[]{:S(2)}, u32[]{:S(2)}) collective-permute-start(f32[8,128]{1,0:T(8,128)S(1)} %get-tuple-element.15), channel_id=1, source_target_pairs={{0,6},{2,4},{4,2},{6,0},{8,14},{10,12},{12,10},{14,8},{1,7},{3,5},... | collective-permute-start | bytes 12296 | tf_op jit(solution)/shard_map/ppermute | solution.py:279
  48.8 2.5 %collective-permute-start.5 = (f32[8,128]{1,0:T(8,128)S(1)}, f32[8,128]{1,0:T(8,128)S(1)}, u32[]{:S(2)}, u32[]{:S(2)}) collective-permute-start(f32[8,128]{1,0:T(8,128)S(1)} %get-tuple-element.15), channel_id=1, source_target_pairs={{0,4},{2,6},{4,0},{6,2},{8,12},{10,14},{12,8},{14,10},{1,5},{3,7},... | collective-permute-start | bytes 12296 | tf_op jit(solution)/shard_map/ppermute | solution.py:279
  48.8 2.5 %collective-permute-start.4 = (f32[8,128]{1,0:T(8,128)S(1)}, f32[8,128]{1,0:T(8,128)S(1)}, u32[]{:S(2)}, u32[]{:S(2)}) collective-permute-start(f32[8,128]{1,0:T(8,128)S(1)} %get-tuple-element.15), channel_id=1, source_target_pairs={{0,2},{2,0},{4,6},{6,4},{8,10},{10,8},{12,14},{14,12},{1,3},{3,1},... | collective-permute-start | bytes 12296 | tf_op jit(solution)/shard_map/ppermute | solution.py:279
  51.4 4.0 %collective-permute-start.7 = (f32[8,128]{1,0:T(8,128)S(1)}, f32[8,128]{1,0:T(8,128)S(1)}, u32[]{:S(2)}, u32[]{:S(2)}) collective-permute-start(f32[8,128]{1,0:T(8,128)S(1)} %add_add_fusion.2), channel_id=1, source_target_pairs={{0,8},{2,10},{4,12},{6,14},{8,0},{10,2},{12,4},{14,6},{1,9},{3,11}... | collective-permute-start | bytes 12296 | tf_op jit(solution)/shard_map/ppermute | solution.py:279
  55.4 10.8 %collective-permute-start.10 = (f32[8,128]{1,0:T(8,128)S(1)}, f32[8,128]{1,0:T(8,128)S(1)}, u32[]{:S(2)}, u32[]{:S(2)}) collective-permute-start(f32[8,128]{1,0:T(8,128)S(1)} %add.60), channel_id=1, source_target_pairs={{0,48},{16,32},{32,16},{48,0},{64,112},{80,96},{96,80},{112,64},{1... | collective-permute-start | bytes 12296 | tf_op jit(solution)/shard_map/ppermute | solution.py:279
  55.4 10.8 %collective-permute-start.9 = (f32[8,128]{1,0:T(8,128)S(1)}, f32[8,128]{1,0:T(8,128)S(1)}, u32[]{:S(2)}, u32[]{:S(2)}) collective-permute-start(f32[8,128]{1,0:T(8,128)S(1)} %add.60), channel_id=1, source_target_pairs={{0,32},{16,48},{32,0},{48,16},{64,96},{80,112},{96,64},{112,80},{1... | collective-permute-start | bytes 12296 | tf_op jit(solution)/shard_map/ppermute | solution.py:279
  55.4 10.8 %collective-permute-start.8 = (f32[8,128]{1,0:T(8,128)S(1)}, f32[8,128]{1,0:T(8,128)S(1)}, u32[]{:S(2)}, u32[]{:S(2)}) collective-permute-start(f32[8,128]{1,0:T(8,128)S(1)} %add.60), channel_id=1, source_target_pairs={{0,16},{16,0},{32,48},{48,32},{64,80},{80,64},{96,112},{112,96},{1... | collective-permute-start | bytes 12296 | tf_op jit(solution)/shard_map/ppermute | solution.py:279
  59.0 10.6 %collective-permute-start.14 = (f32[256,128]{1,0:T(8,128)S(1)}, f32[256,128]{1,0:T(8,128)S(1)}, u32[]{:S(2)}, u32[]{:S(2)}) collective-permute-start(f32[256,128]{1,0:T(8,128)S(1)} %get-tuple-element.17), channel_id=1, source_target_pairs={{0,2},{2,4},{4,6},{6,8},{8,10},{10,12},{12,14},{1,3},{3,5},{5,7},{... | collective-permute-start | bytes 393224 | tf_op jit(solution)/shard_map/ppermute | solution.py:274
  64.2 6.3 %collective-permute-start.15 = (f32[256,128]{1,0:T(8,128)S(1)}, f32[256,128]{1,0:T(8,128)S(1)}, u32[]{:S(2)}, u32[]{:S(2)}) collective-permute-start(f32[256,128]{1,0:T(8,128)S(1)} %get-tuple-element.18), channel_id=1, source_target_pairs={{2,0},{4,2},{6,4},{8,6},{10,8},{12,10},{14,12},{3,1},{5,3},{7,5},{... | collective-permute-start | bytes 393224 | tf_op jit(solution)/shard_map/ppermute | solution.py:274
  66.2 6.2 %collective-permute-start.13 = (f32[8,128]{1,0:T(8,128)S(1)}, f32[8,128]{1,0:T(8,128)S(1)}, u32[]{:S(2)}, u32[]{:S(2)}) collective-permute-start(f32[8,128]{1,0:T(8,128)S(1)} %add_add_fusion.1), channel_id=1, source_target_pairs={{0,192},{16,208},{32,224},{48,240},{64,128},{80,144},{96,160},{112... | collective-permute-start | bytes 12296 | tf_op jit(solution)/shard_map/ppermute | solution.py:279
  66.8 5.7 %collective-permute-start.12 = (f32[8,128]{1,0:T(8,128)S(1)}, f32[8,128]{1,0:T(8,128)S(1)}, u32[]{:S(2)}, u32[]{:S(2)}) collective-permute-start(f32[8,128]{1,0:T(8,128)S(1)} %add_add_fusion.1), channel_id=1, source_target_pairs={{0,128},{16,144},{32,160},{48,176},{64,192},{80,208},{96,224},{112... | collective-permute-start | bytes 12296 | tf_op jit(solution)/shard_map/ppermute | solution.py:279
  66.8 5.6 %collective-permute-start.11 = (f32[8,128]{1,0:T(8,128)S(1)}, f32[8,128]{1,0:T(8,128)S(1)}, u32[]{:S(2)}, u32[]{:S(2)}) collective-permute-start(f32[8,128]{1,0:T(8,128)S(1)} %add_add_fusion.1), channel_id=1, source_target_pairs={{0,64},{16,80},{32,96},{48,112},{64,0},{80,16},{96,32},{112,48},{1... | collective-permute-start | bytes 12296 | tf_op jit(solution)/shard_map/ppermute | solution.py:279
  70.6 6.3 %collective-permute-start.16 = (f32[128,512]{1,0:T(8,128)S(1)}, f32[128,512]{1,0:T(8,128)S(1)}, u32[]{:S(2)}, u32[]{:S(2)}) collective-permute-start(f32[128,512]{1,0:T(8,128)S(1)} %slice.107), channel_id=1, source_target_pairs={{0,240},{16,0},{32,16},{48,32},{64,48},{80,64},{96,80},{112,96},{1... | collective-permute-start | bytes 786440 | tf_op jit(solution)/shard_map/ppermute | solution.py:268
  77.0 11.3 %collective-permute-start.17 = (f32[128,512]{1,0:T(8,128)S(1)}, f32[128,512]{1,0:T(8,128)S(1)}, u32[]{:S(2)}, u32[]{:S(2)}) collective-permute-start(f32[128,512]{1,0:T(8,128)S(1)} %fusion.1.own_ref), channel_id=1, source_target_pairs={{0,16},{16,32},{32,48},{48,64},{64,80},{80,96},{96,112},{112,128},... | collective-permute-start | bytes 786440 | tf_op jit(solution)/shard_map/ppermute | solution.py:268
  77.6 17.7 %collective-permute-start.21 = (f32[128,128]{1,0:T(8,128)S(1)}, f32[128,128]{1,0:T(8,128)S(1)}, u32[]{:S(2)}, u32[]{:S(2)}) collective-permute-start(f32[128,128]{1,0:T(8,128)S(1)} %get-tuple-element.26), channel_id=1, source_target_pairs={{2,0},{4,2},{6,4},{8,6},{10,8},{12,10},{14,12},{3,1},{5,3},{7,5},{... | collective-permute-start | bytes 196616 | tf_op jit(solution)/shard_map/ppermute | solution.py:274
  79.6 15.8 %collective-permute-start.20 = (f32[128,128]{1,0:T(8,128)S(1)}, f32[128,128]{1,0:T(8,128)S(1)}, u32[]{:S(2)}, u32[]{:S(2)}) collective-permute-start(f32[128,128]{1,0:T(8,128)S(1)} %get-tuple-element.27), channel_id=1, source_target_pairs={{0,2},{2,4},{4,6},{6,8},{8,10},{10,12},{12,14},{1,3},{3,5},{5,7},{... | collective-permute-start | bytes 196616 | tf_op jit(solution)/shard_map/ppermute | solution.py:274
  88.2 7.1 %collective-permute-start.19 = (f32[128,128]{1,0:T(8,128)S(1)}, f32[128,128]{1,0:T(8,128)S(1)}, u32[]{:S(2)}, u32[]{:S(2)}) collective-permute-start(f32[128,128]{1,0:T(8,128)S(1)} %get-tuple-element.28), channel_id=1, source_target_pairs={{2,0},{4,2},{6,4},{8,6},{10,8},{12,10},{14,12},{3,1},{5,3},{7,5},{... | collective-permute-start | bytes 196616 | tf_op jit(solution)/shard_map/ppermute | solution.py:274
  90.2 6.3 %collective-permute-start.18 = (f32[128,128]{1,0:T(8,128)S(1)}, f32[128,128]{1,0:T(8,128)S(1)}, u32[]{:S(2)}, u32[]{:S(2)}) collective-permute-start(f32[128,128]{1,0:T(8,128)S(1)} %get-tuple-element.29), channel_id=1, source_target_pairs={{0,2},{2,4},{4,6},{6,8},{8,10},{10,12},{12,14},{1,3},{3,5},{5,7},{... | collective-permute-start | bytes 196616 | tf_op jit(solution)/shard_map/ppermute | solution.py:274
  106.7 6.3 %collective-permute-start.22 = (f32[128,64]{1,0:T(8,128)S(1)}, f32[128,64]{1,0:T(8,128)S(1)}, u32[]{:S(2)}, u32[]{:S(2)}) collective-permute-start(f32[128,64]{1,0:T(8,128)S(1)} %get-tuple-element.21), channel_id=1, source_target_pairs={{0,2},{2,4},{4,6},{6,8},{8,10},{10,12},{12,14},{1,3},{3,5},{5,7},{... | collective-permute-start | bytes 98312 | tf_op jit(solution)/shard_map/ppermute | solution.py:274
  110.9 5.6 %collective-permute-start.23 = (f32[128,64]{1,0:T(8,128)S(1)}, f32[128,64]{1,0:T(8,128)S(1)}, u32[]{:S(2)}, u32[]{:S(2)}) collective-permute-start(f32[128,64]{1,0:T(8,128)S(1)} %get-tuple-element.22), channel_id=1, source_target_pairs={{2,0},{4,2},{6,4},{8,6},{10,8},{12,10},{14,12},{3,1},{5,3},{7,5},{... | collective-permute-start | bytes 98312 | tf_op jit(solution)/shard_map/ppermute | solution.py:274
  116.7 13.3 %collective-permute-start.24 = (f32[64,512]{1,0:T(8,128)S(1)}, f32[64,512]{1,0:T(8,128)S(1)}, u32[]{:S(2)}, u32[]{:S(2)}) collective-permute-start(f32[64,512]{1,0:T(8,128)S(1)} %pad_maximum_fusion.3), channel_id=1, source_target_pairs={{0,1},{1,0},{2,3},{3,2},{4,5},{5,4},{6,7},{7,6},{8,9},{9,8},{10,11... | collective-permute-start | bytes 393224 | tf_op jit(solution)/shard_map/ppermute | solution.py:279
  122.5 14.3 %collective-permute-start.26 = (f32[64,512]{1,0:T(8,128)S(1)}, f32[64,512]{1,0:T(8,128)S(1)}, u32[]{:S(2)}, u32[]{:S(2)}) collective-permute-start(f32[64,512]{1,0:T(8,128)S(1)} %pad_maximum_fusion.4), channel_id=1, source_target_pairs={{0,241},{1,240},{16,1},{17,0},{32,17},{33,16},{48,33},{49,32},{64,... | collective-permute-start | bytes 393224 | tf_op jit(solution)/shard_map/ppermute | solution.py:381
  122.6 14.2 %collective-permute-start.25 = (f32[64,512]{1,0:T(8,128)S(1)}, f32[64,512]{1,0:T(8,128)S(1)}, u32[]{:S(2)}, u32[]{:S(2)}) collective-permute-start(f32[64,512]{1,0:T(8,128)S(1)} %pad_maximum_fusion.4), channel_id=1, source_target_pairs={{0,240},{16,0},{32,16},{48,32},{64,48},{80,64},{96,80},{112,96},{1... | collective-permute-start | bytes 393224 | tf_op jit(solution)/shard_map/ppermute | solution.py:268
  (14 other events, 74.4 us)

commit v2 on v1

v2 whole, which is shorter than its diff:
```python
import functools
import math

import jax
import jax.numpy as jnp
import numpy as np
from jax import lax
from jax.experimental import pallas as pl
from jax.experimental.pallas import tpu as pltpu
from jax.sharding import PartitionSpec as P

S = 128
L = 256
H = 64
F32 = jnp.float32
BF16 = jnp.bfloat16


def half_windows():
    n = np.arange(L, dtype=np.float64)
    s = np.sin(np.pi * (n + 0.5) / L) ** 2
    return s[:S], s[S:]


def phases(freqs, positions):
    product = (2 * np.arange(freqs)[:, None] + 1) * positions[None, :] % (2 * L)
    angle = product.astype(np.float64) * (math.pi / L)
    return np.cos(angle), np.sin(angle)


def forward_left(positions):
    c, s = phases(L, positions)
    return np.block([[c, s], [-s, c]])


def inverse_left(positions):
    c, s = phases(L, positions)
    return np.block([[c.T, -s.T], [s.T, c.T]]) / L


def forward_right(positions):
    c, s = phases(S, positions)
    return np.concatenate([c.T, -s.T], axis=1)


def inverse_right(positions):
    c, s = phases(S, positions)
    return np.concatenate([c, -s], axis=0) * (2.0 / L)


def bf16_parts(table):
    hi = table.astype(np.float32).astype(BF16)
    lo = (table - hi.astype(np.float64)).astype(np.float32).astype(BF16)
    return hi, lo


def left_table(table):
    hi, lo = bf16_parts(table)
    return np.concatenate([hi, hi, lo], axis=-1)


def right_table(table):
    hi, lo = bf16_parts(table)
    return np.concatenate([hi, hi, lo], axis=-2)


@functools.lru_cache(maxsize=1)
def tables():
    near, far = np.arange(S), np.arange(S, L)
    up, down = half_windows()
    masked_up, masked_down = np.where(near < H, 0.0, up), np.where(near < H, down, 0.0)
    pairs = ((up, down), (masked_up, masked_down))
    base, back = forward_left(near), inverse_left(near)
    lanes, lanes_back = forward_right(near), inverse_right(near)
    t = {}
    t["near_right"] = right_table(lanes)
    t["near_left"] = left_table(base)
    t["obj_right"] = np.stack(
        [right_table(np.concatenate([w[:, None] * lanes for w in pair], axis=1)) for pair in pairs]
    )
    t["obj_left"] = np.stack(
        [left_table(np.concatenate([base * np.tile(w, 2)[None, :] for w in pair], axis=0)) for pair in pairs]
    )
    t["top_inverse"] = left_table(inverse_left(near))
    t["bottom_inverse"] = left_table(inverse_left(far))
    t["out_right"] = right_table(inverse_right(np.arange(L)))
    t["far_right"] = right_table(forward_right(far))
    t["res_right"] = right_table(forward_right(np.arange(L)))
    t["bottom_forward"] = left_table(forward_left(far))
    t["grad_left"] = np.stack(
        [left_table(np.concatenate([np.tile(w, 2)[:, None] * back for w in pair], axis=1)) for pair in pairs]
    )
    t["grad_right"] = np.stack(
        [right_table(np.concatenate([lanes_back * w[None, :] for w in pair], axis=0)) for pair in pairs]
    )
    return t


def split(value):
    hi = value.astype(BF16)
    return hi, (value - hi.astype(F32)).astype(BF16)


def wide_parts(value):
    hi, lo = split(value)
    return jnp.concatenate([hi, lo, hi], axis=1)


def store_parts(ref, lanes, value):
    hi, lo = split(value)
    depth = value.shape[0]
    ref[:depth, lanes] = hi
    ref[depth : 2 * depth, lanes] = lo
    ref[2 * depth :, lanes] = hi


def dot(a, b):
    return jnp.dot(a, b, preferred_element_type=F32)


def stacked(value):
    half = value.shape[1] // 2
    return jnp.concatenate([value[:, :half], value[:, half:]], axis=0)


def side_by_side(value):
    half = value.shape[0] // 2
    return jnp.concatenate([value[:half], value[half:]], axis=1)


def at(n, size=S):
    return slice(n * size, (n + 1) * size)


class Copies:
    def __init__(self, sources, buffers, semaphores):
        self.copies = [
            pltpu.make_async_copy(source, buffer, semaphores.at[n])
            for n, (source, buffer) in enumerate(zip(sources, buffers))
        ]
        self.buffers, self.waited = buffers, set()
        for copy in self.copies:
            copy.start()

    def __getitem__(self, n):
        if n not in self.waited:
            self.waited.add(n)
            self.copies[n].wait()
        return self.buffers[n]


def spectra(psfs, right, left, parts_ref):
    lanes = dot(wide_parts(jnp.concatenate(psfs, axis=0)), right[...])
    for n in range(len(psfs)):
        store_parts(parts_ref, at(n), stacked(lanes[at(n)]))
    return dot(left[...], parts_ref[:, : len(psfs) * S])


def psf_kernel(flags, psf_ref, frame_ref, right_hbm, left_hbm, spec_ref, total_ref, right, left, parts, sems):
    t = Copies((right_hbm, left_hbm), (right, left), sems)
    total_ref[...] = jnp.full(total_ref.shape, jnp.sum(frame_ref[...]), F32)
    spec_ref[...] = spectra([psf_ref[j] for j in range(psf_ref.shape[0])], t[0], t[1], parts)


def pack_kernel(obj_ref, psf_ref, right_ref, diagonal_ref):
    last = obj_ref[:, obj_ref.shape[1] - S :]
    right_ref[:S] = psf_ref[psf_ref.shape[0] - 1]
    diagonal_ref[:S] = psf_ref[psf_ref.shape[0] - 1]
    right_ref[S:] = last[:H]
    diagonal_ref[S:] = last[H:]


def model_kernel(
    flags, psf_ref, above_ref, right_ref, diagonal_ref, own_ref, spec_ref, total_ref, *refs
):
    hbm, refs = refs[:7], refs[7:]
    more_ref, mid_top, mid_bottom, first_ref, last_ref, flux_ref = refs[:6]
    buffers, (sems, psf_parts, x_ref, x_parts, top_parts, bottom_parts) = refs[6:14], refs[14:]
    row_edge, column_edge = flags[0], flags[1]
    sources = [hbm[0], hbm[1], hbm[2].at[0], hbm[2].at[column_edge], hbm[3].at[row_edge]] + list(hbm[4:7])
    t = Copies(sources, buffers, sems)
    alpha, beta = 1.0 - row_edge.astype(F32), 1.0 - column_edge.astype(F32)
    width = own_ref.shape[1]
    count = width // S
    psfs = [diagonal_ref[:S]] + [psf_ref[j] for j in range(count)] + [right_ref[:S]]
    more_ref[...] = spectra(psfs, t[0], t[1], psf_parts)
    for q in range(count):
        lo = q * S
        if q == 0:
            left = jnp.concatenate([diagonal_ref[S:], right_ref[S:]], axis=0)[:, H:]
        else:
            left = jnp.concatenate([above_ref[:, lo - S : lo], own_ref[:H, lo - S : lo]], axis=0)[:, H:]
        here = jnp.concatenate([above_ref[:, lo : lo + S], own_ref[:H, lo : lo + S]], axis=0)[:, :H]
        x_ref[at(q)] = jnp.concatenate([left, here], axis=1)
    first = dot(wide_parts(x_ref[:S]), t[3][...])
    others = dot(wide_parts(x_ref[S:]), t[2][...])
    for q in range(count):
        lanes = first if q == 0 else others[at(q - 1)]
        for w in range(2):
            store_parts(x_parts, at(2 * q + w), stacked(lanes[:, at(w, L)]))
    for q in range(count):
        x_spec = dot(t[4][...], x_parts[:, at(q, L)])
        y = {}
        for r in range(2):
            for w in range(2):
                x_re = x_spec[at(2 * r, L), at(w)]
                x_im = x_spec[at(2 * r + 1, L), at(w)]
                j = q - w
                if r == 0:
                    source, lanes = (spec_ref, at(j)) if j >= 0 else (more_ref, at(count + 1))
                else:
                    source, lanes = more_ref, at(j + 1)
                h_re, h_im = source[:L, lanes], source[L:, lanes]
                y[r, w] = (x_re * h_re - x_im * h_im, x_re * h_im + x_im * h_re)
        if q == 0:
            variants = [
                [tuple(y[r, 1][c] + beta * y[r, 0][c] for c in range(2)) for r in range(2)],
                [tuple(y[r, 0][c] + beta * y[r, 1][c] for c in range(2)) for r in range(2)],
            ]
        else:
            variants = [[tuple(y[r, 0][c] + y[r, 1][c] for c in range(2)) for r in range(2)]]
        for v, rows in enumerate(variants):
            slot = at(v if q == 0 else q + 1)
            both = [jnp.concatenate(parts, axis=0) for parts in rows]
            store_parts(top_parts, slot, both[1] + alpha * both[0])
            store_parts(bottom_parts, slot, both[0] + alpha * both[1])
    halves = (dot(t[5][...], top_parts[...]), dot(t[6][...], bottom_parts[...]))
    right = t[7]
    flux = 0.0
    for half, rows in enumerate(halves):
        first_left = dot(wide_parts(side_by_side(rows[:, at(0)])), right[:, :S])
        first_right = dot(wide_parts(side_by_side(rows[:, at(1)])), right[:, S:])
        rest = dot(
            wide_parts(jnp.concatenate([side_by_side(rows[:, at(q + 1)]) for q in range(1, count)], axis=0)),
            right[...],
        )
        lefts = [first_left] + [rest[at(q), :S] for q in range(count - 1)]
        rights = [first_right] + [rest[at(q), S:] for q in range(count - 1)]
        first_ref[at(half)] = lefts[0]
        last_ref[at(half)] = rights[-1]
        middle = mid_bottom if half else mid_top
        total = lefts[0] + rights[-1]
        for q in range(1, count):
            block = lefts[q] + rights[q - 1]
            middle[:, at(q - 1)] = block
            total = total + block
        flux = flux + jnp.sum(total)
    row = lax.broadcasted_iota(jnp.int32, flux_ref.shape, 0)
    flux_ref[...] = jnp.where(row < 4, flux, total_ref[...])


def gradient_kernel(
    flags, top_ref, bottom_ref, above_ref, below_ref,
    obs_ref, obs_above, obs_left, obs_diagonal, gain_ref, spec_ref, more_ref, *refs
):
    hbm, refs = refs[:7], refs[7:]
    residual_ref, out_top, out_bottom = refs[:3]
    buffers, (sems, r_ref, top_parts, bottom_parts, g_parts) = refs[3:11], refs[11:]
    row_edge, column_edge = flags[0], flags[1]
    sources = list(hbm[:5]) + [hbm[5].at[row_edge], hbm[6].at[0], hbm[6].at[column_edge]]
    t = Copies(sources, buffers, sems)
    alpha, beta = 1.0 - row_edge.astype(F32), 1.0 - column_edge.astype(F32)
    width = obs_ref.shape[1]
    count = width // S
    gain = gain_ref[0, 0]
    r_ref[:S] = gain * (top_ref[...] + above_ref[...])
    r_ref[S:] = gain * (bottom_ref[...] + below_ref[...])
    r_ref[:S, :S] -= obs_diagonal[...]
    r_ref[S:, :S] -= obs_left[...]
    r_ref[:S, S:] -= obs_above[...]
    r_ref[S:, S:] -= obs_ref[...]
    residual_ref[...] = r_ref[S:, S:]
    near = dot(wide_parts(r_ref[:, :S]), t[0][...])
    far = dot(wide_parts(r_ref[:, S : 2 * S]), t[1][...])
    lanes = [far + beta * near, near + beta * far]
    rest = dot(wide_parts(jnp.concatenate([r_ref[:, q * S : (q + 2) * S] for q in range(1, count)], axis=0)), t[2][...])
    lanes += [rest[at(q, L)] for q in range(count - 1)]
    for n, value in enumerate(lanes):
        store_parts(top_parts, at(n), stacked(value[:S]))
        store_parts(bottom_parts, at(n), stacked(value[S:]))
    top = dot(t[3][...], top_parts[...])
    bottom = dot(t[4][...], bottom_parts[...])
    rows = []
    for q in range(count):
        for w in range(2):
            slot = at(w if q == 0 else q + 1)
            j = q - w
            for r in range(2):
                if r == 0:
                    source, lanes = (spec_ref, at(j)) if j >= 0 else (more_ref, at(count + 1))
                    seen = bottom[:, slot] + alpha * top[:, slot]
                else:
                    source, lanes = more_ref, at(j + 1)
                    seen = top[:, slot] + alpha * bottom[:, slot]
                h_re, h_im = source[:L, lanes], source[L:, lanes]
                r_re, r_im = seen[:L], seen[L:]
                for c, part in enumerate((r_re * h_re + r_im * h_im, r_im * h_re - r_re * h_im)):
                    hi, lo = split(part)
                    place = (2 * r + c) * L
                    for n, value in enumerate((hi, lo, hi)):
                        g_parts[4 * n * L + place : 4 * n * L + place + L, at(w)] = value
        g = dot(t[5][...], g_parts[...])
        rows.append(jnp.concatenate([side_by_side(g[:, at(w)]) for w in range(2)], axis=1))
    first = dot(wide_parts(rows[0]), t[7][...]) * gain
    rest = dot(wide_parts(jnp.concatenate(rows[1:], axis=0)), t[6][...]) * gain
    grad = jnp.concatenate([first] + [rest[at(q)] for q in range(count - 1)], axis=1)
    out_top[...] = grad[:H]
    out_bottom[...] = grad[H:]


def f32(*shape):
    return jax.ShapeDtypeStruct(shape, F32)


def call(kernel, flags, operands, in_hbm, outs, scratch, flops):
    def spec(shape):
        return pl.BlockSpec(shape, lambda i, flags, n=len(shape): (0,) * n)

    kept = [pl.BlockSpec(memory_space=pltpu.HBM) for _ in in_hbm]
    size = sum(math.prod(x.shape) * x.dtype.itemsize for x in tuple(operands) + tuple(in_hbm))
    return pl.pallas_call(
        kernel,
        out_shape=outs,
        grid_spec=pltpu.PrefetchScalarGridSpec(
            num_scalar_prefetch=1,
            grid=(1,),
            in_specs=[spec(x.shape) for x in operands] + kept,
            out_specs=[spec(o.shape) for o in outs],
            scratch_shapes=scratch,
        ),
        compiler_params=pltpu.CompilerParams(vmem_limit_bytes=60 * 2**20),
        cost_estimate=pl.CostEstimate(flops=flops, bytes_accessed=size, transcendentals=0),
    )(flags, *operands, *in_hbm)


def buffer(table, picks=0):
    return pltpu.VMEM(table.shape[1:] if picks else table.shape, BF16)


def ring(value, axes, moves):
    sizes = [lax.axis_size(a) for a in axes]
    pairs = []
    for source in np.ndindex(*sizes):
        target = [(p + m) % n for p, m, n in zip(source, moves, sizes)]
        pairs.append((int(np.ravel_multi_index(source, sizes)), int(np.ravel_multi_index(target, sizes))))
    return lax.ppermute(value, axes, pairs)


def mirrored(value, axis, bits):
    count = lax.axis_size(axis)
    return lax.ppermute(value, axis, [(s, s ^ bits) for s in range(count)])


def summed(value, axis):
    count = lax.axis_size(axis)
    spread = jnp.broadcast_to(value[None], (count,) + value.shape)
    return jnp.sum(lax.all_to_all(spread, axis, 0, 0), axis=0)


def down(value):
    return ring(value, ("sy",), (1,))


def up(value):
    return ring(value, ("sy",), (-1,))


def per_device(object_field, frames_data, patch_psfs):
    rows, width = object_field.shape
    count = width // S
    psfs = patch_psfs.reshape(count, S, S)
    observed = frames_data[0]
    t = {name: jnp.asarray(value) for name, value in tables().items()}
    y, x = lax.axis_index("sy"), lax.axis_index("sx")
    flags = jnp.stack([y == 0, x == 0]).astype(jnp.int32)

    psf_above = down(psfs)
    obj_above = down(object_field[H:])
    pack_right, pack_diagonal = pl.pallas_call(
        pack_kernel, out_shape=(f32(S + H, S), f32(S + H, S))
    )(object_field, psfs)
    got_diagonal = ring(pack_diagonal, ("sy", "sx"), (1, 1))
    got_right = ring(pack_right, ("sx",), (1,))
    obs_above = down(observed)
    obs_last = observed[:, -S:]
    obs_left = ring(obs_last, ("sx",), (1,))
    obs_diagonal = ring(obs_last, ("sy", "sx"), (1, 1))

    semaphores = pltpu.SemaphoreType.DMA((8,))
    spec, total = call(
        psf_kernel,
        flags,
        (psfs, observed),
        (t["near_right"], t["near_left"]),
        (f32(2 * L, width), f32(8, S)),
        [buffer(t["near_right"]), buffer(t["near_left"]), pltpu.VMEM((6 * S, width), BF16), semaphores],
        6 * 84 * 10**6,
    )
    more, mid_top, mid_bottom, first, last, flux = call(
        model_kernel,
        flags,
        (psf_above, obj_above, got_right, got_diagonal, object_field, spec, total),
        tuple(t[k] for k in ("near_right", "near_left", "obj_right", "obj_left",
                             "top_inverse", "bottom_inverse", "out_right")),
        (f32(2 * L, width + 2 * S), f32(S, width - S), f32(S, width - S), f32(L, S), f32(L, S), f32(8, S)),
        [buffer(t["near_right"]), buffer(t["near_left"]), buffer(t["obj_right"], 1), buffer(t["obj_right"], 1),
         buffer(t["obj_left"], 1), buffer(t["top_inverse"]), buffer(t["bottom_inverse"]), buffer(t["out_right"]),
         semaphores,
         pltpu.VMEM((6 * S, width + 2 * S), BF16), pltpu.VMEM((width, S), F32),
         pltpu.VMEM((6 * S, 2 * width), BF16),
         pltpu.VMEM((6 * L, width + S), BF16), pltpu.VMEM((6 * L, width + S), BF16)],
        6 * 600 * 10**6,
    )
    mid_top, mid_bottom, first, last, obs_above, obs_left, obs_diagonal = lax.optimization_barrier(
        (mid_top, mid_bottom, first, last, obs_above, obs_left, obs_diagonal)
    )
    from_right = ring(first, ("sx",), (-1,))
    from_left = ring(last, ("sx",), (1,))
    flux = summed(flux, "sx")
    flux, from_left, from_right = lax.optimization_barrier((flux, from_left, from_right))
    wide_top = jnp.concatenate([first[:S] + from_left[:S], mid_top, last[:S] + from_right[:S]], axis=1)
    wide_bottom = jnp.concatenate([first[S:] + from_left[S:], mid_bottom, last[S:] + from_right[S:]], axis=1)
    below = up(wide_top)
    above = down(wide_bottom)
    flux = summed(flux, "sy")
    gain = jnp.full((8, S), flux[4, 0] / flux[0, 0])

    residual, g_top, g_bottom = call(
        gradient_kernel,
        flags,
        (wide_top, wide_bottom, above, below,
         observed, obs_above, obs_left, obs_diagonal, gain, spec, more),
        tuple(t[k] for k in ("near_right", "far_right", "res_right", "near_left",
                             "bottom_forward", "grad_left", "grad_right")),
        (f32(S, width), f32(H, width), f32(H, width)),
        [buffer(t["near_right"]), buffer(t["far_right"]), buffer(t["res_right"]), buffer(t["near_left"]),
         buffer(t["bottom_forward"]), buffer(t["grad_left"], 1), buffer(t["grad_right"], 1),
         buffer(t["grad_right"], 1), semaphores,
         pltpu.VMEM((L, width + S), F32), pltpu.VMEM((6 * S, width + S), BF16),
         pltpu.VMEM((6 * S, width + S), BF16), pltpu.VMEM((12 * L, L), BF16)],
        6 * 500 * 10**6,
    )
    bottom_other = mirrored(g_bottom, "fr", 1)
    top_other = ring(g_top, ("sy", "fr"), (-1, 1))
    top_same = up(g_top)
    total = jnp.concatenate([g_bottom + bottom_other, top_same + top_other], axis=0)
    side = ring(total[:, :H], ("sx",), (-1,))
    gradient = jnp.concatenate([total[:, H:], side], axis=1)
    return gradient, residual[None]


def solution(mesh):
    placed = (P("sy", "sx"), P("fr", "sy", "sx"), P("fr", "sy", "sx", None, None))
    return jax.shard_map(
        per_device,
        mesh=mesh,
        in_specs=placed,
        out_specs=(P("sy", "sx"), P("fr", "sy", "sx")),
        check_vma=False,
    )
```

time: 138 us -> 107 us (0.78)
  starting transfers between devices: 59.5 us -> 32.2 us
  waiting for transfers between devices: 33.8 us -> 8.77 us
  blocking collectives: 0 us -> 24.5 us
  local copies, waits for them, and re-layouts: 15.8 us -> 4.5 us
  Pallas kernels: 24.7 us -> 29.3 us
  other arithmetic: 1.49 us -> 5.42 us
    all_to_all x0 -> x2, blocking collectives: none -> 24.5 us  [summed(): return jnp.sum(lax.all_to_all(spread, axis, 0, 0), axis=0)]
    ppermute x16 -> x14, waiting for transfers between devices: 23.6 us -> 8.76 us  [ring(): return lax.ppermute(value, axes, pairs)]
    ppermute x16 -> x14, starting transfers between devices: 41.4 us -> 26.6 us  [ring(): return lax.ppermute(value, axes, pairs)]
    ppermute x11 -> x1, starting transfers between devices: 18.1 us -> 5.59 us  [mirrored(): return lax.ppermute(value, axis, [(s, s ^ bits) for s in range(count)])]
    unnamed x38 -> x22, local copies, waits for them, and re-layouts: 13.2 us -> 0.88 us
    ppermute x11 -> x1, waiting for transfers between devices: 10.2 us -> 0.01 us  [mirrored(): return lax.ppermute(value, axis, [(s, s ^ bits) for s in range(count)])]
    pallas_call x3, Pallas kernels: 24.7 us -> 27.6 us  [call(): pl.pallas_call(kernel, out_shape=outs, grid_spec=pltpu.PrefetchScalarGrid...]
    concatenate x4 -> x3, other arithmetic: 0.37 us -> 2.7 us  [the longest x1 0.96 us: per_device(): jnp.concatenate([first[:S] + from_left[:S], mid_top, last[:S] + from_righ...]
  transfers between devices with their start and end apart: 27 -> 15, of which waited for: 12 -> 4; matrix products, arithmetic and copies ran while one was open for 2% -> 5% of each run, Pallas kernels for 1% -> 17%
where the time goes in v2:
time: 107 us
  starting transfers between devices  32.2 us (30%)
  Pallas kernels  29.3 us (27%)
  blocking collectives  24.5 us (23%)
  waiting for transfers between devices  8.77 us (8%)
  other arithmetic  5.42 us (5%)
  local copies, waits for them, and re-layouts  4.5 us (4%)
  between operations  2.14 us (2%)
    pallas_call x3, Pallas kernels, call(): pl.pallas_call(kernel, out_shape=outs, grid_spec=pltpu.PrefetchScalarGrid...  27.6 us
    ppermute x14, starting transfers between devices, ring(): return lax.ppermute(value, axes, pairs)  26.6 us
    all_to_all x2, blocking collectives, summed(): return jnp.sum(lax.all_to_all(spread, axis, 0, 0), axis=0)  24.5 us
    ppermute x14, waiting for transfers between devices, ring(): return lax.ppermute(value, axes, pairs)  8.76 us
    ppermute x1, starting transfers between devices, mirrored(): return lax.ppermute(value, axis, [(s, s ^ bits) for s in range(count)])  5.59 us
  transfers between devices with their start and end apart: 15, of which 4 were waited for; matrix products, arithmetic and copies ran while one was open for 5% of the time, Pallas kernels for 17%

profile of v2, /device:TPU:1, one launch (start us, length us, event | category | flops | bytes accessed | tf_op | source)
XLA Modules:
  0.0 106.9 jit_solution(3280519888101435030)
XLA Ops:
  0.6 2.5 %collective-permute-start = (f32[4,128,128]{2,1,0:T(8,128)}, f32[4,128,128]{2,1,0:T(8,128)S(1)}, u32[]{:S(2)}, u32[]{:S(2)}) collective-permute-start(f32[4,128,128]{2,1,0:T(8,128)} %bitcast.6), channel_id=1, source_target_pairs={{0,16},{16,32},{32,48},{48,64},{64,80},{80,96},{96,112},{112,128},... | collective-permute-start | bytes 786440 | tf_op jit(solution)/shard_map/ppermute | solution.py:346
  3.2 0.8 slice.56
  4.0 3.4 %collective-permute-start.6 = (f32[128,128]{1,0:T(8,128)S(1)}, f32[128,128]{1,0:T(8,128)S(1)}, u32[]{:S(2)}, u32[]{:S(2)}) collective-permute-start(f32[128,128]{1,0:T(8,128)S(1)} %slice.56), channel_id=1, source_target_pairs={{0,18},{2,20},{4,22},{6,24},{8,26},{10,28},{12,30},{14,16},{16,34}... | collective-permute-start | bytes 196616 | tf_op jit(solution)/shard_map/ppermute | solution.py:346
  7.4 0.9 slice.42
  8.3 1.7 %collective-permute-start.1 = (f32[64,512]{1,0:T(8,128)S(1)}, f32[64,512]{1,0:T(8,128)S(1)}, u32[]{:S(2)}, u32[]{:S(2)}) collective-permute-start(f32[64,512]{1,0:T(8,128)S(1)} %slice.42), channel_id=1, source_target_pairs={{0,16},{16,32},{32,48},{48,64},{64,80},{80,96},{96,112},{112,128},... | collective-permute-start | bytes 393224 | tf_op jit(solution)/shard_map/ppermute | solution.py:346
  10.1 1.7 %shard_map.158 = (f32[192,128]{1,0:T(8,128)}, f32[192,128]{1,0:T(8,128)}) custom-call(f32[128,512]{1,0:T(8,128)} %own_ref.1, f32[4,128,128]{2,1,0:T(8,128)} %bitcast.7), custom_call_target="tpu_custom_call" | custom-call | tf_op jit(solution)/shard_map/pallas_call | solution.py:379
  11.8 1.3 %collective-permute-start.3 = (f32[192,128]{1,0:T(8,128)}, f32[192,128]{1,0:T(8,128)S(1)}, u32[]{:S(2)}, u32[]{:S(2)}) collective-permute-start(f32[192,128]{1,0:T(8,128)} %get-tuple-element.26), channel_id=1, source_target_pairs={{0,18},{2,20},{4,22},{6,24},{8,26},{10,28},{12,30},{14,16},{16,34}... | collective-permute-start | bytes 294920 | tf_op jit(solution)/shard_map/ppermute | solution.py:346
  13.1 0.6 add_convert_fusion.flags
  13.7 4.8 %shard_map.159 = (f32[512,512]{1,0:T(8,128)}, f32[8,128]{1,0:T(8,128)}) custom-call(s32[2]{0:T(128)} %add_convert_fusion.flags, f32[4,128,128]{2,1,0:T(8,128)} %bitcast.8, f32[128,512]{1,0:T(8,128)} %bitcast.10, bf16[384,256]{1,0:T(8,128)(2,1)} %constant.39.clone.right_hbm.refs_0_, bf16[512,768]{1,0:T(8,128)(2,1)} %constant.40.clone.left_hbm.refs_1_.refs_3_), custom_call_target="tpu_custom_call" | custom-call | flops 504000000 | bytes 1507328 | tf_op jit(solution)/shard_map/pallas_call | solution.py:321
  18.6 0.7 collective-permute-start.5
  19.3 2.6 %collective-permute-done.3.diagonal_ref = f32[192,128]{1,0:T(8,128)S(1)} collective-permute-done((f32[192,128]{1,0:T(8,128)}, f32[192,128]{1,0:T(8,128)S(1)}, u32[]{:S(2)}, u32[]{:S(2)}) %collective-permute-start.3) | collective-permute-done | bytes 98336 | tf_op jit(solution)/shard_map/ppermute | solution.py:346
  22.0 0.6 copy-done.8
  22.7 11.2 %shard_map.160 = (f32[512,768]{1,0:T(8,128)}, f32[128,384]{1,0:T(8,128)}, f32[128,384]{1,0:T(8,128)}, f32[256,128]{1,0:T(8,128)}, f32[256,128]{1,0:T(8,128)}, /*index=5*/f32[8,128]{1,0:T(8,128)}) custom-call(s32[2]{0:T(128)} %add_convert_fusion.flags, f32[4,128,128]{2,1,0:T(8,128)} %copy-done.5, f32[64,512]{1,0:T(8,128)} %copy-done.6, f32[192,128]{1,0:T(8,128)} %copy-done.7, ...), custom_call_target="tpu_custom_call" | custom-call | flops 3600000000 | bytes 8785920 | tf_op jit(solution)/shard_map/pallas_call | solution.py:321
  33.9 1.9 %collective-permute-start.8 = (f32[256,128]{1,0:T(8,128)}, f32[256,128]{1,0:T(8,128)S(1)}, u32[]{:S(2)}, u32[]{:S(2)}) collective-permute-start(f32[256,128]{1,0:T(8,128)} %get-tuple-element.33), channel_id=1, source_target_pairs={{0,14},{2,0},{4,2},{6,4},{8,6},{10,8},{12,10},{14,12},{1,15},{3,1}... | collective-permute-start | bytes 393224 | tf_op jit(solution)/shard_map/ppermute | solution.py:346
  35.9 0.7 broadcast_in_dim.8
  36.6 9.3 %all_to_all.10 = f32[8,8,128]{2,1,0:T(8,128)S(1)} all-to-all(f32[8,8,128]{2,1,0:T(8,128)S(1)} %broadcast_in_dim.8), channel_id=1, replica_groups=mesh['sy'=16,'sx'=8,'fr'=2] {'sx'}, dimensions={0} | all-to-all | bytes 65536 | tf_op jit(solution)/shard_map/all_to_all | solution.py:357
  45.9 1.0 slice_add_fusion
  46.9 1.0 pad_maximum_fusion.top_ref
  47.9 5.4 %collective-permute-start.10 = (f32[128,640]{1,0:T(8,128)S(1)}, f32[128,640]{1,0:T(8,128)S(1)}, u32[]{:S(2)}, u32[]{:S(2)}) collective-permute-start(f32[128,640]{1,0:T(8,128)S(1)} %pad_maximum_fusion.top_ref), channel_id=1, source_target_pairs={{0,240},{16,0},{32,16},{48,32},{64,48},{80,64},{96,80},{112,96},{1... | collective-permute-start | bytes 983048 | tf_op jit(solution)/shard_map/ppermute | solution.py:346
  53.3 1.0 pad_maximum_fusion.1.bottom_ref
  54.4 15.2 %all_to_all.11 = f32[16,8,128]{2,1,0:T(8,128)S(1)} all-to-all(f32[16,8,128]{2,1,0:T(8,128)S(1)} %broadcast_in_dim.9), channel_id=1, replica_groups=mesh['sy'=16,'sx'=8,'fr'=2] {'sy'}, dimensions={0} | all-to-all | bytes 131072 | tf_op jit(solution)/shard_map/all_to_all | solution.py:357
  71.4 0.7 broadcast_in_dim.20.gain_ref
  72.2 11.6 %shard_map.161 = (f32[128,512]{1,0:T(8,128)}, f32[64,512]{1,0:T(8,128)}, f32[64,512]{1,0:T(8,128)}) custom-call(s32[2]{0:T(128)} %add_convert_fusion.flags, f32[128,640]{1,0:T(8,128)} %copy-done, f32[128,640]{1,0:T(8,128)} %copy-done.1, f32[128,640]{1,0:T(8,128)} %copy-done.3, f32[128,640]{1,0:T(8,128)} %copy-done.2, f32[128,512]{1,0:T(8,128)} %bitcast.12, ...), custom_call_target="tpu_custom_call" | custom-call | flops 3000000000 | bytes 10883072 | tf_op jit(solution)/shard_map/pallas_call | solution.py:321
  83.8 5.6 %collective-permute-start.11 = (f32[64,512]{1,0:T(8,128)}, f32[64,512]{1,0:T(8,128)S(1)}, u32[]{:S(2)}, u32[]{:S(2)}) collective-permute-start(f32[64,512]{1,0:T(8,128)} %get-tuple-element.45), channel_id=1, source_target_pairs={{0,1},{1,0},{2,3},{3,2},{4,5},{5,4},{6,7},{7,6},{8,9},{9,8},{10,11... | collective-permute-start | bytes 393224 | tf_op jit(solution)/shard_map/ppermute | solution.py:351
  89.4 1.1 %collective-permute-start.13 = (f32[64,512]{1,0:T(8,128)}, f32[64,512]{1,0:T(8,128)S(1)}, u32[]{:S(2)}, u32[]{:S(2)}) collective-permute-start(f32[64,512]{1,0:T(8,128)} %get-tuple-element.46), channel_id=1, source_target_pairs={{0,241},{1,240},{16,1},{17,0},{32,17},{33,16},{48,33},{49,32},{64,... | collective-permute-start | bytes 393224 | tf_op jit(solution)/shard_map/ppermute | solution.py:346
  90.5 2.9 %collective-permute-start.12 = (f32[64,512]{1,0:T(8,128)}, f32[64,512]{1,0:T(8,128)S(1)}, u32[]{:S(2)}, u32[]{:S(2)}) collective-permute-start(f32[64,512]{1,0:T(8,128)} %get-tuple-element.46), channel_id=1, source_target_pairs={{0,240},{16,0},{32,16},{48,32},{64,48},{80,64},{96,80},{112,96},{1... | collective-permute-start | bytes 393224 | tf_op jit(solution)/shard_map/ppermute | solution.py:346
  93.4 0.9 add.22
  94.3 3.6 %collective-permute-done.13 = f32[64,512]{1,0:T(8,128)S(1)} collective-permute-done((f32[64,512]{1,0:T(8,128)}, f32[64,512]{1,0:T(8,128)S(1)}, u32[]{:S(2)}, u32[]{:S(2)}) %collective-permute-start.13) | collective-permute-done | bytes 131104 | tf_op jit(solution)/shard_map/ppermute | solution.py:346
  97.9 0.6 collective-permute-done.12
  98.5 5.5 %collective-permute-start.14 = (f32[128,64]{1,0:T(8,128)S(1)}, f32[128,64]{1,0:T(8,128)S(1)}, u32[]{:S(2)}, u32[]{:S(2)}) collective-permute-start(f32[128,64]{1,0:T(8,128)S(1)} %pad_maximum_fusion.3), channel_id=1, source_target_pairs={{0,14},{2,0},{4,2},{6,4},{8,6},{10,8},{12,10},{14,12},{1,15},{3,1}... | collective-permute-start | bytes 98312 | tf_op jit(solution)/shard_map/ppermute | solution.py:346
  104.1 2.0 %collective-permute-done.14 = f32[128,64]{1,0:T(8,128)S(1)} collective-permute-done((f32[128,64]{1,0:T(8,128)S(1)}, f32[128,64]{1,0:T(8,128)S(1)}, u32[]{:S(2)}, u32[]{:S(2)}) %collective-permute-start.14) | collective-permute-done | bytes 32800 | tf_op jit(solution)/shard_map/ppermute | solution.py:346
  106.1 0.8 pad_maximum_fusion.2
  (43 shorter events, 1.2 us)
Async XLA Ops:
  0.6 21.3 %collective-permute-start = (f32[4,128,128]{2,1,0:T(8,128)}, f32[4,128,128]{2,1,0:T(8,128)S(1)}, u32[]{:S(2)}, u32[]{:S(2)}) collective-permute-start(f32[4,128,128]{2,1,0:T(8,128)} %bitcast.6), channel_id=1, source_target_pairs={{0,16},{16,32},{32,48},{48,64},{64,80},{80,96},{96,112},{112,128},... | collective-permute-start | bytes 786440 | tf_op jit(solution)/shard_map/ppermute | solution.py:346
  4.0 29.9 %collective-permute-start.6 = (f32[128,128]{1,0:T(8,128)S(1)}, f32[128,128]{1,0:T(8,128)S(1)}, u32[]{:S(2)}, u32[]{:S(2)}) collective-permute-start(f32[128,128]{1,0:T(8,128)S(1)} %slice.56), channel_id=1, source_target_pairs={{0,18},{2,20},{4,22},{6,24},{8,26},{10,28},{12,30},{14,16},{16,34}... | collective-permute-start | bytes 196616 | tf_op jit(solution)/shard_map/ppermute | solution.py:346
  8.3 13.6 %collective-permute-start.1 = (f32[64,512]{1,0:T(8,128)S(1)}, f32[64,512]{1,0:T(8,128)S(1)}, u32[]{:S(2)}, u32[]{:S(2)}) collective-permute-start(f32[64,512]{1,0:T(8,128)S(1)} %slice.42), channel_id=1, source_target_pairs={{0,16},{16,32},{32,48},{48,64},{64,80},{80,96},{96,112},{112,128},... | collective-permute-start | bytes 393224 | tf_op jit(solution)/shard_map/ppermute | solution.py:346
  11.8 6.8 %collective-permute-start.2 = (f32[192,128]{1,0:T(8,128)}, f32[192,128]{1,0:T(8,128)S(1)}, u32[]{:S(2)}, u32[]{:S(2)}) collective-permute-start(f32[192,128]{1,0:T(8,128)} %get-tuple-element.25), channel_id=1, source_target_pairs={{0,2},{2,4},{4,6},{6,8},{8,10},{10,12},{12,14},{14,0},{1,3},{3,5},... | collective-permute-start | bytes 294920 | tf_op jit(solution)/shard_map/ppermute | solution.py:346
  11.8 10.1 %collective-permute-start.3 = (f32[192,128]{1,0:T(8,128)}, f32[192,128]{1,0:T(8,128)S(1)}, u32[]{:S(2)}, u32[]{:S(2)}) collective-permute-start(f32[192,128]{1,0:T(8,128)} %get-tuple-element.26), channel_id=1, source_target_pairs={{0,18},{2,20},{4,22},{6,24},{8,26},{10,28},{12,30},{14,16},{16,34}... | collective-permute-start | bytes 294920 | tf_op jit(solution)/shard_map/ppermute | solution.py:346
  18.6 3.3 %copy-start.7 = (f32[192,128]{1,0:T(8,128)}, f32[192,128]{1,0:T(8,128)S(1)}, u32[]{:S(2)}) copy-start(f32[192,128]{1,0:T(8,128)S(1)} %collective-permute-done.2.right_ref) | copy-start | bytes 294916
  18.6 15.3 %collective-permute-start.5 = (f32[128,128]{1,0:T(8,128)S(1)}, f32[128,128]{1,0:T(8,128)S(1)}, u32[]{:S(2)}, u32[]{:S(2)}) collective-permute-start(f32[128,128]{1,0:T(8,128)S(1)} %slice.56), channel_id=1, source_target_pairs={{0,2},{2,4},{4,6},{6,8},{8,10},{10,12},{12,14},{14,0},{1,3},{3,5},... | collective-permute-start | bytes 196616 | tf_op jit(solution)/shard_map/ppermute | solution.py:346
  21.9 0.6 copy-start.8
  21.9 12.0 %collective-permute-start.4 = (f32[128,512]{1,0:T(8,128)}, f32[128,512]{1,0:T(8,128)S(1)}, u32[]{:S(2)}, u32[]{:S(2)}) collective-permute-start(f32[128,512]{1,0:T(8,128)} %bitcast.11), channel_id=1, source_target_pairs={{0,16},{16,32},{32,48},{48,64},{64,80},{80,96},{96,112},{112,128},... | collective-permute-start | bytes 786440 | tf_op jit(solution)/shard_map/ppermute | solution.py:346
  21.9 0.7 copy-start.6
  21.9 0.7 copy-start.5
  33.9 38.2 %copy-start.9 = (f32[128,128]{1,0:T(8,128)}, f32[128,128]{1,0:T(8,128)S(1)}, u32[]{:S(2)}) copy-start(f32[128,128]{1,0:T(8,128)S(1)} %collective-permute-done.6.obs_diagonal) | copy-start | bytes 196612
  33.9 38.1 %copy-start.10 = (f32[128,128]{1,0:T(8,128)}, f32[128,128]{1,0:T(8,128)S(1)}, u32[]{:S(2)}) copy-start(f32[128,128]{1,0:T(8,128)S(1)} %collective-permute-done.5.obs_left) | copy-start | bytes 196612
  33.9 38.1 %copy-start.4 = (f32[128,512]{1,0:T(8,128)}, f32[128,512]{1,0:T(8,128)S(1)}, u32[]{:S(2)}) copy-start(f32[128,512]{1,0:T(8,128)S(1)} %collective-permute-done.4.obs_above) | copy-start | bytes 786436
  33.9 12.0 %collective-permute-start.8 = (f32[256,128]{1,0:T(8,128)}, f32[256,128]{1,0:T(8,128)S(1)}, u32[]{:S(2)}, u32[]{:S(2)}) collective-permute-start(f32[256,128]{1,0:T(8,128)} %get-tuple-element.33), channel_id=1, source_target_pairs={{0,14},{2,0},{4,2},{6,4},{8,6},{10,8},{12,10},{14,12},{1,15},{3,1}... | collective-permute-start | bytes 393224 | tf_op jit(solution)/shard_map/ppermute | solution.py:346
  35.8 10.1 %collective-permute-start.7 = (f32[256,128]{1,0:T(8,128)}, f32[256,128]{1,0:T(8,128)S(1)}, u32[]{:S(2)}, u32[]{:S(2)}) collective-permute-start(f32[256,128]{1,0:T(8,128)} %get-tuple-element.35), channel_id=1, source_target_pairs={{0,2},{2,4},{4,6},{6,8},{8,10},{10,12},{12,14},{14,0},{1,3},{3,5},... | collective-permute-start | bytes 393224 | tf_op jit(solution)/shard_map/ppermute | solution.py:346
  47.9 24.2 %copy-start = (f32[128,640]{1,0:T(8,128)}, f32[128,640]{1,0:T(8,128)S(1)}, u32[]{:S(2)}) copy-start(f32[128,640]{1,0:T(8,128)S(1)} %pad_maximum_fusion.top_ref) | copy-start | bytes 983044
  47.9 23.5 %collective-permute-start.10 = (f32[128,640]{1,0:T(8,128)S(1)}, f32[128,640]{1,0:T(8,128)S(1)}, u32[]{:S(2)}, u32[]{:S(2)}) collective-permute-start(f32[128,640]{1,0:T(8,128)S(1)} %pad_maximum_fusion.top_ref), channel_id=1, source_target_pairs={{0,240},{16,0},{32,16},{48,32},{64,48},{80,64},{96,80},{112,96},{1... | collective-permute-start | bytes 983048 | tf_op jit(solution)/shard_map/ppermute | solution.py:346
  54.3 17.8 %copy-start.1 = (f32[128,640]{1,0:T(8,128)}, f32[128,640]{1,0:T(8,128)S(1)}, u32[]{:S(2)}) copy-start(f32[128,640]{1,0:T(8,128)S(1)} %pad_maximum_fusion.1.bottom_ref) | copy-start | bytes 983044
  54.3 17.1 %collective-permute-start.9 = (f32[128,640]{1,0:T(8,128)S(1)}, f32[128,640]{1,0:T(8,128)S(1)}, u32[]{:S(2)}, u32[]{:S(2)}) collective-permute-start(f32[128,640]{1,0:T(8,128)S(1)} %pad_maximum_fusion.1.bottom_ref), channel_id=1, source_target_pairs={{0,16},{16,32},{32,48},{48,64},{64,80},{80,96},{96,112},{112,128},... | collective-permute-start | bytes 983048 | tf_op jit(solution)/shard_map/ppermute | solution.py:346
  71.4 0.7 copy-start.2
  71.4 0.8 copy-start.3
  83.8 9.6 %collective-permute-start.11 = (f32[64,512]{1,0:T(8,128)}, f32[64,512]{1,0:T(8,128)S(1)}, u32[]{:S(2)}, u32[]{:S(2)}) collective-permute-start(f32[64,512]{1,0:T(8,128)} %get-tuple-element.45), channel_id=1, source_target_pairs={{0,1},{1,0},{2,3},{3,2},{4,5},{5,4},{6,7},{7,6},{8,9},{9,8},{10,11... | collective-permute-start | bytes 393224 | tf_op jit(solution)/shard_map/ppermute | solution.py:351
  89.4 8.5 %collective-permute-start.13 = (f32[64,512]{1,0:T(8,128)}, f32[64,512]{1,0:T(8,128)S(1)}, u32[]{:S(2)}, u32[]{:S(2)}) collective-permute-start(f32[64,512]{1,0:T(8,128)} %get-tuple-element.46), channel_id=1, source_target_pairs={{0,241},{1,240},{16,1},{17,0},{32,17},{33,16},{48,33},{49,32},{64,... | collective-permute-start | bytes 393224 | tf_op jit(solution)/shard_map/ppermute | solution.py:346
  90.5 8.0 %collective-permute-start.12 = (f32[64,512]{1,0:T(8,128)}, f32[64,512]{1,0:T(8,128)S(1)}, u32[]{:S(2)}, u32[]{:S(2)}) collective-permute-start(f32[64,512]{1,0:T(8,128)} %get-tuple-element.46), channel_id=1, source_target_pairs={{0,240},{16,0},{32,16},{48,32},{64,48},{80,64},{96,80},{112,96},{1... | collective-permute-start | bytes 393224 | tf_op jit(solution)/shard_map/ppermute | solution.py:346
  98.5 7.6 %collective-permute-start.14 = (f32[128,64]{1,0:T(8,128)S(1)}, f32[128,64]{1,0:T(8,128)S(1)}, u32[]{:S(2)}, u32[]{:S(2)}) collective-permute-start(f32[128,64]{1,0:T(8,128)S(1)} %pad_maximum_fusion.3), channel_id=1, source_target_pairs={{0,14},{2,0},{4,2},{6,4},{8,6},{10,8},{12,10},{14,12},{1,15},{3,1}... | collective-permute-start | bytes 98312 | tf_op jit(solution)/shard_map/ppermute | solution.py:346

commit v3 on v2

v3 whole, which is shorter than its diff:
```python
import functools
import math

import jax
import jax.numpy as jnp
import numpy as np
from jax import lax
from jax.experimental import pallas as pl
from jax.experimental.pallas import tpu as pltpu
from jax.sharding import PartitionSpec as P

S = 128
L = 256
H = 64
F32 = jnp.float32
BF16 = jnp.bfloat16


def half_windows():
    n = np.arange(L, dtype=np.float64)
    s = np.sin(np.pi * (n + 0.5) / L) ** 2
    return s[:S], s[S:]


def phases(freqs, positions):
    product = (2 * np.arange(freqs)[:, None] + 1) * positions[None, :] % (2 * L)
    angle = product.astype(np.float64) * (math.pi / L)
    return np.cos(angle), np.sin(angle)


def forward_left(positions):
    c, s = phases(L, positions)
    return np.block([[c, s], [-s, c]])


def inverse_left(positions):
    c, s = phases(L, positions)
    return np.block([[c.T, -s.T], [s.T, c.T]]) / L


def forward_right(positions):
    c, s = phases(S, positions)
    return np.concatenate([c.T, -s.T], axis=1)


def inverse_right(positions):
    c, s = phases(S, positions)
    return np.concatenate([c, -s], axis=0) * (2.0 / L)


def bf16_parts(table):
    hi = table.astype(np.float32).astype(BF16)
    lo = (table - hi.astype(np.float64)).astype(np.float32).astype(BF16)
    return hi, lo


def left_table(table):
    hi, lo = bf16_parts(table)
    return np.concatenate([hi, hi, lo], axis=-1)


def right_table(table):
    hi, lo = bf16_parts(table)
    return np.concatenate([hi, hi, lo], axis=-2)


@functools.lru_cache(maxsize=1)
def tables():
    near = np.arange(S)
    up, down = half_windows()
    pairs = ((up, down), (np.where(near < H, 0.0, up), np.where(near < H, down, 0.0)))
    base, back = forward_left(near), inverse_left(near)
    t = {}
    t["near_right"] = right_table(forward_right(near))
    t["near_left"] = left_table(base)
    t["obj_left"] = np.stack(
        [left_table(np.concatenate([base * np.tile(w, 2)[None, :] for w in pair], axis=0)) for pair in pairs]
    )
    t["near_inverse"] = left_table(back)
    t["out_right"] = right_table(inverse_right(np.arange(L)))
    t["res_right"] = right_table(forward_right(np.arange(L)))
    t["grad_left"] = np.stack(
        [left_table(np.concatenate([np.tile(w, 2)[:, None] * back for w in pair], axis=1)) for pair in pairs]
    )
    t["grad_right"] = right_table(inverse_right(near))
    t["windows"] = np.stack([np.stack([np.tile(w, (8, 1)) for w in pair]) for pair in pairs]).astype(np.float32)
    return t


def split(value):
    hi = value.astype(BF16)
    return hi, (value - hi.astype(F32)).astype(BF16)


def wide_parts(value):
    hi, lo = split(value)
    return jnp.concatenate([hi, lo, hi], axis=1)


def store_parts(ref, lanes, value):
    hi, lo = split(value)
    depth = value.shape[0]
    ref[:depth, lanes] = hi
    ref[depth : 2 * depth, lanes] = lo
    ref[2 * depth :, lanes] = hi


def dot(a, b):
    return jnp.dot(a, b, preferred_element_type=F32)


def stacked(value):
    half = value.shape[1] // 2
    return jnp.concatenate([value[:, :half], value[:, half:]], axis=0)


def side_by_side(value):
    half = value.shape[0] // 2
    return jnp.concatenate([value[:half], value[half:]], axis=1)


def at(n, size=S):
    return slice(n * size, (n + 1) * size)


class Copies:
    def __init__(self, names, sources, refs, semaphores):
        self.buffers = dict(zip(names, refs))
        self.copies = {
            name: pltpu.make_async_copy(source, buffer, semaphores.at[n])
            for n, (name, source, buffer) in enumerate(zip(names, sources, refs))
        }
        self.waited = set()
        for name in names:
            self.copies[name].start()

    def __getitem__(self, name):
        if name not in self.waited:
            self.waited.add(name)
            self.copies[name].wait()
        return self.buffers[name]


def edges():
    return [(lax.axis_index(axis) == 0).astype(jnp.int32) for axis in ("sy", "sx")]


def picked(names, hbm):
    rows, columns = edges()
    edge = {"obj_left": rows, "grad_left": rows, "windows": columns}
    return [h.at[edge[n]] if n in edge else h for n, h in zip(names, hbm)]


def psf_kernel(names, *refs):
    total = len(names)
    hbm, refs = refs[:total], refs[total:]
    spec_hbm, spec_ref, total_ref, *buffers = refs[:-4]
    psf, frame, sems, parts = refs[-4:]
    t = Copies(names, picked(names, hbm), (psf, frame) + tuple(buffers), sems)
    psf = t["psf"]
    lanes = dot(wide_parts(jnp.concatenate([psf[j] for j in range(psf.shape[0])], axis=0)), t["near_right"][...])
    for j in range(psf.shape[0]):
        store_parts(parts, at(j), stacked(lanes[at(j)]))
    spec_ref[...] = dot(t["near_left"][...], parts[...])
    out = pltpu.make_async_copy(spec_ref, spec_hbm, sems.at[total])
    out.start()
    total_ref[...] = jnp.full(total_ref.shape, jnp.sum(t["frame"][...]), F32)
    for name in names:
        t[name]
    out.wait()


def pack_kernel(obj_ref, frame_ref, psf_ref, down_ref, right_ref, diagonal_ref, frame_last):
    width = obj_ref.shape[1]
    last = obj_ref[:, width - S :]
    down_ref[...] = obj_ref[H:]
    right_ref[:S] = psf_ref[psf_ref.shape[0] - 1]
    right_ref[S:] = last[:H]
    diagonal_ref[:S] = psf_ref[psf_ref.shape[0] - 1]
    diagonal_ref[S:] = last[H:]
    frame_last[...] = frame_ref[:, width - S :]


def alternating():
    k = lax.broadcasted_iota(jnp.int32, (L, S), 0)
    return jnp.where(k % 2 == 0, 1.0, -1.0).astype(F32)


def model_kernel(names, ready, *refs):
    total = len(names)
    hbm, refs = refs[:total], refs[total:]
    t, refs = dict(zip(ready, refs)), refs[len(ready) :]
    outs_hbm, flux_ref, refs = refs[:5], refs[5], refs[6:]
    buffers, sems, (more_ref, mid_top, mid_bottom, first_ref, last_ref) = refs[:total], refs[total], refs[total + 1 : total + 6]
    x_ref, x_parts, y_parts = refs[total + 6 :]
    got = Copies(names, hbm, buffers, sems)
    outs = [
        pltpu.make_async_copy(source, out, sems.at[total + n])
        for n, (source, out) in enumerate(zip((more_ref, mid_top, mid_bottom, first_ref, last_ref), outs_hbm))
    ]
    row_edge, column_edge = edges()
    alpha, beta = 1.0 - row_edge.astype(F32), 1.0 - column_edge.astype(F32)
    right_ref, diagonal_ref, above_ref, own_ref = [got[n] for n in ("right", "diagonal", "above", "own")]
    count = own_ref.shape[1] // S
    windows = [t["windows"][w, :1] for w in range(2)]
    plain = [t["plain"][w, :1] for w in range(2)]
    for q in range(count):
        lo = q * S
        if q == 0:
            left = jnp.concatenate([diagonal_ref[S:], right_ref[S:]], axis=0)[:, H:]
        else:
            left = jnp.concatenate([above_ref[:, lo - S : lo], own_ref[:H, lo - S : lo]], axis=0)[:, H:]
        here = jnp.concatenate([above_ref[:, lo : lo + S], own_ref[:H, lo : lo + S]], axis=0)[:, :H]
        x = jnp.concatenate([left, here], axis=1)
        for w in range(2):
            x_ref[at(2 * q + w)] = x * (windows if q == 0 else plain)[w]
    psf_above = got["psf_above"]
    psfs = [diagonal_ref[:S]] + [psf_above[j] for j in range(count)] + [right_ref[:S]]
    lanes = dot(wide_parts(jnp.concatenate([x_ref[...]] + psfs, axis=0)), t["near_right"][...])
    for n in range(3 * count + 2):
        store_parts(x_parts, at(n), stacked(lanes[at(n)]))
    more_ref[...] = dot(t["near_left"][...], x_parts[:, 2 * count * S :])
    outs[0].start()
    spec_ref = t["spec"]
    obj_left = t["obj_left"]
    sign = alternating()
    for pair in range(count // 2):
        x_specs = dot(obj_left[...], x_parts[:, pair * 4 * S : (pair + 1) * 4 * S])
        for q in (2 * pair, 2 * pair + 1):
            y = {}
            for r in range(2):
                for w in range(2):
                    lanes = at(2 * (q % 2) + w)
                    x_re = x_specs[at(2 * r, L), lanes]
                    x_im = x_specs[at(2 * r + 1, L), lanes]
                    j = q - w
                    if r == 0:
                        source, lanes = (spec_ref, at(j)) if j >= 0 else (more_ref, at(count + 1))
                    else:
                        source, lanes = more_ref, at(j + 1)
                    h_re, h_im = source[:L, lanes], source[L:, lanes]
                    y[r, w] = (x_re * h_re - x_im * h_im, x_re * h_im + x_im * h_re)
            if q == 0:
                variants = [
                    [tuple(y[r, 1][c] + beta * y[r, 0][c] for c in range(2)) for r in range(2)],
                    [tuple(y[r, 0][c] + beta * y[r, 1][c] for c in range(2)) for r in range(2)],
                ]
            else:
                variants = [[tuple(y[r, 0][c] + y[r, 1][c] for c in range(2)) for r in range(2)]]
            for v, (upper, lower) in enumerate(variants):
                slot = v if q == 0 else q + 1
                top = [lower[c] + alpha * upper[c] for c in range(2)]
                bottom = [upper[c] + alpha * lower[c] for c in range(2)]
                store_parts(y_parts, at(slot), jnp.concatenate(top, axis=0))
                turned = jnp.concatenate([-sign * bottom[1], sign * bottom[0]], axis=0)
                store_parts(y_parts, at(count + 1 + slot), turned)
    rows = dot(t["near_inverse"][...], y_parts[...])
    blocks = jnp.concatenate([side_by_side(rows[:, at(n)]) for n in range(2 * count + 2)], axis=0)
    out = dot(wide_parts(blocks), t["out_right"][...])
    flux = 0.0
    for half in range(2):
        base = half * (count + 1)
        lefts = [out[at(base), :S]] + [out[at(base + q + 1), :S] for q in range(1, count)]
        rights = [out[at(base + q + 1), S:] for q in range(count)]
        first_ref[at(half)] = lefts[0]
        last_ref[at(half)] = rights[-1]
        middle = mid_bottom if half else mid_top
        together = lefts[0] + rights[-1]
        for q in range(1, count):
            block = lefts[q] + rights[q - 1]
            middle[:, at(q - 1)] = block
            together = together + block
        flux = flux + jnp.sum(together)
    for copy in outs[1:]:
        copy.start()
    row = lax.broadcasted_iota(jnp.int32, flux_ref.shape, 1)
    flux_ref[...] = jnp.where(row < 4, flux, t["total"][...][None])
    for copy in outs:
        copy.wait()


def edge_kernel(first, last, from_left, from_right, flux_ref, top_ref, bottom_ref, totals_ref):
    for half, out in ((0, top_ref), (1, bottom_ref)):
        out[:, :S] = first[at(half)] + from_left[at(half)]
        out[:, S:] = last[at(half)] + from_right[at(half)]
    totals_ref[...] = jnp.broadcast_to(jnp.sum(flux_ref[...], axis=0)[None], totals_ref.shape)


def gradient_kernel(names, *refs):
    total = len(names)
    hbm, refs = refs[:total], refs[total:]
    residual_hbm, top_hbm, bottom_hbm = refs[:3]
    buffers, sems, (residual_ref, out_top, out_bottom) = refs[3 : 3 + total], refs[3 + total], refs[4 + total : 7 + total]
    r_ref, r_parts, g_parts = refs[7 + total :]
    t = Copies(names, picked(names, hbm), buffers, sems)
    sent = [
        pltpu.make_async_copy(source, out, sems.at[total + n])
        for n, (source, out) in enumerate(
            zip((residual_ref, out_top, out_bottom), (residual_hbm, top_hbm, bottom_hbm))
        )
    ]
    row_edge, column_edge = edges()
    alpha, beta = 1.0 - row_edge.astype(F32), 1.0 - column_edge.astype(F32)
    width = residual_ref.shape[1]
    count = width // S
    sums = jnp.sum(t["flux"][...], axis=0)
    gain = sums[4, 0] / sums[0, 0]
    r_ref[:S, S:width] = gain * (t["mid_top"][...] + t["mid_above"][...]) - t["obs_above"][:, : width - S]
    r_ref[S:, S:width] = gain * (t["mid_bottom"][...] + t["mid_below"][...]) - t["obs"][:, : width - S]
    top, bottom, above, below = (t[n] for n in ("edge_top", "edge_bottom", "edge_above", "edge_below"))
    r_ref[:S, :S] = gain * (top[:, :S] + above[:, :S]) - t["obs_diagonal"][...]
    r_ref[S:, :S] = gain * (bottom[:, :S] + below[:, :S]) - t["obs_left"][...]
    r_ref[:S, width:] = gain * (top[:, S:] + above[:, S:]) - t["obs_above"][:, width - S :]
    r_ref[S:, width:] = gain * (bottom[:, S:] + below[:, S:]) - t["obs"][:, width - S :]
    residual_ref[...] = r_ref[S:, S:]
    sent[0].start()
    near, far = r_ref[:, :S], r_ref[:, S : 2 * S]
    blocks = [
        jnp.concatenate([beta * near, far], axis=1),
        jnp.concatenate([near, beta * far], axis=1),
    ] + [r_ref[:, q * S : (q + 2) * S] for q in range(1, count)]
    lanes = dot(wide_parts(jnp.concatenate(blocks, axis=0)), t["res_right"][...])
    for n in range(count + 1):
        value = lanes[at(n, L)]
        store_parts(r_parts, at(n), stacked(value[:S]))
        store_parts(r_parts, at(count + 1 + n), stacked(value[S:]))
    spectra = dot(t["near_left"][...], r_parts[...])
    sign = alternating()
    spec_ref, more_ref = t["spec"], t["more"]
    seen = []
    for n in range(count + 1):
        top = [spectra[at(c, L), at(n)] for c in range(2)]
        raw = [spectra[at(c, L), at(count + 1 + n)] for c in range(2)]
        bottom = [sign * raw[1], -sign * raw[0]]
        seen.append(
            [
                [bottom[c] + alpha * top[c] for c in range(2)],
                [top[c] + alpha * bottom[c] for c in range(2)],
            ]
        )
    grad_left = t["grad_left"]
    outs = []
    for pair in range(count // 2):
        for q in (2 * pair, 2 * pair + 1):
            for w in range(2):
                slot = w if q == 0 else q + 1
                j = q - w
                for r in range(2):
                    if r == 0:
                        source, lanes = (spec_ref, at(j)) if j >= 0 else (more_ref, at(count + 1))
                    else:
                        source, lanes = more_ref, at(j + 1)
                    h_re, h_im = source[:L, lanes], source[L:, lanes]
                    r_re, r_im = seen[slot][r]
                    for c, part in enumerate((r_re * h_re + r_im * h_im, r_im * h_re - r_re * h_im)):
                        hi, lo = split(part)
                        place = (2 * r + c) * L
                        for n, value in enumerate((hi, lo, hi)):
                            g_parts[4 * n * L + place : 4 * n * L + place + L, at(2 * q + w)] = value
        g = dot(grad_left[...], g_parts[:, pair * 4 * S : (pair + 1) * 4 * S])
        outs += [side_by_side(g[:, at(n)]) for n in range(4)]
    out = dot(wide_parts(jnp.concatenate(outs, axis=0)), t["grad_right"][...])
    for q in range(count):
        windows = t["windows"] if q == 0 else t["plain"]
        grad = gain * (out[at(2 * q)] * windows[0, :1] + out[at(2 * q + 1)] * windows[1, :1])
        out_top[:, at(q)] = grad[:H]
        out_bottom[:, at(q)] = grad[H:]
    for copy in sent[1:]:
        copy.start()
    for copy in sent:
        copy.wait()


def f32(*shape):
    return jax.ShapeDtypeStruct(shape, F32)


def call(kernel, named, ready, outs, scratch, limit, flops):
    hbm, vmem = pl.BlockSpec(memory_space=pltpu.HBM), pl.BlockSpec(memory_space=pltpu.VMEM)
    held = [pltpu.with_memory_space_constraint(x, pltpu.HBM) for x in named.values()]
    size = sum(math.prod(x.shape) * x.dtype.itemsize for x in named.values())
    return pl.pallas_call(
        kernel,
        out_shape=[place(o.shape, o.dtype) for place, o in outs],
        in_specs=[hbm] * len(named) + [vmem] * len(ready),
        out_specs=[hbm if place is pltpu.HBM else vmem for place, _ in outs],
        scratch_shapes=scratch,
        compiler_params=pltpu.CompilerParams(vmem_limit_bytes=limit * 2**20),
        cost_estimate=pl.CostEstimate(flops=flops, bytes_accessed=size, transcendentals=0),
    )(*held, *ready.values())


def like(arrays):
    return [pltpu.VMEM(x.shape[1:] if n in PICKED else x.shape, x.dtype) for n, x in arrays.items()]


PICKED = ("windows", "obj_left", "grad_left")


def ring(value, axes, moves):
    sizes = [lax.axis_size(a) for a in axes]
    pairs = []
    for source in np.ndindex(*sizes):
        target = [(p + m) % n for p, m, n in zip(source, moves, sizes)]
        pairs.append((int(np.ravel_multi_index(source, sizes)), int(np.ravel_multi_index(target, sizes))))
    return lax.ppermute(value, axes, pairs)


def mirrored(value, axis, bits):
    count = lax.axis_size(axis)
    return lax.ppermute(value, axis, [(s, s ^ bits) for s in range(count)])


def exchanged(value, axis):
    return lax.all_to_all(value, axis, 0, 0)


def down(value):
    return ring(value, ("sy",), (1,))


def up(value):
    return ring(value, ("sy",), (-1,))


def per_device(object_field, frames_data, patch_psfs):
    rows, width = object_field.shape
    count = width // S
    psfs = patch_psfs.reshape(count, S, S)
    observed = frames_data[0]
    t = {name: jnp.asarray(value) for name, value in tables().items()}
    psf_above = down(psfs)
    pack_down, pack_right, pack_diagonal, obs_last = pl.pallas_call(
        pack_kernel,
        out_shape=(f32(H, width), f32(S + H, S), f32(S + H, S), f32(S, S)),
    )(object_field, observed, psfs)
    obj_above = down(pack_down)
    got_diagonal = ring(pack_diagonal, ("sy", "sx"), (1, 1))
    got_right = ring(pack_right, ("sx",), (1,))
    obs_above = down(observed)
    obs_left = ring(obs_last, ("sx",), (1,))
    obs_diagonal = ring(obs_last, ("sy", "sx"), (1, 1))

    kept = {k: t[k] for k in ("near_right", "near_left", "windows", "obj_left", "near_inverse", "out_right")}
    named = {"psf": psfs, "frame": observed} | kept
    spec, spec_here, total, *got = call(
        functools.partial(psf_kernel, tuple(named)),
        named,
        {},
        [(pltpu.HBM, f32(2 * L, width)), (pltpu.VMEM, f32(2 * L, width)), (pltpu.VMEM, f32(8, S))]
        + [(pltpu.VMEM, x) for x in like(kept)],
        [pltpu.VMEM(psfs.shape, F32), pltpu.VMEM(observed.shape, F32),
         pltpu.SemaphoreType.DMA((len(named) + 1,)), pltpu.VMEM((6 * S, width), BF16)],
        16,
        6 * 84 * 10**6,
    )
    ready = dict(zip(kept, got)) | {"spec": spec_here, "total": total, "plain": t["windows"][0]}
    named = {"right": got_right, "diagonal": got_diagonal, "above": obj_above, "own": object_field,
             "psf_above": psf_above}
    outs = [f32(2 * L, width + 2 * S), f32(S, width - S), f32(S, width - S), f32(L, S), f32(L, S)]
    more, mid_top, mid_bottom, first, last, flux = call(
        functools.partial(model_kernel, tuple(named), tuple(ready)),
        named,
        ready,
        [(pltpu.HBM, o) for o in outs] + [(pltpu.VMEM, f32(lax.axis_size("sx"), 8, S))],
        like(named) + [pltpu.SemaphoreType.DMA((len(named) + len(outs),))]
        + [pltpu.VMEM(o.shape, F32) for o in outs]
        + [pltpu.VMEM((2 * width, S), F32), pltpu.VMEM((6 * S, 3 * width + 2 * S), BF16),
           pltpu.VMEM((6 * L, 2 * width + 2 * S), BF16)],
        36,
        6 * 600 * 10**6,
    )
    mid_top, mid_bottom, first, last, flux, obs_above, obs_left, obs_diagonal = lax.optimization_barrier(
        (mid_top, mid_bottom, first, last, flux, obs_above, obs_left, obs_diagonal)
    )
    mid_below = up(mid_top)
    mid_above = down(mid_bottom)
    from_right = ring(first, ("sx",), (-1,))
    from_left = ring(last, ("sx",), (1,))
    flux = exchanged(flux, "sx")
    edge_top, edge_bottom, flux = pl.pallas_call(
        edge_kernel, out_shape=(f32(S, L), f32(S, L), f32(lax.axis_size("sy"), 8, S))
    )(first, last, from_left, from_right, flux)
    edge_below = up(edge_top)
    edge_above = down(edge_bottom)
    flux = exchanged(flux, "sy")

    named = {"flux": flux, "mid_top": mid_top, "mid_above": mid_above, "obs_above": obs_above,
             "mid_bottom": mid_bottom, "mid_below": mid_below, "obs": observed,
             "edge_top": edge_top, "edge_above": edge_above, "edge_bottom": edge_bottom, "edge_below": edge_below,
             "obs_diagonal": obs_diagonal, "obs_left": obs_left,
             "res_right": t["res_right"], "near_left": t["near_left"], "spec": spec, "more": more,
             "grad_left": t["grad_left"], "grad_right": t["grad_right"],
             "windows": t["windows"], "plain": t["windows"][0]}
    outs = [f32(S, width), f32(H, width), f32(H, width)]
    residual, g_top, g_bottom = call(
        functools.partial(gradient_kernel, tuple(named)),
        named,
        {},
        [(pltpu.HBM, o) for o in outs],
        like(named) + [pltpu.SemaphoreType.DMA((len(named) + len(outs),))]
        + [pltpu.VMEM(o.shape, F32) for o in outs]
        + [pltpu.VMEM((L, width + S), F32), pltpu.VMEM((6 * S, 2 * width + 2 * S), BF16),
           pltpu.VMEM((12 * L, 2 * width), BF16)],
        44,
        6 * 500 * 10**6,
    )
    bottom_other = mirrored(g_bottom, "fr", 1)
    top_other = ring(g_top, ("sy", "fr"), (-1, 1))
    top_same = up(g_top)
    total = jnp.concatenate([g_bottom + bottom_other, top_same + top_other], axis=0)
    side = ring(total[:, :H], ("sx",), (-1,))
    gradient = jnp.concatenate([total[:, H:], side], axis=1)
    return gradient, residual[None]


def solution(mesh):
    placed = (P("sy", "sx"), P("fr", "sy", "sx"), P("fr", "sy", "sx", None, None))
    return jax.shard_map(
        per_device,
        mesh=mesh,
        in_specs=placed,
        out_specs=(P("sy", "sx"), P("fr", "sy", "sx")),
        check_vma=False,
    )
```

time: 107 us -> 101 us (0.944)
  waiting for transfers between devices: 8.77 us -> 28.4 us
  blocking collectives: 24.5 us -> 11.2 us
  Pallas kernels: 29.3 us -> 24.3 us
  other arithmetic: 5.42 us -> 1.87 us
  local copies, waits for them, and re-layouts: 4.5 us -> 2.71 us
  between operations: 2.14 us -> 0.9 us
    all_to_all x2 -> x1, blocking collectives: 24.5 us -> 11.2 us  [exchanged(): return lax.all_to_all(value, axis, 0, 0)]
    ppermute x14 -> x16, waiting for transfers between devices: 8.76 us -> 19.9 us  [ring(): return lax.ppermute(value, axes, pairs)]
    all_to_all x0 -> x1, waiting for transfers between devices: none -> 6.89 us  [exchanged(): return lax.all_to_all(value, axis, 0, 0)]
    pallas_call x4 -> x5, Pallas kernels: 29.3 us -> 24.3 us  [the longest x3 20.6 us: call(): pl.pallas_call(kernel, out_shape=[place(o.shape, o.dtype) for place, o in...]
    ppermute x14 -> x16, starting transfers between devices: 26.6 us -> 22.9 us  [ring(): return lax.ppermute(value, axes, pairs)]
    all_to_all x0 -> x1, starting transfers between devices: none -> 3.49 us  [exchanged(): return lax.all_to_all(value, axis, 0, 0)]
    slice x3 -> x0, local copies, waits for them, and re-layouts: 2.27 us -> none  [the longest x1 0.91 us: per_device(): obj_above = down(object_field[H:])]
    concatenate x2 -> x0, other arithmetic: 1.91 us -> none  [the longest x1 0.96 us: per_device(): jnp.concatenate([first[:S] + from_left[:S], mid_top, last[:S] + from_righ...]
  transfers between devices with their start and end apart: 15 -> 18, of which waited for: 4 -> 7; matrix products, arithmetic and copies ran while one was open for 5% -> 1% of each run, Pallas kernels for 17% -> 15%
where the time goes in v3:
time: 101 us
  starting transfers between devices  31.8 us (31%)
  waiting for transfers between devices  28.4 us (28%)
  Pallas kernels  24.3 us (24%)
  blocking collectives  11.2 us (11%)
  local copies, waits for them, and re-layouts  2.71 us (3%)
  other arithmetic  1.87 us (2%)
    ppermute x16, starting transfers between devices, ring(): return lax.ppermute(value, axes, pairs)  22.9 us
    pallas_call x3, Pallas kernels, call(): pl.pallas_call(kernel, out_shape=[place(o.shape, o.dtype) for place, o in...  20.6 us
    ppermute x16, waiting for transfers between devices, ring(): return lax.ppermute(value, axes, pairs)  19.9 us
    all_to_all x1, blocking collectives, exchanged(): return lax.all_to_all(value, axis, 0, 0)  11.2 us
    all_to_all x1, waiting for transfers between devices, exchanged(): return lax.all_to_all(value, axis, 0, 0)  6.89 us
    ppermute x1, starting transfers between devices, mirrored(): return lax.ppermute(value, axis, [(s, s ^ bits) for s in range(count)])  5.41 us
    all_to_all x1, starting transfers between devices, exchanged(): return lax.all_to_all(value, axis, 0, 0)  3.49 us
    unnamed x34, local copies, waits for them, and re-layouts  2.71 us
  transfers between devices with their start and end apart: 18, of which 7 were waited for; matrix products, arithmetic and copies ran while one was open for 1% of the time, Pallas kernels for 15%

profile of v3, /device:TPU:1, one launch (start us, length us, event | category | flops | bytes accessed | tf_op | source)
XLA Modules:
  0.0 101.2 jit_solution(5293316115457354757)
XLA Ops:
  0.6 2.5 %collective-permute-start.3 = (f32[4,128,128]{2,1,0:T(8,128)}, f32[4,128,128]{2,1,0:T(8,128)S(1)}, u32[]{:S(2)}, u32[]{:S(2)}) collective-permute-start(f32[4,128,128]{2,1,0:T(8,128)} %bitcast.3), channel_id=1, source_target_pairs={{0,16},{16,32},{32,48},{48,64},{64,80},{80,96},{96,112},{112,128},... | collective-permute-start | bytes 786440 | tf_op jit(solution)/shard_map/ppermute | solution.py:406
  3.2 1.9 %shard_map.131 = (f32[64,512]{1,0:T(8,128)}, f32[192,128]{1,0:T(8,128)}, f32[192,128]{1,0:T(8,128)}, f32[128,128]{1,0:T(8,128)}) custom-call(f32[128,512]{1,0:T(8,128)} %refs_3_.2, f32[128,512]{1,0:T(8,128)} %bitcast.6, f32[4,128,128]{2,1,0:T(8,128)} %bitcast.4), custom_call_target="tpu_custom_call" | custom-call | tf_op jit(solution)/shard_map/pallas_call | solution.py:433
  5.1 1.6 %collective-permute-start.2 = (f32[64,512]{1,0:T(8,128)}, f32[64,512]{1,0:T(8,128)S(1)}, u32[]{:S(2)}, u32[]{:S(2)}) collective-permute-start(f32[64,512]{1,0:T(8,128)} %get-tuple-element.37), channel_id=1, source_target_pairs={{0,16},{16,32},{32,48},{48,64},{64,80},{80,96},{96,112},{112,128},... | collective-permute-start | bytes 393224 | tf_op jit(solution)/shard_map/ppermute | solution.py:406
  6.7 2.3 %collective-permute-start = (f32[192,128]{1,0:T(8,128)}, f32[192,128]{1,0:T(8,128)S(1)}, u32[]{:S(2)}, u32[]{:S(2)}) collective-permute-start(f32[192,128]{1,0:T(8,128)} %get-tuple-element.35), channel_id=1, source_target_pairs={{0,2},{2,4},{4,6},{6,8},{8,10},{10,12},{12,14},{14,0},{1,3},{3,5},... | collective-permute-start | bytes 294920 | tf_op jit(solution)/shard_map/ppermute | solution.py:406
  9.0 1.4 %collective-permute-start.1 = (f32[192,128]{1,0:T(8,128)}, f32[192,128]{1,0:T(8,128)S(1)}, u32[]{:S(2)}, u32[]{:S(2)}) collective-permute-start(f32[192,128]{1,0:T(8,128)} %get-tuple-element.36), channel_id=1, source_target_pairs={{0,18},{2,20},{4,22},{6,24},{8,26},{10,28},{12,30},{14,16},{16,34}... | collective-permute-start | bytes 294920 | tf_op jit(solution)/shard_map/ppermute | solution.py:406
  10.4 1.8 %collective-permute-start.5 = (f32[128,128]{1,0:T(8,128)}, f32[128,128]{1,0:T(8,128)S(1)}, u32[]{:S(2)}, u32[]{:S(2)}) collective-permute-start(f32[128,128]{1,0:T(8,128)} %get-tuple-element.51), channel_id=1, source_target_pairs={{0,2},{2,4},{4,6},{6,8},{8,10},{10,12},{12,14},{14,0},{1,3},{3,5},... | collective-permute-start | bytes 196616 | tf_op jit(solution)/shard_map/ppermute | solution.py:406
  12.2 3.0 %shard_map.132 = (f32[512,512]{1,0:T(8,128)}, f32[512,512]{1,0:T(8,128)S(1)}, f32[8,128]{1,0:T(8,128)S(1)}, bf16[384,256]{1,0:T(8,128)(2,1)S(1)}, bf16[512,768]{...) custom-call(f32[4,128,128]{2,1,0:T(8,128)} %bitcast.5, ...), custom_call_target="tpu_custom_call" | custom-call | flops 504000000 | bytes 5849088 | tf_op jit(solution)/shard_map/pallas_call | solution.py:382
  15.3 5.1 %collective-permute-done.1.refs_1_ = f32[192,128]{1,0:T(8,128)S(1)} collective-permute-done((f32[192,128]{1,0:T(8,128)}, f32[192,128]{1,0:T(8,128)S(1)}, u32[]{:S(2)}, u32[]{:S(2)}) %collective-permute-start.1) | collective-permute-done | bytes 98336 | tf_op jit(solution)/shard_map/ppermute | solution.py:406
  20.5 0.6 copy-done.13
  21.2 8.0 %shard_map.133 = (f32[512,768]{1,0:T(8,128)}, f32[128,384]{1,0:T(8,128)}, f32[128,384]{1,0:T(8,128)}, f32[256,128]{1,0:T(8,128)}, f32[256,128]{1,0:T(8,128)}, /*index=5*/f32[8,8,128]{2,1,0:T(8,128)S(1)}) custom-call(f32[192,128]{1,0:T(8,128)} %copy-done.12, f32[192,128]{1,0:T(8,128)} %copy-done.13, f32[64,512]{1,0:T(8,128)} %copy-done.9, ...), custom_call_target="tpu_custom_call" | custom-call | flops 3600000000 | bytes 851968 | tf_op jit(solution)/shard_map/pallas_call | solution.py:382
  29.3 1.2 %collective-permute-done.4.refs_3_ = f32[128,512]{1,0:T(8,128)S(1)} collective-permute-done((f32[128,512]{1,0:T(8,128)S(1)}, f32[128,512]{1,0:T(8,128)S(1)}, u32[]{:S(2)}, u32[]{:S(2)}) %collective-permute-start.4) | collective-permute-done | bytes 262176 | tf_op jit(solution)/shard_map/ppermute | solution.py:406
  30.4 3.3 %collective-permute-start.7 = (f32[256,128]{1,0:T(8,128)}, f32[256,128]{1,0:T(8,128)S(1)}, u32[]{:S(2)}, u32[]{:S(2)}) collective-permute-start(f32[256,128]{1,0:T(8,128)} %get-tuple-element.53.last), channel_id=1, source_target_pairs={{0,2},{2,4},{4,6},{6,8},{8,10},{10,12},{12,14},{14,0},{1,3},{3,5},... | collective-permute-start | bytes 393224 | tf_op jit(solution)/shard_map/ppermute | solution.py:406
  33.7 2.9 %collective-permute-start.10 = (f32[128,384]{1,0:T(8,128)}, f32[128,384]{1,0:T(8,128)S(1)}, u32[]{:S(2)}, u32[]{:S(2)}) collective-permute-start(f32[128,384]{1,0:T(8,128)} %get-tuple-element.56.refs_1_), channel_id=1, source_target_pairs={{0,240},{16,0},{32,16},{48,32},{64,48},{80,64},{96,80},{112,96},{1... | collective-permute-start | bytes 589832 | tf_op jit(solution)/shard_map/ppermute | solution.py:406
  36.6 11.2 %all_to_all.10.flux_ref = f32[8,8,128]{2,1,0:T(8,128)} all-to-all(f32[8,8,128]{2,1,0:T(8,128)S(1)} %get-tuple-element.54), channel_id=1, replica_groups=mesh['sy'=16,'sx'=8,'fr'=2] {'sx'}, dimensions={0} | all-to-all | bytes 65536 | tf_op jit(solution)/shard_map/all_to_all | solution.py:415
  47.8 0.6 copy-done.2
  48.5 0.6 copy-done.3
  49.1 1.8 %shard_map.134 = (f32[128,256]{1,0:T(8,128)}, f32[128,256]{1,0:T(8,128)}, f32[16,8,128]{2,1,0:T(8,128)}) custom-call(f32[256,128]{1,0:T(8,128)} %get-tuple-element.52.first, f32[256,128]{1,0:T(8,128)} %get-tuple-element.53.last, f32[256,128]{1,0:T(8,128)} %copy-done.2, f32[256,128]{1,0:T(8,128)} %copy-done.3, f32[8,8,128]{2,1,0:T(8,128)} %all_to_all.10.flux_ref), custom_call_target="tpu_custom_call" | custom-call | tf_op jit(solution)/shard_map/pallas_call | solution.py:481
  50.9 5.5 %collective-permute-start.12 = (f32[128,256]{1,0:T(8,128)}, f32[128,256]{1,0:T(8,128)S(1)}, u32[]{:S(2)}, u32[]{:S(2)}) collective-permute-start(f32[128,256]{1,0:T(8,128)} %get-tuple-element.59.refs_7_), channel_id=1, source_target_pairs={{0,240},{16,0},{32,16},{48,32},{64,48},{80,64},{96,80},{112,96},{1... | collective-permute-start | bytes 393224 | tf_op jit(solution)/shard_map/ppermute | solution.py:406
  56.4 3.5 %all-to-all-start.1 = ((f32[16,8,128]{2,1,0:T(8,128)}), f32[16,8,128]{2,1,0:T(8,128)S(1)}, u32[]{:S(2)}, u32[]{:S(2)}) async-start(f32[16,8,128]{2,1,0:T(8,128)} %get-tuple-element.55), calls=%async_computation.1 | async-start | bytes 131072 | tf_op jit(solution)/shard_map/all_to_all | solution.py:415
  59.9 6.9 %all-to-all-done.1.refs_0_ = f32[16,8,128]{2,1,0:T(8,128)S(1)} async-done(((f32[16,8,128]{2,1,0:T(8,128)}), f32[16,8,128]{2,1,0:T(8,128)S(1)}, u32[]{:S(2)}, u32[]{:S(2)}) %all-to-all-start.1) | async-done | bytes 65568 | tf_op jit(solution)/shard_map/all_to_all | solution.py:415
  66.9 0.6 copy-done.4
  67.5 9.5 %shard_map.135 = (f32[128,512]{1,0:T(8,128)}, f32[64,512]{1,0:T(8,128)}, f32[64,512]{1,0:T(8,128)}) custom-call(f32[16,8,128]{2,1,0:T(8,128)} %copy-done.4, f32[128,384]{1,0:T(8,128)} %get-tuple-element.56.refs_1_, f32[128,384]{1,0:T(8,128)} %copy-done.8, f32[128,512]{1,0:T(8,128)} %copy-done.5, f32[128,384]{1,0:T(8,128)} %get-tuple-element.57.refs_4_, ...), custom_call_target="tpu_custom_call" | custom-call | flops 3000000000 | bytes 9199616 | tf_op jit(solution)/shard_map/pallas_call | solution.py:382
  77.1 5.4 %collective-permute-start.13 = (f32[64,512]{1,0:T(8,128)}, f32[64,512]{1,0:T(8,128)S(1)}, u32[]{:S(2)}, u32[]{:S(2)}) collective-permute-start(f32[64,512]{1,0:T(8,128)} %get-tuple-element.65), channel_id=1, source_target_pairs={{0,1},{1,0},{2,3},{3,2},{4,5},{5,4},{6,7},{7,6},{8,9},{9,8},{10,11... | collective-permute-start | bytes 393224 | tf_op jit(solution)/shard_map/ppermute | solution.py:411
  82.5 1.0 %collective-permute-start.14 = (f32[64,512]{1,0:T(8,128)}, f32[64,512]{1,0:T(8,128)S(1)}, u32[]{:S(2)}, u32[]{:S(2)}) collective-permute-start(f32[64,512]{1,0:T(8,128)} %get-tuple-element.66), channel_id=1, source_target_pairs={{0,240},{16,0},{32,16},{48,32},{64,48},{80,64},{96,80},{112,96},{1... | collective-permute-start | bytes 393224 | tf_op jit(solution)/shard_map/ppermute | solution.py:406
  83.5 1.6 %collective-permute-done.13 = f32[64,512]{1,0:T(8,128)S(1)} collective-permute-done((f32[64,512]{1,0:T(8,128)}, f32[64,512]{1,0:T(8,128)S(1)}, u32[]{:S(2)}, u32[]{:S(2)}) %collective-permute-start.13) | collective-permute-done | bytes 131104 | tf_op jit(solution)/shard_map/ppermute | solution.py:411
  85.2 0.9 add.6
  86.1 5.4 %collective-permute-done.14 = f32[64,512]{1,0:T(8,128)S(1)} collective-permute-done((f32[64,512]{1,0:T(8,128)}, f32[64,512]{1,0:T(8,128)S(1)}, u32[]{:S(2)}, u32[]{:S(2)}) %collective-permute-start.14) | collective-permute-done | bytes 131104 | tf_op jit(solution)/shard_map/ppermute | solution.py:406
  91.5 5.2 %collective-permute-done.15 = f32[64,512]{1,0:T(8,128)S(1)} collective-permute-done((f32[64,512]{1,0:T(8,128)}, f32[64,512]{1,0:T(8,128)S(1)}, u32[]{:S(2)}, u32[]{:S(2)}) %collective-permute-start.15) | collective-permute-done | bytes 131104 | tf_op jit(solution)/shard_map/ppermute | solution.py:406
  96.7 0.5 collective-permute-start.16
  97.2 0.1 slice_maximum_fusion
  97.3 3.1 %collective-permute-done.16 = f32[128,64]{1,0:T(8,128)S(1)} collective-permute-done((f32[128,64]{1,0:T(8,128)S(1)}, f32[128,64]{1,0:T(8,128)S(1)}, u32[]{:S(2)}, u32[]{:S(2)}) %collective-permute-start.16) | collective-permute-done | bytes 32800 | tf_op jit(solution)/shard_map/ppermute | solution.py:406
  100.4 0.8 pad_maximum_fusion
  (49 shorter events, 0.4 us)
Async XLA Ops:
  0.6 19.8 %collective-permute-start.3 = (f32[4,128,128]{2,1,0:T(8,128)}, f32[4,128,128]{2,1,0:T(8,128)S(1)}, u32[]{:S(2)}, u32[]{:S(2)}) collective-permute-start(f32[4,128,128]{2,1,0:T(8,128)} %bitcast.3), channel_id=1, source_target_pairs={{0,16},{16,32},{32,48},{48,64},{64,80},{80,96},{96,112},{112,128},... | collective-permute-start | bytes 786440 | tf_op jit(solution)/shard_map/ppermute | solution.py:406
  3.2 17.2 %copy-start.1 = (f32[1,128,512]{2,1,0:T(8,128)S(1)}, f32[1,128,512]{2,1,0:T(8,128)}, u32[]{:S(2)}) copy-start(f32[1,128,512]{2,1,0:T(8,128)} %param.13) | copy-start | bytes 786436
  3.2 18.0 %copy-start = (f32[2,8,128]{2,1,0:T(8,128)S(1)}, f32[2,8,128]{2,1,0:T(8,128)}, u32[]{:S(2)}) copy-start(f32[2,8,128]{2,1,0:T(8,128)} %constant.30.refs_13_.refs_20_) | copy-start | bytes 24580
  5.1 10.1 %copy-start.16 = (f32[128,128]{1,0:T(8,128)S(1)}, f32[128,128]{1,0:T(8,128)}, u32[]{:S(2)}) copy-start(f32[128,128]{1,0:T(8,128)} %get-tuple-element.51) | copy-start | bytes 196612
  5.1 15.3 %collective-permute-start.2 = (f32[64,512]{1,0:T(8,128)}, f32[64,512]{1,0:T(8,128)S(1)}, u32[]{:S(2)}, u32[]{:S(2)}) collective-permute-start(f32[64,512]{1,0:T(8,128)} %get-tuple-element.37), channel_id=1, source_target_pairs={{0,16},{16,32},{32,48},{48,64},{64,80},{80,96},{96,112},{112,128},... | collective-permute-start | bytes 393224 | tf_op jit(solution)/shard_map/ppermute | solution.py:406
  6.7 8.5 %collective-permute-start = (f32[192,128]{1,0:T(8,128)}, f32[192,128]{1,0:T(8,128)S(1)}, u32[]{:S(2)}, u32[]{:S(2)}) collective-permute-start(f32[192,128]{1,0:T(8,128)} %get-tuple-element.35), channel_id=1, source_target_pairs={{0,2},{2,4},{4,6},{6,8},{8,10},{10,12},{12,14},{14,0},{1,3},{3,5},... | collective-permute-start | bytes 294920 | tf_op jit(solution)/shard_map/ppermute | solution.py:406
  9.0 11.4 %collective-permute-start.1 = (f32[192,128]{1,0:T(8,128)}, f32[192,128]{1,0:T(8,128)S(1)}, u32[]{:S(2)}, u32[]{:S(2)}) collective-permute-start(f32[192,128]{1,0:T(8,128)} %get-tuple-element.36), channel_id=1, source_target_pairs={{0,18},{2,20},{4,22},{6,24},{8,26},{10,28},{12,30},{14,16},{16,34}... | collective-permute-start | bytes 294920 | tf_op jit(solution)/shard_map/ppermute | solution.py:406
  10.4 18.8 %collective-permute-start.5 = (f32[128,128]{1,0:T(8,128)}, f32[128,128]{1,0:T(8,128)S(1)}, u32[]{:S(2)}, u32[]{:S(2)}) collective-permute-start(f32[128,128]{1,0:T(8,128)} %get-tuple-element.51), channel_id=1, source_target_pairs={{0,2},{2,4},{4,6},{6,8},{8,10},{10,12},{12,14},{14,0},{1,3},{3,5},... | collective-permute-start | bytes 196616 | tf_op jit(solution)/shard_map/ppermute | solution.py:406
  15.2 5.3 %copy-start.12 = (f32[192,128]{1,0:T(8,128)}, f32[192,128]{1,0:T(8,128)S(1)}, u32[]{:S(2)}) copy-start(f32[192,128]{1,0:T(8,128)S(1)} %collective-permute-done.refs_0_) | copy-start | bytes 294916
  15.2 14.0 %collective-permute-start.6 = (f32[128,128]{1,0:T(8,128)S(1)}, f32[128,128]{1,0:T(8,128)S(1)}, u32[]{:S(2)}, u32[]{:S(2)}) collective-permute-start(f32[128,128]{1,0:T(8,128)S(1)} %copy-done.16), channel_id=1, source_target_pairs={{0,18},{2,20},{4,22},{6,24},{8,26},{10,28},{12,30},{14,16},{16,34}... | collective-permute-start | bytes 196616 | tf_op jit(solution)/shard_map/ppermute | solution.py:406
  20.4 10.0 %collective-permute-start.4 = (f32[128,512]{1,0:T(8,128)S(1)}, f32[128,512]{1,0:T(8,128)S(1)}, u32[]{:S(2)}, u32[]{:S(2)}) collective-permute-start(f32[128,512]{1,0:T(8,128)S(1)} %bitcast.9), channel_id=1, source_target_pairs={{0,16},{16,32},{32,48},{48,64},{64,80},{80,96},{96,112},{112,128},... | collective-permute-start | bytes 786440 | tf_op jit(solution)/shard_map/ppermute | solution.py:406
  20.4 0.7 copy-start.9
  20.4 0.7 copy-start.6
  29.2 37.6 %copy-start.14 = (f32[128,128]{1,0:T(8,128)}, f32[128,128]{1,0:T(8,128)S(1)}, u32[]{:S(2)}) copy-start(f32[128,128]{1,0:T(8,128)S(1)} %collective-permute-done.5.refs_12_) | copy-start | bytes 196612
  29.3 37.6 %copy-start.15 = (f32[128,128]{1,0:T(8,128)}, f32[128,128]{1,0:T(8,128)S(1)}, u32[]{:S(2)}) copy-start(f32[128,128]{1,0:T(8,128)S(1)} %collective-permute-done.6.refs_11_) | copy-start | bytes 196612
  30.4 36.4 %copy-start.5 = (f32[128,512]{1,0:T(8,128)}, f32[128,512]{1,0:T(8,128)S(1)}, u32[]{:S(2)}) copy-start(f32[128,512]{1,0:T(8,128)S(1)} %collective-permute-done.4.refs_3_) | copy-start | bytes 786436
  30.4 17.4 %collective-permute-start.7 = (f32[256,128]{1,0:T(8,128)}, f32[256,128]{1,0:T(8,128)S(1)}, u32[]{:S(2)}, u32[]{:S(2)}) collective-permute-start(f32[256,128]{1,0:T(8,128)} %get-tuple-element.53.last), channel_id=1, source_target_pairs={{0,2},{2,4},{4,6},{6,8},{8,10},{10,12},{12,14},{14,0},{1,3},{3,5},... | collective-permute-start | bytes 393224 | tf_op jit(solution)/shard_map/ppermute | solution.py:406
  33.7 14.1 %collective-permute-start.8 = (f32[256,128]{1,0:T(8,128)}, f32[256,128]{1,0:T(8,128)S(1)}, u32[]{:S(2)}, u32[]{:S(2)}) collective-permute-start(f32[256,128]{1,0:T(8,128)} %get-tuple-element.52.first), channel_id=1, source_target_pairs={{0,14},{2,0},{4,2},{6,4},{8,6},{10,8},{12,10},{14,12},{1,15},{3,1}... | collective-permute-start | bytes 393224 | tf_op jit(solution)/shard_map/ppermute | solution.py:406
  33.7 26.2 %collective-permute-start.10 = (f32[128,384]{1,0:T(8,128)}, f32[128,384]{1,0:T(8,128)S(1)}, u32[]{:S(2)}, u32[]{:S(2)}) collective-permute-start(f32[128,384]{1,0:T(8,128)} %get-tuple-element.56.refs_1_), channel_id=1, source_target_pairs={{0,240},{16,0},{32,16},{48,32},{64,48},{80,64},{96,80},{112,96},{1... | collective-permute-start | bytes 589832 | tf_op jit(solution)/shard_map/ppermute | solution.py:406
  36.6 23.3 %collective-permute-start.9 = (f32[128,384]{1,0:T(8,128)}, f32[128,384]{1,0:T(8,128)S(1)}, u32[]{:S(2)}, u32[]{:S(2)}) collective-permute-start(f32[128,384]{1,0:T(8,128)} %get-tuple-element.57.refs_4_), channel_id=1, source_target_pairs={{0,16},{16,32},{32,48},{48,64},{64,80},{80,96},{96,112},{112,128},... | collective-permute-start | bytes 589832 | tf_op jit(solution)/shard_map/ppermute | solution.py:406
  47.8 0.7 copy-start.2
  50.9 15.9 %collective-permute-start.11 = (f32[128,256]{1,0:T(8,128)}, f32[128,256]{1,0:T(8,128)S(1)}, u32[]{:S(2)}, u32[]{:S(2)}) collective-permute-start(f32[128,256]{1,0:T(8,128)} %get-tuple-element.60.refs_9_), channel_id=1, source_target_pairs={{0,16},{16,32},{32,48},{48,64},{64,80},{80,96},{96,112},{112,128},... | collective-permute-start | bytes 393224 | tf_op jit(solution)/shard_map/ppermute | solution.py:406
  50.9 15.9 %collective-permute-start.12 = (f32[128,256]{1,0:T(8,128)}, f32[128,256]{1,0:T(8,128)S(1)}, u32[]{:S(2)}, u32[]{:S(2)}) collective-permute-start(f32[128,256]{1,0:T(8,128)} %get-tuple-element.59.refs_7_), channel_id=1, source_target_pairs={{0,240},{16,0},{32,16},{48,32},{64,48},{80,64},{96,80},{112,96},{1... | collective-permute-start | bytes 393224 | tf_op jit(solution)/shard_map/ppermute | solution.py:406
  56.4 10.4 %all-to-all-start.1 = ((f32[16,8,128]{2,1,0:T(8,128)}), f32[16,8,128]{2,1,0:T(8,128)S(1)}, u32[]{:S(2)}, u32[]{:S(2)}) async-start(f32[16,8,128]{2,1,0:T(8,128)} %get-tuple-element.55), calls=%async_computation.1 | async-start | bytes 131072 | tf_op jit(solution)/shard_map/all_to_all | solution.py:415
  59.9 7.0 %copy-start.7 = (f32[128,384]{1,0:T(8,128)}, f32[128,384]{1,0:T(8,128)S(1)}, u32[]{:S(2)}) copy-start(f32[128,384]{1,0:T(8,128)S(1)} %collective-permute-done.10.refs_5_) | copy-start | bytes 589828
  59.9 7.0 %copy-start.8 = (f32[128,384]{1,0:T(8,128)}, f32[128,384]{1,0:T(8,128)S(1)}, u32[]{:S(2)}) copy-start(f32[128,384]{1,0:T(8,128)S(1)} %collective-permute-done.9.refs_2_) | copy-start | bytes 589828
  66.8 0.7 copy-start.10
  66.8 0.7 copy-start.11
  77.1 8.1 %collective-permute-start.13 = (f32[64,512]{1,0:T(8,128)}, f32[64,512]{1,0:T(8,128)S(1)}, u32[]{:S(2)}, u32[]{:S(2)}) collective-permute-start(f32[64,512]{1,0:T(8,128)} %get-tuple-element.65), channel_id=1, source_target_pairs={{0,1},{1,0},{2,3},{3,2},{4,5},{5,4},{6,7},{7,6},{8,9},{9,8},{10,11... | collective-permute-start | bytes 393224 | tf_op jit(solution)/shard_map/ppermute | solution.py:411
  82.5 9.0 %collective-permute-start.14 = (f32[64,512]{1,0:T(8,128)}, f32[64,512]{1,0:T(8,128)S(1)}, u32[]{:S(2)}, u32[]{:S(2)}) collective-permute-start(f32[64,512]{1,0:T(8,128)} %get-tuple-element.66), channel_id=1, source_target_pairs={{0,240},{16,0},{32,16},{48,32},{64,48},{80,64},{96,80},{112,96},{1... | collective-permute-start | bytes 393224 | tf_op jit(solution)/shard_map/ppermute | solution.py:406
  83.5 13.1 %collective-permute-start.15 = (f32[64,512]{1,0:T(8,128)}, f32[64,512]{1,0:T(8,128)S(1)}, u32[]{:S(2)}, u32[]{:S(2)}) collective-permute-start(f32[64,512]{1,0:T(8,128)} %get-tuple-element.66), channel_id=1, source_target_pairs={{0,241},{1,240},{16,1},{17,0},{32,17},{33,16},{48,33},{49,32},{64,... | collective-permute-start | bytes 393224 | tf_op jit(solution)/shard_map/ppermute | solution.py:406
  96.7 3.7 %collective-permute-start.16 = (f32[128,64]{1,0:T(8,128)S(1)}, f32[128,64]{1,0:T(8,128)S(1)}, u32[]{:S(2)}, u32[]{:S(2)}) collective-permute-start(f32[128,64]{1,0:T(8,128)S(1)} %pad_maximum_fusion.1), channel_id=1, source_target_pairs={{0,14},{2,0},{4,2},{6,4},{8,6},{10,8},{12,10},{14,12},{1,15},{3,1}... | collective-permute-start | bytes 98312 | tf_op jit(solution)/shard_map/ppermute | solution.py:406
  (3 other events, 1.9 us)

commit v4 on v3

--- a/solution.py
+++ b/solution.py
@@ -273,22 +273,36 @@
         flux = flux + jnp.sum(together)
     for copy in outs[1:]:
         copy.start()
-    row = lax.broadcasted_iota(jnp.int32, flux_ref.shape, 1)
-    flux_ref[...] = jnp.where(row < 4, flux, t["total"][...][None])
+    lane = lax.broadcasted_iota(jnp.int32, flux_ref.shape, 1)
+    flux_ref[...] = jnp.where(lane < H, flux, t["total"][...])
     for copy in outs:
         copy.wait()
 
 
-def edge_kernel(first, last, from_left, from_right, flux_ref, top_ref, bottom_ref, totals_ref):
-    for half, out in ((0, top_ref), (1, bottom_ref)):
-        out[:, :S] = first[at(half)] + from_left[at(half)]
-        out[:, S:] = last[at(half)] + from_right[at(half)]
-    totals_ref[...] = jnp.broadcast_to(jnp.sum(flux_ref[...], axis=0)[None], totals_ref.shape)
+def join_kernel(names, parts, *refs):
+    total = len(names)
+    hbm, fluxes, refs = refs[:total], refs[total : total + parts], refs[total + parts :]
+    top_hbm, bottom_hbm, totals_ref = refs[:3]
+    buffers, sems, top_ref, bottom_ref = refs[3 : 3 + total], refs[3 + total], refs[4 + total], refs[5 + total]
+    t = Copies(names, hbm, buffers, sems)
+    outs = []
+    for half, out, place in ((0, top_ref, top_hbm), (1, bottom_ref, bottom_hbm)):
+        mid = t["mid_bottom" if half else "mid_top"]
+        width = mid.shape[1]
+        out[:, S : S + width] = mid[...]
+        out[:, :S] = t["first"][at(half)] + t["from_left"][at(half)]
+        out[:, S + width :] = t["last"][at(half)] + t["from_right"][at(half)]
+        outs.append(pltpu.make_async_copy(out, place, sems.at[total + half]))
+        outs[-1].start()
+    flux = sum([f[...] for f in fluxes[1:]], fluxes[0][...])
+    totals_ref[...] = jnp.broadcast_to(flux[None], totals_ref.shape)
+    for copy in outs:
+        copy.wait()
 
 
 def gradient_kernel(names, *refs):
     total = len(names)
-    hbm, refs = refs[:total], refs[total:]
+    hbm, flux_ref, refs = refs[:total], refs[total], refs[total + 1 :]
     residual_hbm, top_hbm, bottom_hbm = refs[:3]
     buffers, sems, (residual_ref, out_top, out_bottom) = refs[3 : 3 + total], refs[3 + total], refs[4 + total : 7 + total]
     r_ref, r_parts, g_parts = refs[7 + total :]
@@ -303,15 +317,14 @@
     alpha, beta = 1.0 - row_edge.astype(F32), 1.0 - column_edge.astype(F32)
     width = residual_ref.shape[1]
     count = width // S
-    sums = jnp.sum(t["flux"][...], axis=0)
-    gain = sums[4, 0] / sums[0, 0]
-    r_ref[:S, S:width] = gain * (t["mid_top"][...] + t["mid_above"][...]) - t["obs_above"][:, : width - S]
-    r_ref[S:, S:width] = gain * (t["mid_bottom"][...] + t["mid_below"][...]) - t["obs"][:, : width - S]
-    top, bottom, above, below = (t[n] for n in ("edge_top", "edge_bottom", "edge_above", "edge_below"))
-    r_ref[:S, :S] = gain * (top[:, :S] + above[:, :S]) - t["obs_diagonal"][...]
-    r_ref[S:, :S] = gain * (bottom[:, :S] + below[:, :S]) - t["obs_left"][...]
-    r_ref[:S, width:] = gain * (top[:, S:] + above[:, S:]) - t["obs_above"][:, width - S :]
-    r_ref[S:, width:] = gain * (bottom[:, S:] + below[:, S:]) - t["obs"][:, width - S :]
+    sums = jnp.sum(flux_ref[...], axis=0)
+    gain = sums[0, H] / sums[0, 0]
+    r_ref[:S] = gain * (t["top"][...] + t["above"][...])
+    r_ref[S:] = gain * (t["bottom"][...] + t["below"][...])
+    r_ref[:S, S:] -= t["obs_above"][...]
+    r_ref[S:, S:] -= t["obs"][...]
+    r_ref[:S, :S] -= t["obs_diagonal"][...]
+    r_ref[S:, :S] -= t["obs_left"][...]
     residual_ref[...] = r_ref[S:, S:]
     sent[0].start()
     near, far = r_ref[:, :S], r_ref[:, S : 2 * S]
@@ -375,9 +388,9 @@
     return jax.ShapeDtypeStruct(shape, F32)
 
 
-def call(kernel, named, ready, outs, scratch, limit, flops):
+def call(kernel, named, ready, outs, scratch, limit, flops, loose=()):
     hbm, vmem = pl.BlockSpec(memory_space=pltpu.HBM), pl.BlockSpec(memory_space=pltpu.VMEM)
-    held = [pltpu.with_memory_space_constraint(x, pltpu.HBM) for x in named.values()]
+    held = [x if n in loose else pltpu.with_memory_space_constraint(x, pltpu.HBM) for n, x in named.items()]
     size = sum(math.prod(x.shape) * x.dtype.itemsize for x in named.values())
     return pl.pallas_call(
         kernel,
@@ -411,8 +424,16 @@
     return lax.ppermute(value, axis, [(s, s ^ bits) for s in range(count)])
 
 
-def exchanged(value, axis):
-    return lax.all_to_all(value, axis, 0, 0)
+def runs():
+    count = lax.axis_size("sy")
+    return 4 if count % 4 == 0 else count
+
+
+def exchanged(value):
+    count_y, count_x, run = lax.axis_size("sy"), lax.axis_size("sx"), runs()
+    index = np.arange(count_y * count_x).reshape(count_y // run, run, count_x)
+    groups = index.transpose(1, 0, 2).reshape(run, -1).tolist()
+    return lax.all_to_all(value, ("sy", "sx"), 0, 0, axis_index_groups=groups)
 
 
 def down(value):
@@ -462,32 +483,41 @@
         functools.partial(model_kernel, tuple(named), tuple(ready)),
         named,
         ready,
-        [(pltpu.HBM, o) for o in outs] + [(pltpu.VMEM, f32(lax.axis_size("sx"), 8, S))],
+        [(pltpu.HBM, o) for o in outs] + [(pltpu.VMEM, f32(8, S))],
         like(named) + [pltpu.SemaphoreType.DMA((len(named) + len(outs),))]
         + [pltpu.VMEM(o.shape, F32) for o in outs]
         + [pltpu.VMEM((2 * width, S), F32), pltpu.VMEM((6 * S, 3 * width + 2 * S), BF16),
            pltpu.VMEM((6 * L, 2 * width + 2 * S), BF16)],
         36,
         6 * 600 * 10**6,
+        ("right", "diagonal", "above", "psf_above"),
     )
     mid_top, mid_bottom, first, last, flux, obs_above, obs_left, obs_diagonal = lax.optimization_barrier(
         (mid_top, mid_bottom, first, last, flux, obs_above, obs_left, obs_diagonal)
     )
-    mid_below = up(mid_top)
-    mid_above = down(mid_bottom)
     from_right = ring(first, ("sx",), (-1,))
     from_left = ring(last, ("sx",), (1,))
-    flux = exchanged(flux, "sx")
-    edge_top, edge_bottom, flux = pl.pallas_call(
-        edge_kernel, out_shape=(f32(S, L), f32(S, L), f32(lax.axis_size("sy"), 8, S))
-    )(first, last, from_left, from_right, flux)
-    edge_below = up(edge_top)
-    edge_above = down(edge_bottom)
-    flux = exchanged(flux, "sy")
-
-    named = {"flux": flux, "mid_top": mid_top, "mid_above": mid_above, "obs_above": obs_above,
-             "mid_bottom": mid_bottom, "mid_below": mid_below, "obs": observed,
-             "edge_top": edge_top, "edge_above": edge_above, "edge_bottom": edge_bottom, "edge_below": edge_below,
+    fluxes = [flux] + [mirrored(flux, "sy", k) for k in range(1, runs())]
+    named = {"mid_top": mid_top, "mid_bottom": mid_bottom, "first": first, "from_left": from_left,
+             "last": last, "from_right": from_right}
+    outs = [f32(S, width + S)] * 2
+    top, bottom, flux = call(
+        functools.partial(join_kernel, tuple(named), len(fluxes)),
+        named,
+        dict(enumerate(fluxes)),
+        [(pltpu.HBM, o) for o in outs]
+        + [(pltpu.VMEM, f32(lax.axis_size("sy") // runs() * lax.axis_size("sx"), 8, S))],
+        like(named) + [pltpu.SemaphoreType.DMA((len(named) + len(outs),))] + [pltpu.VMEM(o.shape, F32) for o in outs],
+        16,
+        10**6,
+        ("from_left", "from_right"),
+    )
+    below = up(top)
+    above = down(bottom)
+    flux = exchanged(flux)
+
+    named = {"top": top, "above": above, "bottom": bottom, "below": below,
+             "obs_above": obs_above, "obs": observed,
              "obs_diagonal": obs_diagonal, "obs_left": obs_left,
              "res_right": t["res_right"], "near_left": t["near_left"], "spec": spec, "more": more,
              "grad_left": t["grad_left"], "grad_right": t["grad_right"],
@@ -496,7 +526,7 @@
     residual, g_top, g_bottom = call(
         functools.partial(gradient_kernel, tuple(named)),
         named,
-        {},
+        {"flux": flux},
         [(pltpu.HBM, o) for o in outs],
         like(named) + [pltpu.SemaphoreType.DMA((len(named) + len(outs),))]
         + [pltpu.VMEM(o.shape, F32) for o in outs]
@@ -504,6 +534,7 @@
            pltpu.VMEM((12 * L, 2 * width), BF16)],
         44,
         6 * 500 * 10**6,
+        ("above", "below", "obs_above", "obs_diagonal", "obs_left"),
     )
     bottom_other = mirrored(g_bottom, "fr", 1)
     top_other = ring(g_top, ("sy", "fr"), (-1, 1))

time: 101 us -> 95.6 us (0.947)
  waiting for transfers between devices: 28.4 us -> 18.5 us
  starting transfers between devices: 31.8 us -> 35.6 us
  blocking collectives: 11.2 us -> 13.9 us
  local copies, waits for them, and re-layouts: 2.71 us -> 0.01 us
    ppermute x16 -> x14, waiting for transfers between devices: 19.9 us -> 9.94 us  [ring(): return lax.ppermute(value, axes, pairs)]
    ppermute x1 -> x4, waiting for transfers between devices: 1.63 us -> 8.52 us  [mirrored(): return lax.ppermute(value, axis, [(s, s ^ bits) for s in range(count)])]
    all_to_all x1 -> x0, waiting for transfers between devices: 6.89 us -> none  [exchanged(): return lax.all_to_all(value, axis, 0, 0)]
    ppermute x16 -> x14, starting transfers between devices: 22.9 us -> 27.3 us  [ring(): return lax.ppermute(value, axes, pairs)]
    all_to_all x1 -> x0, starting transfers between devices: 3.49 us -> none  [exchanged(): return lax.all_to_all(value, axis, 0, 0)]
    ppermute x1 -> x4, starting transfers between devices: 5.41 us -> 8.37 us  [mirrored(): return lax.ppermute(value, axis, [(s, s ^ bits) for s in range(count)])]
    all_to_all x1, blocking collectives: 11.2 us -> 13.9 us  [exchanged(): return lax.all_to_all(value, ('sy', 'sx'), 0, 0, axis_index_groups=groups)]
    unnamed x34 -> x6, local copies, waits for them, and re-layouts: 2.71 us -> 0.01 us
  transfers between devices with their start and end apart: 18 -> 18, of which waited for: 7 -> 9; matrix products, arithmetic and copies ran while one was open for 1% -> 1% of each run, Pallas kernels for 15% -> 14%
where the time goes in v4:
time: 95.6 us; the launch traced here: 95.4 us
  starting transfers between devices  35.6 us (37%)
  Pallas kernels  24.7 us (26%)
  waiting for transfers between devices  18.5 us (19%)
  blocking collectives  13.9 us (15%)
  other arithmetic  1.87 us (2%)
    ppermute x14, starting transfers between devices, ring(): return lax.ppermute(value, axes, pairs)  27.3 us
    pallas_call x4, Pallas kernels, call(): pl.pallas_call(kernel, out_shape=[place(o.shape, o.dtype) for place, o in...  22.9 us
    all_to_all x1, blocking collectives, exchanged(): return lax.all_to_all(value, ('sy', 'sx'), 0, 0, axis_index_groups=groups)  13.9 us
    ppermute x14, waiting for transfers between devices, ring(): return lax.ppermute(value, axes, pairs)  9.94 us
    ppermute x4, waiting for transfers between devices, mirrored(): return lax.ppermute(value, axis, [(s, s ^ bits) for s in range(count)])  8.52 us
    ppermute x4, starting transfers between devices, mirrored(): return lax.ppermute(value, axis, [(s, s ^ bits) for s in range(count)])  8.37 us
  transfers between devices with their start and end apart: 18, of which 9 were waited for; matrix products, arithmetic and copies ran while one was open for 1% of the time, Pallas kernels for 14%

profile of v4, /device:TPU:1, one launch (start us, length us, event | category | flops | bytes accessed | tf_op | source)
XLA Modules:
  0.0 95.4 jit_solution(12920561043141716226)
XLA Ops:
  0.6 2.5 %collective-permute-start.3 = (f32[4,128,128]{2,1,0:T(8,128)}, f32[4,128,128]{2,1,0:T(8,128)S(1)}, u32[]{:S(2)}, u32[]{:S(2)}) collective-permute-start(f32[4,128,128]{2,1,0:T(8,128)} %bitcast.3), channel_id=1, source_target_pairs={{0,16},{16,32},{32,48},{48,64},{64,80},{80,96},{96,112},{112,128},... | collective-permute-start | bytes 786440 | tf_op jit(solution)/shard_map/ppermute | solution.py:419
  3.2 1.9 %shard_map.131 = (f32[64,512]{1,0:T(8,128)}, f32[192,128]{1,0:T(8,128)}, f32[192,128]{1,0:T(8,128)}, f32[128,128]{1,0:T(8,128)}) custom-call(f32[128,512]{1,0:T(8,128)} %refs_3_.2, f32[128,512]{1,0:T(8,128)} %bitcast.6, f32[4,128,128]{2,1,0:T(8,128)} %bitcast.4), custom_call_target="tpu_custom_call" | custom-call | tf_op jit(solution)/shard_map/pallas_call | solution.py:454
  5.1 1.6 %collective-permute-start.2 = (f32[64,512]{1,0:T(8,128)}, f32[64,512]{1,0:T(8,128)S(1)}, u32[]{:S(2)}, u32[]{:S(2)}) collective-permute-start(f32[64,512]{1,0:T(8,128)} %get-tuple-element.37), channel_id=1, source_target_pairs={{0,16},{16,32},{32,48},{48,64},{64,80},{80,96},{96,112},{112,128},... | collective-permute-start | bytes 393224 | tf_op jit(solution)/shard_map/ppermute | solution.py:419
  6.7 2.3 %collective-permute-start = (f32[192,128]{1,0:T(8,128)}, f32[192,128]{1,0:T(8,128)S(1)}, u32[]{:S(2)}, u32[]{:S(2)}) collective-permute-start(f32[192,128]{1,0:T(8,128)} %get-tuple-element.35), channel_id=1, source_target_pairs={{0,2},{2,4},{4,6},{6,8},{8,10},{10,12},{12,14},{14,0},{1,3},{3,5},... | collective-permute-start | bytes 294920 | tf_op jit(solution)/shard_map/ppermute | solution.py:419
  9.0 1.4 %collective-permute-start.1 = (f32[192,128]{1,0:T(8,128)}, f32[192,128]{1,0:T(8,128)S(1)}, u32[]{:S(2)}, u32[]{:S(2)}) collective-permute-start(f32[192,128]{1,0:T(8,128)} %get-tuple-element.36), channel_id=1, source_target_pairs={{0,18},{2,20},{4,22},{6,24},{8,26},{10,28},{12,30},{14,16},{16,34}... | collective-permute-start | bytes 294920 | tf_op jit(solution)/shard_map/ppermute | solution.py:419
  10.4 1.8 %collective-permute-start.5 = (f32[128,128]{1,0:T(8,128)}, f32[128,128]{1,0:T(8,128)S(1)}, u32[]{:S(2)}, u32[]{:S(2)}) collective-permute-start(f32[128,128]{1,0:T(8,128)} %get-tuple-element.51), channel_id=1, source_target_pairs={{0,2},{2,4},{4,6},{6,8},{8,10},{10,12},{12,14},{14,0},{1,3},{3,5},... | collective-permute-start | bytes 196616 | tf_op jit(solution)/shard_map/ppermute | solution.py:419
  12.2 3.0 %shard_map.132 = (f32[512,512]{1,0:T(8,128)}, f32[512,512]{1,0:T(8,128)S(1)}, f32[8,128]{1,0:T(8,128)S(1)}, bf16[384,256]{1,0:T(8,128)(2,1)S(1)}, bf16[512,768]{...) custom-call(f32[4,128,128]{2,1,0:T(8,128)} %bitcast.5, ...), custom_call_target="tpu_custom_call" | custom-call | flops 504000000 | bytes 5849088 | tf_op jit(solution)/shard_map/pallas_call | solution.py:395
  15.2 0.1 collective-permute-start.6
  15.3 5.1 %collective-permute-done.1.refs_1_ = f32[192,128]{1,0:T(8,128)S(1)} collective-permute-done((f32[192,128]{1,0:T(8,128)}, f32[192,128]{1,0:T(8,128)S(1)}, u32[]{:S(2)}, u32[]{:S(2)}) %collective-permute-start.1) | collective-permute-done | bytes 98336 | tf_op jit(solution)/shard_map/ppermute | solution.py:419
  20.4 0.0 collective-permute-start.4
  20.4 8.5 %shard_map.133 = (f32[512,768]{1,0:T(8,128)}, f32[128,384]{1,0:T(8,128)}, f32[128,384]{1,0:T(8,128)}, f32[256,128]{1,0:T(8,128)}, f32[256,128]{1,0:T(8,128)}, /*index=5*/f32[8,128]{1,0:T(8,128)S(1)}) custom-call(f32[192,128]{1,0:T(8,128)S(1)} %collective-permute-done.refs_0_, f32[192,128]{1,0:T(8,128)S(1)} %collective-permute-done.1.refs_1_, ...), custom_call_target="tpu_custom_call" | custom-call | flops 3600000000 | bytes 851968 | tf_op jit(solution)/shard_map/pallas_call | solution.py:395
  29.0 1.4 %collective-permute-done.4.refs_4_ = f32[128,512]{1,0:T(8,128)S(1)} collective-permute-done((f32[128,512]{1,0:T(8,128)S(1)}, f32[128,512]{1,0:T(8,128)S(1)}, u32[]{:S(2)}, u32[]{:S(2)}) %collective-permute-start.4) | collective-permute-done | bytes 262176 | tf_op jit(solution)/shard_map/ppermute | solution.py:419
  30.4 3.3 %collective-permute-start.7 = (f32[256,128]{1,0:T(8,128)}, f32[256,128]{1,0:T(8,128)S(1)}, u32[]{:S(2)}, u32[]{:S(2)}) collective-permute-start(f32[256,128]{1,0:T(8,128)} %get-tuple-element.55.refs_4_), channel_id=1, source_target_pairs={{0,2},{2,4},{4,6},{6,8},{8,10},{10,12},{12,14},{14,0},{1,3},{3,5},... | collective-permute-start | bytes 393224 | tf_op jit(solution)/shard_map/ppermute | solution.py:419
  33.7 2.6 %collective-permute-start.9 = (f32[8,128]{1,0:T(8,128)S(1)}, f32[8,128]{1,0:T(8,128)S(1)}, u32[]{:S(2)}, u32[]{:S(2)}) collective-permute-start(f32[8,128]{1,0:T(8,128)S(1)} %get-tuple-element.56.refs_6_), channel_id=1, source_target_pairs={{0,16},{16,0},{32,48},{48,32},{64,80},{80,64},{96,112},{112,96},{1... | collective-permute-start | bytes 12296 | tf_op jit(solution)/shard_map/ppermute | solution.py:424
  36.3 1.0 %collective-permute-done.10.refs_8_ = f32[8,128]{1,0:T(8,128)S(1)} collective-permute-done((f32[8,128]{1,0:T(8,128)S(1)}, f32[8,128]{1,0:T(8,128)S(1)}, u32[]{:S(2)}, u32[]{:S(2)}) %collective-permute-start.10) | collective-permute-done | bytes 4128 | tf_op jit(solution)/shard_map/ppermute | solution.py:424
  37.3 0.6 collective-permute-done.11.refs_9_
  38.0 0.5 collective-permute-done.8.refs_5_
  38.4 2.1 %shard_map.134 = (f32[128,640]{1,0:T(8,128)}, f32[128,640]{1,0:T(8,128)}, f32[32,8,128]{2,1,0:T(8,128)S(1)}) custom-call(f32[128,384]{1,0:T(8,128)} %get-tuple-element.52.refs_0_, f32[128,384]{1,0:T(8,128)} %get-tuple-element.53.refs_1_, f32[256,128]{1,0:T(8,128)} %get-tuple-element.54.refs_2_, f32[256,128]{1,0:T(8,128)S(1)} %collective-permute-done.7.refs_3_, ...), custom_call_target="tpu_custom_call" | custom-call | flops 1000000 | bytes 917504 | tf_op jit(solution)/shard_map/pallas_call | solution.py:395
  40.6 0.6 collective-permute-start.12
  41.2 5.0 %collective-permute-start.13 = (f32[128,640]{1,0:T(8,128)}, f32[128,640]{1,0:T(8,128)S(1)}, u32[]{:S(2)}, u32[]{:S(2)}) collective-permute-start(f32[128,640]{1,0:T(8,128)} %get-tuple-element.57.refs_0_), channel_id=1, source_target_pairs={{0,240},{16,0},{32,16},{48,32},{64,48},{80,64},{96,80},{112,96},{1... | collective-permute-start | bytes 983048 | tf_op jit(solution)/shard_map/ppermute | solution.py:419
  46.2 13.9 %all_to_all.5.refs_16_ = f32[32,8,128]{2,1,0:T(8,128)S(1)} all-to-all(f32[32,8,128]{2,1,0:T(8,128)S(1)} %get-tuple-element.64), channel_id=1, replica_groups={{0,2,4,6,8,10,12,14,64,66,68,70,72,74,76,78,128,130,132,134,136,138,140..., dimensions={0} | all-to-all | bytes 262144 | tf_op jit(solution)/shard_map/all_to_all | solution.py:436
  60.1 9.2 %shard_map.135 = (f32[128,512]{1,0:T(8,128)}, f32[64,512]{1,0:T(8,128)}, f32[64,512]{1,0:T(8,128)}) custom-call(f32[128,640]{1,0:T(8,128)} %get-tuple-element.57.refs_0_, f32[128,640]{1,0:T(8,128)S(1)} %collective-permute-done.12.refs_1_, f32[128,640]{1,0:T(8,128)} %get-tuple-element.58.refs_2_, f32[128,640]{1,0:T(8,128)S(1)} %collective-permute-done.13.refs_3_, ...), custom_call_target="tpu_custom_call" | custom-call | flops 3000000000 | bytes 9134080 | tf_op jit(solution)/shard_map/pallas_call | solution.py:395
  69.3 5.7 %collective-permute-start.14 = (f32[64,512]{1,0:T(8,128)}, f32[64,512]{1,0:T(8,128)S(1)}, u32[]{:S(2)}, u32[]{:S(2)}) collective-permute-start(f32[64,512]{1,0:T(8,128)} %get-tuple-element.65), channel_id=1, source_target_pairs={{0,1},{1,0},{2,3},{3,2},{4,5},{5,4},{6,7},{7,6},{8,9},{9,8},{10,11... | collective-permute-start | bytes 393224 | tf_op jit(solution)/shard_map/ppermute | solution.py:424
  75.0 0.6 collective-permute-start.15
  75.6 6.9 %collective-permute-done.14 = f32[64,512]{1,0:T(8,128)S(1)} collective-permute-done((f32[64,512]{1,0:T(8,128)}, f32[64,512]{1,0:T(8,128)S(1)}, u32[]{:S(2)}, u32[]{:S(2)}) %collective-permute-start.14) | collective-permute-done | bytes 131104 | tf_op jit(solution)/shard_map/ppermute | solution.py:424
  82.6 0.9 add.6
  83.5 0.3 collective-permute-done.15
  83.8 0.6 collective-permute-done.16
  84.4 8.0 %collective-permute-start.17 = (f32[128,64]{1,0:T(8,128)S(1)}, f32[128,64]{1,0:T(8,128)S(1)}, u32[]{:S(2)}, u32[]{:S(2)}) collective-permute-start(f32[128,64]{1,0:T(8,128)S(1)} %pad_maximum_fusion.1), channel_id=1, source_target_pairs={{0,14},{2,0},{4,2},{6,4},{8,6},{10,8},{12,10},{14,12},{1,15},{3,1}... | collective-permute-start | bytes 98312 | tf_op jit(solution)/shard_map/ppermute | solution.py:419
  92.4 0.1 slice_maximum_fusion
  92.6 2.0 %collective-permute-done.17 = f32[128,64]{1,0:T(8,128)S(1)} collective-permute-done((f32[128,64]{1,0:T(8,128)S(1)}, f32[128,64]{1,0:T(8,128)S(1)}, u32[]{:S(2)}, u32[]{:S(2)}) %collective-permute-start.17) | collective-permute-done | bytes 32800 | tf_op jit(solution)/shard_map/ppermute | solution.py:419
  94.6 0.8 pad_maximum_fusion
  (21 shorter events, 0.1 us)
Async XLA Ops:
  0.6 19.8 %collective-permute-start.3 = (f32[4,128,128]{2,1,0:T(8,128)}, f32[4,128,128]{2,1,0:T(8,128)S(1)}, u32[]{:S(2)}, u32[]{:S(2)}) collective-permute-start(f32[4,128,128]{2,1,0:T(8,128)} %bitcast.3), channel_id=1, source_target_pairs={{0,16},{16,32},{32,48},{48,64},{64,80},{80,96},{96,112},{112,128},... | collective-permute-start | bytes 786440 | tf_op jit(solution)/shard_map/ppermute | solution.py:419
  3.2 17.2 %copy-start.1 = (f32[1,128,512]{2,1,0:T(8,128)S(1)}, f32[1,128,512]{2,1,0:T(8,128)}, u32[]{:S(2)}) copy-start(f32[1,128,512]{2,1,0:T(8,128)} %param.13) | copy-start | bytes 786436
  3.2 17.2 %copy-start = (f32[2,8,128]{2,1,0:T(8,128)S(1)}, f32[2,8,128]{2,1,0:T(8,128)}, u32[]{:S(2)}) copy-start(f32[2,8,128]{2,1,0:T(8,128)} %constant.30.refs_13_.refs_15_) | copy-start | bytes 24580
  5.1 10.1 %copy-start.2 = (f32[128,128]{1,0:T(8,128)S(1)}, f32[128,128]{1,0:T(8,128)}, u32[]{:S(2)}) copy-start(f32[128,128]{1,0:T(8,128)} %get-tuple-element.51) | copy-start | bytes 196612
  5.1 15.3 %collective-permute-start.2 = (f32[64,512]{1,0:T(8,128)}, f32[64,512]{1,0:T(8,128)S(1)}, u32[]{:S(2)}, u32[]{:S(2)}) collective-permute-start(f32[64,512]{1,0:T(8,128)} %get-tuple-element.37), channel_id=1, source_target_pairs={{0,16},{16,32},{32,48},{48,64},{64,80},{80,96},{96,112},{112,128},... | collective-permute-start | bytes 393224 | tf_op jit(solution)/shard_map/ppermute | solution.py:419
  6.7 8.5 %collective-permute-start = (f32[192,128]{1,0:T(8,128)}, f32[192,128]{1,0:T(8,128)S(1)}, u32[]{:S(2)}, u32[]{:S(2)}) collective-permute-start(f32[192,128]{1,0:T(8,128)} %get-tuple-element.35), channel_id=1, source_target_pairs={{0,2},{2,4},{4,6},{6,8},{8,10},{10,12},{12,14},{14,0},{1,3},{3,5},... | collective-permute-start | bytes 294920 | tf_op jit(solution)/shard_map/ppermute | solution.py:419
  9.0 11.4 %collective-permute-start.1 = (f32[192,128]{1,0:T(8,128)}, f32[192,128]{1,0:T(8,128)S(1)}, u32[]{:S(2)}, u32[]{:S(2)}) collective-permute-start(f32[192,128]{1,0:T(8,128)} %get-tuple-element.36), channel_id=1, source_target_pairs={{0,18},{2,20},{4,22},{6,24},{8,26},{10,28},{12,30},{14,16},{16,34}... | collective-permute-start | bytes 294920 | tf_op jit(solution)/shard_map/ppermute | solution.py:419
  10.4 18.6 %collective-permute-start.5 = (f32[128,128]{1,0:T(8,128)}, f32[128,128]{1,0:T(8,128)S(1)}, u32[]{:S(2)}, u32[]{:S(2)}) collective-permute-start(f32[128,128]{1,0:T(8,128)} %get-tuple-element.51), channel_id=1, source_target_pairs={{0,2},{2,4},{4,6},{6,8},{8,10},{10,12},{12,14},{14,0},{1,3},{3,5},... | collective-permute-start | bytes 196616 | tf_op jit(solution)/shard_map/ppermute | solution.py:419
  15.2 13.8 %collective-permute-start.6 = (f32[128,128]{1,0:T(8,128)S(1)}, f32[128,128]{1,0:T(8,128)S(1)}, u32[]{:S(2)}, u32[]{:S(2)}) collective-permute-start(f32[128,128]{1,0:T(8,128)S(1)} %copy-done.2), channel_id=1, source_target_pairs={{0,18},{2,20},{4,22},{6,24},{8,26},{10,28},{12,30},{14,16},{16,34}... | collective-permute-start | bytes 196616 | tf_op jit(solution)/shard_map/ppermute | solution.py:419
  20.4 10.0 %collective-permute-start.4 = (f32[128,512]{1,0:T(8,128)S(1)}, f32[128,512]{1,0:T(8,128)S(1)}, u32[]{:S(2)}, u32[]{:S(2)}) collective-permute-start(f32[128,512]{1,0:T(8,128)S(1)} %bitcast.9), channel_id=1, source_target_pairs={{0,16},{16,32},{32,48},{48,64},{64,80},{80,96},{96,112},{112,128},... | collective-permute-start | bytes 786440 | tf_op jit(solution)/shard_map/ppermute | solution.py:419
  30.4 7.5 %collective-permute-start.7 = (f32[256,128]{1,0:T(8,128)}, f32[256,128]{1,0:T(8,128)S(1)}, u32[]{:S(2)}, u32[]{:S(2)}) collective-permute-start(f32[256,128]{1,0:T(8,128)} %get-tuple-element.55.refs_4_), channel_id=1, source_target_pairs={{0,2},{2,4},{4,6},{6,8},{8,10},{10,12},{12,14},{14,0},{1,3},{3,5},... | collective-permute-start | bytes 393224 | tf_op jit(solution)/shard_map/ppermute | solution.py:419
  33.7 4.8 %collective-permute-start.8 = (f32[256,128]{1,0:T(8,128)}, f32[256,128]{1,0:T(8,128)S(1)}, u32[]{:S(2)}, u32[]{:S(2)}) collective-permute-start(f32[256,128]{1,0:T(8,128)} %get-tuple-element.54.refs_2_), channel_id=1, source_target_pairs={{0,14},{2,0},{4,2},{6,4},{8,6},{10,8},{12,10},{14,12},{1,15},{3,1}... | collective-permute-start | bytes 393224 | tf_op jit(solution)/shard_map/ppermute | solution.py:419
  33.7 3.7 %collective-permute-start.10 = (f32[8,128]{1,0:T(8,128)S(1)}, f32[8,128]{1,0:T(8,128)S(1)}, u32[]{:S(2)}, u32[]{:S(2)}) collective-permute-start(f32[8,128]{1,0:T(8,128)S(1)} %get-tuple-element.56.refs_6_), channel_id=1, source_target_pairs={{0,32},{16,48},{32,0},{48,16},{64,96},{80,112},{96,64},{112,80},{1... | collective-permute-start | bytes 12296 | tf_op jit(solution)/shard_map/ppermute | solution.py:424
  33.7 4.3 %collective-permute-start.11 = (f32[8,128]{1,0:T(8,128)S(1)}, f32[8,128]{1,0:T(8,128)S(1)}, u32[]{:S(2)}, u32[]{:S(2)}) collective-permute-start(f32[8,128]{1,0:T(8,128)S(1)} %get-tuple-element.56.refs_6_), channel_id=1, source_target_pairs={{0,48},{16,32},{32,16},{48,0},{64,112},{80,96},{96,80},{112,64},{1... | collective-permute-start | bytes 12296 | tf_op jit(solution)/shard_map/ppermute | solution.py:424
  33.7 4.3 %collective-permute-start.9 = (f32[8,128]{1,0:T(8,128)S(1)}, f32[8,128]{1,0:T(8,128)S(1)}, u32[]{:S(2)}, u32[]{:S(2)}) collective-permute-start(f32[8,128]{1,0:T(8,128)S(1)} %get-tuple-element.56.refs_6_), channel_id=1, source_target_pairs={{0,16},{16,0},{32,48},{48,32},{64,80},{80,64},{96,112},{112,96},{1... | collective-permute-start | bytes 12296 | tf_op jit(solution)/shard_map/ppermute | solution.py:424
  40.6 19.5 %collective-permute-start.12 = (f32[128,640]{1,0:T(8,128)}, f32[128,640]{1,0:T(8,128)S(1)}, u32[]{:S(2)}, u32[]{:S(2)}) collective-permute-start(f32[128,640]{1,0:T(8,128)} %get-tuple-element.58.refs_2_), channel_id=1, source_target_pairs={{0,16},{16,32},{32,48},{48,64},{64,80},{80,96},{96,112},{112,128},... | collective-permute-start | bytes 983048 | tf_op jit(solution)/shard_map/ppermute | solution.py:419
  41.2 18.9 %collective-permute-start.13 = (f32[128,640]{1,0:T(8,128)}, f32[128,640]{1,0:T(8,128)S(1)}, u32[]{:S(2)}, u32[]{:S(2)}) collective-permute-start(f32[128,640]{1,0:T(8,128)} %get-tuple-element.57.refs_0_), channel_id=1, source_target_pairs={{0,240},{16,0},{32,16},{48,32},{64,48},{80,64},{96,80},{112,96},{1... | collective-permute-start | bytes 983048 | tf_op jit(solution)/shard_map/ppermute | solution.py:419
  69.3 13.2 %collective-permute-start.14 = (f32[64,512]{1,0:T(8,128)}, f32[64,512]{1,0:T(8,128)S(1)}, u32[]{:S(2)}, u32[]{:S(2)}) collective-permute-start(f32[64,512]{1,0:T(8,128)} %get-tuple-element.65), channel_id=1, source_target_pairs={{0,1},{1,0},{2,3},{3,2},{4,5},{5,4},{6,7},{7,6},{8,9},{9,8},{10,11... | collective-permute-start | bytes 393224 | tf_op jit(solution)/shard_map/ppermute | solution.py:424
  75.0 8.8 %collective-permute-start.15 = (f32[64,512]{1,0:T(8,128)}, f32[64,512]{1,0:T(8,128)S(1)}, u32[]{:S(2)}, u32[]{:S(2)}) collective-permute-start(f32[64,512]{1,0:T(8,128)} %get-tuple-element.66), channel_id=1, source_target_pairs={{0,240},{16,0},{32,16},{48,32},{64,48},{80,64},{96,80},{112,96},{1... | collective-permute-start | bytes 393224 | tf_op jit(solution)/shard_map/ppermute | solution.py:419
  75.6 8.7 %collective-permute-start.16 = (f32[64,512]{1,0:T(8,128)}, f32[64,512]{1,0:T(8,128)S(1)}, u32[]{:S(2)}, u32[]{:S(2)}) collective-permute-start(f32[64,512]{1,0:T(8,128)} %get-tuple-element.66), channel_id=1, source_target_pairs={{0,241},{1,240},{16,1},{17,0},{32,17},{33,16},{48,33},{49,32},{64,... | collective-permute-start | bytes 393224 | tf_op jit(solution)/shard_map/ppermute | solution.py:419
  84.4 10.1 %collective-permute-start.17 = (f32[128,64]{1,0:T(8,128)S(1)}, f32[128,64]{1,0:T(8,128)S(1)}, u32[]{:S(2)}, u32[]{:S(2)}) collective-permute-start(f32[128,64]{1,0:T(8,128)S(1)} %pad_maximum_fusion.1), channel_id=1, source_target_pairs={{0,14},{2,0},{4,2},{6,4},{8,6},{10,8},{12,10},{14,12},{1,15},{3,1}... | collective-permute-start | bytes 98312 | tf_op jit(solution)/shard_map/ppermute | solution.py:419

commit v5 on v4

--- a/solution.py
+++ b/solution.py
@@ -148,18 +148,32 @@
 def picked(names, hbm):
     rows, columns = edges()
     edge = {"obj_left": rows, "grad_left": rows, "windows": columns}
-    return [h.at[edge[n]] if n in edge else h for n, h in zip(names, hbm)]
+    part = {"right": pl.ds(0, S + H), "obs_left": pl.ds(S + H, S)}
+    return [h.at[edge[n]] if n in edge else h.at[part[n]] if n in part else h for n, h in zip(names, hbm)]
 
 
 def psf_kernel(names, *refs):
     total = len(names)
     hbm, refs = refs[:total], refs[total:]
-    spec_hbm, spec_ref, total_ref, *buffers = refs[:-4]
-    psf, frame, sems, parts = refs[-4:]
-    t = Copies(names, picked(names, hbm), (psf, frame) + tuple(buffers), sems)
-    psf = t["psf"]
-    lanes = dot(wide_parts(jnp.concatenate([psf[j] for j in range(psf.shape[0])], axis=0)), t["near_right"][...])
-    for j in range(psf.shape[0]):
+    down_hbm, right_hbm, diagonal_hbm, frame_hbm, spec_hbm, spec_ref, total_ref, *buffers = refs[:-5]
+    psf, obj, frame, sems, parts = refs[-5:]
+    t = Copies(names, picked(names, hbm), (psf, obj, frame) + tuple(buffers), sems)
+    count, last = psf.shape[0], pl.ds(obj.shape[1] - S, S)
+    psf, obj, frame = t["psf"], t["object"], t["frame"]
+    moves = [
+        (obj.at[pl.ds(H, H)], down_hbm),
+        (psf.at[count - 1], right_hbm.at[pl.ds(0, S)]),
+        (obj.at[pl.ds(0, H), last], right_hbm.at[pl.ds(S, H)]),
+        (frame.at[:, last], right_hbm.at[pl.ds(S + H, S)]),
+        (psf.at[count - 1], diagonal_hbm.at[pl.ds(0, S)]),
+        (obj.at[pl.ds(H, H), last], diagonal_hbm.at[pl.ds(S, H)]),
+        (frame.at[:, last], frame_hbm),
+    ]
+    moves = [pltpu.make_async_copy(*move, sems.at[total + 1 + n]) for n, move in enumerate(moves)]
+    for copy in moves:
+        copy.start()
+    lanes = dot(wide_parts(jnp.concatenate([psf[j] for j in range(count)], axis=0)), t["near_right"][...])
+    for j in range(count):
         store_parts(parts, at(j), stacked(lanes[at(j)]))
     spec_ref[...] = dot(t["near_left"][...], parts[...])
     out = pltpu.make_async_copy(spec_ref, spec_hbm, sems.at[total])
@@ -167,18 +181,20 @@
     total_ref[...] = jnp.full(total_ref.shape, jnp.sum(t["frame"][...]), F32)
     for name in names:
         t[name]
+    for copy in moves + [out]:
+        copy.wait()
+
+
+def above_kernel(psf_hbm, right, left, spec_hbm, spec_ref, psf, sems, parts):
+    t = Copies(("psf",), (psf_hbm,), (psf,), sems)
+    count = psf.shape[0]
+    lanes = dot(wide_parts(jnp.concatenate([t["psf"][j] for j in range(count)], axis=0)), right[...])
+    for j in range(count):
+        store_parts(parts, at(j), stacked(lanes[at(j)]))
+    spec_ref[...] = dot(left[...], parts[...])
+    out = pltpu.make_async_copy(spec_ref, spec_hbm, sems.at[1])
+    out.start()
     out.wait()
-
-
-def pack_kernel(obj_ref, frame_ref, psf_ref, down_ref, right_ref, diagonal_ref, frame_last):
-    width = obj_ref.shape[1]
-    last = obj_ref[:, width - S :]
-    down_ref[...] = obj_ref[H:]
-    right_ref[:S] = psf_ref[psf_ref.shape[0] - 1]
-    right_ref[S:] = last[:H]
-    diagonal_ref[:S] = psf_ref[psf_ref.shape[0] - 1]
-    diagonal_ref[S:] = last[H:]
-    frame_last[...] = frame_ref[:, width - S :]
 
 
 def alternating():
@@ -193,7 +209,7 @@
     outs_hbm, flux_ref, refs = refs[:5], refs[5], refs[6:]
     buffers, sems, (more_ref, mid_top, mid_bottom, first_ref, last_ref) = refs[:total], refs[total], refs[total + 1 : total + 6]
     x_ref, x_parts, y_parts = refs[total + 6 :]
-    got = Copies(names, hbm, buffers, sems)
+    got = Copies(names, picked(names, hbm), buffers, sems)
     outs = [
         pltpu.make_async_copy(source, out, sems.at[total + n])
         for n, (source, out) in enumerate(zip((more_ref, mid_top, mid_bottom, first_ref, last_ref), outs_hbm))
@@ -214,14 +230,13 @@
         x = jnp.concatenate([left, here], axis=1)
         for w in range(2):
             x_ref[at(2 * q + w)] = x * (windows if q == 0 else plain)[w]
-    psf_above = got["psf_above"]
-    psfs = [diagonal_ref[:S]] + [psf_above[j] for j in range(count)] + [right_ref[:S]]
+    psfs = [diagonal_ref[:S], right_ref[:S]]
     lanes = dot(wide_parts(jnp.concatenate([x_ref[...]] + psfs, axis=0)), t["near_right"][...])
-    for n in range(3 * count + 2):
+    for n in range(2 * count + 2):
         store_parts(x_parts, at(n), stacked(lanes[at(n)]))
     more_ref[...] = dot(t["near_left"][...], x_parts[:, 2 * count * S :])
     outs[0].start()
-    spec_ref = t["spec"]
+    spec_ref, spec_above = t["spec"], t["spec_above"]
     obj_left = t["obj_left"]
     sign = alternating()
     for pair in range(count // 2):
@@ -234,10 +249,8 @@
                     x_re = x_specs[at(2 * r, L), lanes]
                     x_im = x_specs[at(2 * r + 1, L), lanes]
                     j = q - w
-                    if r == 0:
-                        source, lanes = (spec_ref, at(j)) if j >= 0 else (more_ref, at(count + 1))
-                    else:
-                        source, lanes = more_ref, at(j + 1)
+                    own = (spec_ref, spec_above)[r]
+                    source, lanes = (own, at(j)) if j >= 0 else (more_ref, at(1 - r))
                     h_re, h_im = source[:L, lanes], source[L:, lanes]
                     y[r, w] = (x_re * h_re - x_im * h_im, x_re * h_im + x_im * h_re)
             if q == 0:
@@ -339,7 +352,7 @@
         store_parts(r_parts, at(count + 1 + n), stacked(value[S:]))
     spectra = dot(t["near_left"][...], r_parts[...])
     sign = alternating()
-    spec_ref, more_ref = t["spec"], t["more"]
+    spec_ref, spec_above, more_ref = t["spec"], t["spec_above"], t["more"]
     seen = []
     for n in range(count + 1):
         top = [spectra[at(c, L), at(n)] for c in range(2)]
@@ -359,10 +372,8 @@
                 slot = w if q == 0 else q + 1
                 j = q - w
                 for r in range(2):
-                    if r == 0:
-                        source, lanes = (spec_ref, at(j)) if j >= 0 else (more_ref, at(count + 1))
-                    else:
-                        source, lanes = more_ref, at(j + 1)
+                    own = (spec_ref, spec_above)[r]
+                    source, lanes = (own, at(j)) if j >= 0 else (more_ref, at(1 - r))
                     h_re, h_im = source[:L, lanes], source[L:, lanes]
                     r_re, r_im = seen[slot][r]
                     for c, part in enumerate((r_re * h_re + r_im * h_im, r_im * h_re - r_re * h_im)):
@@ -404,10 +415,9 @@
 
 
 def like(arrays):
-    return [pltpu.VMEM(x.shape[1:] if n in PICKED else x.shape, x.dtype) for n, x in arrays.items()]
-
-
-PICKED = ("windows", "obj_left", "grad_left")
+    shapes = {"right": (S + H, S), "obs_left": (S, S)}
+    shapes |= {n: arrays[n].shape[1:] for n in ("windows", "obj_left", "grad_left") if n in arrays}
+    return [pltpu.VMEM(shapes.get(n, x.shape), x.dtype) for n, x in arrays.items()]
 
 
 def ring(value, axes, moves):
@@ -451,34 +461,40 @@
     observed = frames_data[0]
     t = {name: jnp.asarray(value) for name, value in tables().items()}
     psf_above = down(psfs)
-    pack_down, pack_right, pack_diagonal, obs_last = pl.pallas_call(
-        pack_kernel,
-        out_shape=(f32(H, width), f32(S + H, S), f32(S + H, S), f32(S, S)),
-    )(object_field, observed, psfs)
+    kept = {k: t[k] for k in ("near_right", "near_left", "windows", "obj_left", "near_inverse", "out_right")}
+    named = {"psf": psfs, "object": object_field, "frame": observed} | kept
+    pack_down, pack_right, pack_diagonal, obs_last, spec, spec_here, total, *got = call(
+        functools.partial(psf_kernel, tuple(named)),
+        named,
+        {},
+        [(pltpu.HBM, f32(H, width)), (pltpu.HBM, f32(2 * S + H, S)), (pltpu.HBM, f32(S + H, S)),
+         (pltpu.HBM, f32(S, S)),
+         (pltpu.HBM, f32(2 * L, width)), (pltpu.VMEM, f32(2 * L, width)), (pltpu.VMEM, f32(8, S))]
+        + [(pltpu.VMEM, x) for x in like(kept)],
+        [pltpu.VMEM(psfs.shape, F32), pltpu.VMEM(object_field.shape, F32), pltpu.VMEM(observed.shape, F32),
+         pltpu.SemaphoreType.DMA((len(named) + 8,)), pltpu.VMEM((6 * S, width), BF16)],
+        16,
+        6 * 84 * 10**6,
+    )
     obj_above = down(pack_down)
     got_diagonal = ring(pack_diagonal, ("sy", "sx"), (1, 1))
     got_right = ring(pack_right, ("sx",), (1,))
     obs_above = down(observed)
-    obs_left = ring(obs_last, ("sx",), (1,))
     obs_diagonal = ring(obs_last, ("sy", "sx"), (1, 1))
-
-    kept = {k: t[k] for k in ("near_right", "near_left", "windows", "obj_left", "near_inverse", "out_right")}
-    named = {"psf": psfs, "frame": observed} | kept
-    spec, spec_here, total, *got = call(
-        functools.partial(psf_kernel, tuple(named)),
-        named,
-        {},
-        [(pltpu.HBM, f32(2 * L, width)), (pltpu.VMEM, f32(2 * L, width)), (pltpu.VMEM, f32(8, S))]
-        + [(pltpu.VMEM, x) for x in like(kept)],
-        [pltpu.VMEM(psfs.shape, F32), pltpu.VMEM(observed.shape, F32),
-         pltpu.SemaphoreType.DMA((len(named) + 1,)), pltpu.VMEM((6 * S, width), BF16)],
+    ready = dict(zip(kept, got))
+    spec_above, spec_above_here = call(
+        above_kernel,
+        {"psf": psf_above},
+        {k: ready[k] for k in ("near_right", "near_left")},
+        [(pltpu.HBM, f32(2 * L, width)), (pltpu.VMEM, f32(2 * L, width))],
+        [pltpu.VMEM(psfs.shape, F32), pltpu.SemaphoreType.DMA((2,)), pltpu.VMEM((6 * S, width), BF16)],
         16,
         6 * 84 * 10**6,
-    )
-    ready = dict(zip(kept, got)) | {"spec": spec_here, "total": total, "plain": t["windows"][0]}
-    named = {"right": got_right, "diagonal": got_diagonal, "above": obj_above, "own": object_field,
-             "psf_above": psf_above}
-    outs = [f32(2 * L, width + 2 * S), f32(S, width - S), f32(S, width - S), f32(L, S), f32(L, S)]
+        ("psf",),
+    )
+    ready |= {"spec_above": spec_above_here, "spec": spec_here, "total": total, "plain": t["windows"][0]}
+    named = {"right": got_right, "diagonal": got_diagonal, "above": obj_above, "own": object_field}
+    outs = [f32(2 * L, 2 * S), f32(S, width - S), f32(S, width - S), f32(L, S), f32(L, S)]
     more, mid_top, mid_bottom, first, last, flux = call(
         functools.partial(model_kernel, tuple(named), tuple(ready)),
         named,
@@ -486,14 +502,14 @@
         [(pltpu.HBM, o) for o in outs] + [(pltpu.VMEM, f32(8, S))],
         like(named) + [pltpu.SemaphoreType.DMA((len(named) + len(outs),))]
         + [pltpu.VMEM(o.shape, F32) for o in outs]
-        + [pltpu.VMEM((2 * width, S), F32), pltpu.VMEM((6 * S, 3 * width + 2 * S), BF16),
+        + [pltpu.VMEM((2 * width, S), F32), pltpu.VMEM((6 * S, 2 * width + 2 * S), BF16),
            pltpu.VMEM((6 * L, 2 * width + 2 * S), BF16)],
         36,
         6 * 600 * 10**6,
-        ("right", "diagonal", "above", "psf_above"),
-    )
-    mid_top, mid_bottom, first, last, flux, obs_above, obs_left, obs_diagonal = lax.optimization_barrier(
-        (mid_top, mid_bottom, first, last, flux, obs_above, obs_left, obs_diagonal)
+        ("right", "diagonal", "above"),
+    )
+    mid_top, mid_bottom, first, last, flux, obs_above, obs_diagonal = lax.optimization_barrier(
+        (mid_top, mid_bottom, first, last, flux, obs_above, obs_diagonal)
     )
     from_right = ring(first, ("sx",), (-1,))
     from_left = ring(last, ("sx",), (1,))
@@ -518,8 +534,8 @@
 
     named = {"top": top, "above": above, "bottom": bottom, "below": below,
              "obs_above": obs_above, "obs": observed,
-             "obs_diagonal": obs_diagonal, "obs_left": obs_left,
-             "res_right": t["res_right"], "near_left": t["near_left"], "spec": spec, "more": more,
+             "obs_diagonal": obs_diagonal, "obs_left": got_right,
+             "res_right": t["res_right"], "near_left": t["near_left"], "spec": spec, "spec_above": spec_above, "more": more,
              "grad_left": t["grad_left"], "grad_right": t["grad_right"],
              "windows": t["windows"], "plain": t["windows"][0]}
     outs = [f32(S, width), f32(H, width), f32(H, width)]

time: 95.6 us -> 92.7 us (0.970)
  starting transfers between devices: 35.6 us -> 31.9 us
  blocking collectives: 13.9 us -> 15 us
    ppermute x14 -> x13, starting transfers between devices: 27.3 us -> 22.6 us  [ring(): return lax.ppermute(value, axes, pairs)]
    ppermute x14 -> x13, waiting for transfers between devices: 9.94 us -> 13.9 us  [ring(): return lax.ppermute(value, axes, pairs)]
    ppermute x4, waiting for transfers between devices: 8.52 us -> 4.85 us  [mirrored(): return lax.ppermute(value, axis, [(s, s ^ bits) for s in range(count)])]
    pallas_call x1 -> x0, Pallas kernels: 1.89 us -> none  [per_device(): pl.pallas_call(pack_kernel, out_shape=(f32(H, width), f32(S + H, S), f32(...]
    pallas_call x4 -> x5, Pallas kernels: 22.9 us -> 24.2 us  [call(): pl.pallas_call(kernel, out_shape=[place(o.shape, o.dtype) for place, o in...]
    all_to_all x1, blocking collectives: 13.9 us -> 15 us  [exchanged(): return lax.all_to_all(value, ('sy', 'sx'), 0, 0, axis_index_groups=groups)]
  transfers between devices with their start and end apart: 18 -> 17, of which waited for: 9 -> 8; matrix products, arithmetic and copies ran while one was open for 1% -> 1% of each run, Pallas kernels for 14% -> 14%
where the time goes in v5:
time: 92.7 us; the launch traced here: 92.5 us
  starting transfers between devices  31.9 us (34%)
  Pallas kernels  24.2 us (26%)
  waiting for transfers between devices  18.8 us (20%)
  blocking collectives  15 us (16%)
  other arithmetic  1.87 us (2%)
    pallas_call x5, Pallas kernels, call(): pl.pallas_call(kernel, out_shape=[place(o.shape, o.dtype) for place, o in...  24.2 us
    ppermute x13, starting transfers between devices, ring(): return lax.ppermute(value, axes, pairs)  22.6 us
    all_to_all x1, blocking collectives, exchanged(): return lax.all_to_all(value, ('sy', 'sx'), 0, 0, axis_index_groups=groups)  15 us
    ppermute x13, waiting for transfers between devices, ring(): return lax.ppermute(value, axes, pairs)  13.9 us
    ppermute x4, starting transfers between devices, mirrored(): return lax.ppermute(value, axis, [(s, s ^ bits) for s in range(count)])  9.31 us
    ppermute x4, waiting for transfers between devices, mirrored(): return lax.ppermute(value, axis, [(s, s ^ bits) for s in range(count)])  4.85 us
  transfers between devices with their start and end apart: 17, of which 8 were waited for; matrix products, arithmetic and copies ran while one was open for 1% of the time, Pallas kernels for 14%

profile of v5, /device:TPU:1, one launch (start us, length us, event | category | flops | bytes accessed | tf_op | source)
XLA Modules:
  0.0 92.5 jit_solution(8757703145425559472)
XLA Ops:
  0.6 0.0 copy-start.1
  0.6 2.5 %collective-permute-start.3 = (f32[4,128,128]{2,1,0:T(8,128)}, f32[4,128,128]{2,1,0:T(8,128)S(1)}, u32[]{:S(2)}, u32[]{:S(2)}) collective-permute-start(f32[4,128,128]{2,1,0:T(8,128)} %bitcast.3), channel_id=1, source_target_pairs={{0,16},{16,32},{32,48},{48,64},{64,80},{80,96},{96,112},{112,128},... | collective-permute-start | bytes 786440 | tf_op jit(solution)/shard_map/ppermute | solution.py:429
  3.2 3.2 %shard_map.131 = (f32[64,512]{1,0:T(8,128)}, f32[320,128]{1,0:T(8,128)}, f32[192,128]{1,0:T(8,128)}, f32[128,128]{1,0:T(8,128)}, f32[512,512]{1,0:T(8,128)}, /*i...) custom-call(f32[4,128,128]{2,1,0:T(8,128)} %bitcast.4, ...), custom_call_target="tpu_custom_call" | custom-call | flops 504000000 | bytes 6111232 | tf_op jit(solution)/shard_map/pallas_call | solution.py:406
  6.4 2.1 %collective-permute-start = (f32[320,128]{1,0:T(8,128)}, f32[320,128]{1,0:T(8,128)S(1)}, u32[]{:S(2)}, u32[]{:S(2)}) collective-permute-start(f32[320,128]{1,0:T(8,128)} %get-tuple-element.36), channel_id=1, source_target_pairs={{0,2},{2,4},{4,6},{6,8},{8,10},{10,12},{12,14},{14,0},{1,3},{3,5},... | collective-permute-start | bytes 491528 | tf_op jit(solution)/shard_map/ppermute | solution.py:429
  8.5 1.6 %collective-permute-start.2 = (f32[64,512]{1,0:T(8,128)}, f32[64,512]{1,0:T(8,128)S(1)}, u32[]{:S(2)}, u32[]{:S(2)}) collective-permute-start(f32[64,512]{1,0:T(8,128)} %get-tuple-element.38), channel_id=1, source_target_pairs={{0,16},{16,32},{32,48},{48,64},{64,80},{80,96},{96,112},{112,128},... | collective-permute-start | bytes 393224 | tf_op jit(solution)/shard_map/ppermute | solution.py:429
  10.1 1.7 %collective-permute-start.1 = (f32[192,128]{1,0:T(8,128)}, f32[192,128]{1,0:T(8,128)S(1)}, u32[]{:S(2)}, u32[]{:S(2)}) collective-permute-start(f32[192,128]{1,0:T(8,128)} %get-tuple-element.37), channel_id=1, source_target_pairs={{0,18},{2,20},{4,22},{6,24},{8,26},{10,28},{12,30},{14,16},{16,34}... | collective-permute-start | bytes 294920 | tf_op jit(solution)/shard_map/ppermute | solution.py:429
  11.8 0.0 collective-permute-start.4
  11.8 2.1 %collective-permute-done.3.psf_hbm = f32[4,128,128]{2,1,0:T(8,128)S(1)} collective-permute-done((f32[4,128,128]{2,1,0:T(8,128)}, f32[4,128,128]{2,1,0:T(8,128)S(1)}, u32[]{:S(2)}, u32[]{:S(2)}) %collective-permute-start.3) | collective-permute-done | bytes 262176 | tf_op jit(solution)/shard_map/ppermute | solution.py:429
  13.9 0.9 collective-permute-start.5
  14.8 1.9 %shard_map.132 = (f32[512,512]{1,0:T(8,128)}, f32[512,512]{1,0:T(8,128)S(1)}) custom-call(f32[4,128,128]{2,1,0:T(8,128)S(1)} %collective-permute-done.3.psf_hbm, bf16[384,256]{1,0:T(8,128)(2,1)S(1)} %get-tuple-element.39.right.refs_4_, bf16[512,768]{1,0:T(8,128)(2,1)S(1)} %get-tuple-element.40.left.refs_5_), custom_call_target="tpu_custom_call" | custom-call | flops 504000000 | bytes 262144 | tf_op jit(solution)/shard_map/pallas_call | solution.py:406
  16.7 3.7 %collective-permute-done.1.refs_1_ = f32[192,128]{1,0:T(8,128)S(1)} collective-permute-done((f32[192,128]{1,0:T(8,128)}, f32[192,128]{1,0:T(8,128)S(1)}, u32[]{:S(2)}, u32[]{:S(2)}) %collective-permute-start.1) | collective-permute-done | bytes 98336 | tf_op jit(solution)/shard_map/ppermute | solution.py:429
  20.4 7.8 %shard_map.133 = (f32[512,256]{1,0:T(8,128)}, f32[128,384]{1,0:T(8,128)}, f32[128,384]{1,0:T(8,128)}, f32[256,128]{1,0:T(8,128)}, f32[256,128]{1,0:T(8,128)}, /*index=5*/f32[8,128]{1,0:T(8,128)S(1)}) custom-call(f32[320,128]{1,0:T(8,128)S(1)} %collective-permute-done.refs_0_.refs_7_, f32[192,128]{1,0:T(8,128)S(1)} %collective-permute-done.1.refs_1_, ...), custom_call_target="tpu_custom_call" | custom-call | flops 3600000000 | bytes 655360 | tf_op jit(solution)/shard_map/pallas_call | solution.py:406
  28.2 1.3 %collective-permute-start.6 = (f32[256,128]{1,0:T(8,128)}, f32[256,128]{1,0:T(8,128)S(1)}, u32[]{:S(2)}, u32[]{:S(2)}) collective-permute-start(f32[256,128]{1,0:T(8,128)} %get-tuple-element.57.refs_4_), channel_id=1, source_target_pairs={{0,2},{2,4},{4,6},{6,8},{8,10},{10,12},{12,14},{14,0},{1,3},{3,5},... | collective-permute-start | bytes 393224 | tf_op jit(solution)/shard_map/ppermute | solution.py:429
  29.6 1.0 %collective-permute-start.7 = (f32[256,128]{1,0:T(8,128)}, f32[256,128]{1,0:T(8,128)S(1)}, u32[]{:S(2)}, u32[]{:S(2)}) collective-permute-start(f32[256,128]{1,0:T(8,128)} %get-tuple-element.56.refs_2_), channel_id=1, source_target_pairs={{0,14},{2,0},{4,2},{6,4},{8,6},{10,8},{12,10},{14,12},{1,15},{3,1}... | collective-permute-start | bytes 393224 | tf_op jit(solution)/shard_map/ppermute | solution.py:429
  30.6 3.5 %collective-permute-start.9 = (f32[8,128]{1,0:T(8,128)S(1)}, f32[8,128]{1,0:T(8,128)S(1)}, u32[]{:S(2)}, u32[]{:S(2)}) collective-permute-start(f32[8,128]{1,0:T(8,128)S(1)} %get-tuple-element.58.refs_6_), channel_id=1, source_target_pairs={{0,32},{16,48},{32,0},{48,16},{64,96},{80,112},{96,64},{112,80},{1... | collective-permute-start | bytes 12296 | tf_op jit(solution)/shard_map/ppermute | solution.py:434
  34.1 0.7 collective-permute-done.10.refs_9_
  34.8 0.6 collective-permute-done.9.refs_8_
  35.5 2.1 %shard_map.134 = (f32[128,640]{1,0:T(8,128)}, f32[128,640]{1,0:T(8,128)}, f32[32,8,128]{2,1,0:T(8,128)S(1)}) custom-call(f32[128,384]{1,0:T(8,128)} %get-tuple-element.54.refs_0_, f32[128,384]{1,0:T(8,128)} %get-tuple-element.55.refs_1_, f32[256,128]{1,0:T(8,128)} %get-tuple-element.56.refs_2_, f32[256,128]{1,0:T(8,128)S(1)} %collective-permute-done.6.refs_3_, ...), custom_call_target="tpu_custom_call" | custom-call | flops 1000000 | bytes 917504 | tf_op jit(solution)/shard_map/pallas_call | solution.py:406
  37.6 0.3 collective-permute-start.11
  37.9 5.4 %collective-permute-start.12 = (f32[128,640]{1,0:T(8,128)}, f32[128,640]{1,0:T(8,128)S(1)}, u32[]{:S(2)}, u32[]{:S(2)}) collective-permute-start(f32[128,640]{1,0:T(8,128)} %get-tuple-element.59.refs_0_), channel_id=1, source_target_pairs={{0,240},{16,0},{32,16},{48,32},{64,48},{80,64},{96,80},{112,96},{1... | collective-permute-start | bytes 983048 | tf_op jit(solution)/shard_map/ppermute | solution.py:429
  43.2 15.0 %all_to_all.5.refs_17_ = f32[32,8,128]{2,1,0:T(8,128)S(1)} all-to-all(f32[32,8,128]{2,1,0:T(8,128)S(1)} %get-tuple-element.66), channel_id=1, replica_groups={{0,2,4,6,8,10,12,14,64,66,68,70,72,74,76,78,128,130,132,134,136,138,140..., dimensions={0} | all-to-all | bytes 262144 | tf_op jit(solution)/shard_map/all_to_all | solution.py:446
  58.2 9.2 %shard_map.135 = (f32[128,512]{1,0:T(8,128)}, f32[64,512]{1,0:T(8,128)}, f32[64,512]{1,0:T(8,128)}) custom-call(f32[128,640]{1,0:T(8,128)} %get-tuple-element.59.refs_0_, f32[128,640]{1,0:T(8,128)S(1)} %collective-permute-done.11.refs_1_, f32[128,640]{1,0:T(8,128)} %get-tuple-element.60.refs_2_, f32[128,640]{1,0:T(8,128)S(1)} %collective-permute-done.12.refs_3_, ...), custom_call_target="tpu_custom_call" | custom-call | flops 3000000000 | bytes 9232384 | tf_op jit(solution)/shard_map/pallas_call | solution.py:406
  67.5 5.8 %collective-permute-start.13 = (f32[64,512]{1,0:T(8,128)}, f32[64,512]{1,0:T(8,128)S(1)}, u32[]{:S(2)}, u32[]{:S(2)}) collective-permute-start(f32[64,512]{1,0:T(8,128)} %get-tuple-element.67), channel_id=1, source_target_pairs={{0,1},{1,0},{2,3},{3,2},{4,5},{5,4},{6,7},{7,6},{8,9},{9,8},{10,11... | collective-permute-start | bytes 393224 | tf_op jit(solution)/shard_map/ppermute | solution.py:434
  73.2 0.2 collective-permute-start.14
  73.4 3.5 %collective-permute-done.13 = f32[64,512]{1,0:T(8,128)S(1)} collective-permute-done((f32[64,512]{1,0:T(8,128)}, f32[64,512]{1,0:T(8,128)S(1)}, u32[]{:S(2)}, u32[]{:S(2)}) %collective-permute-start.13) | collective-permute-done | bytes 131104 | tf_op jit(solution)/shard_map/ppermute | solution.py:434
  77.0 0.9 %add.6 = f32[64,512]{1,0:T(8,128)S(1)} add(f32[64,512]{1,0:T(8,128)} %get-tuple-element.67, f32[64,512]{1,0:T(8,128)S(1)} %collective-permute-done.13) | non-fusion elementwise | flops 32768 | bytes 393216 | tf_op jit(solution)/shard_map/add | solution.py:558
  77.9 4.2 %collective-permute-done.14 = f32[64,512]{1,0:T(8,128)S(1)} collective-permute-done((f32[64,512]{1,0:T(8,128)}, f32[64,512]{1,0:T(8,128)S(1)}, u32[]{:S(2)}, u32[]{:S(2)}) %collective-permute-start.14) | collective-permute-done | bytes 131104 | tf_op jit(solution)/shard_map/ppermute | solution.py:429
  82.1 1.5 %collective-permute-done.15 = f32[64,512]{1,0:T(8,128)S(1)} collective-permute-done((f32[64,512]{1,0:T(8,128)}, f32[64,512]{1,0:T(8,128)S(1)}, u32[]{:S(2)}, u32[]{:S(2)}) %collective-permute-start.15) | collective-permute-done | bytes 131104 | tf_op jit(solution)/shard_map/ppermute | solution.py:429
  83.6 5.6 %collective-permute-start.16 = (f32[128,64]{1,0:T(8,128)S(1)}, f32[128,64]{1,0:T(8,128)S(1)}, u32[]{:S(2)}, u32[]{:S(2)}) collective-permute-start(f32[128,64]{1,0:T(8,128)S(1)} %pad_maximum_fusion.1), channel_id=1, source_target_pairs={{0,14},{2,0},{4,2},{6,4},{8,6},{10,8},{12,10},{14,12},{1,15},{3,1}... | collective-permute-start | bytes 98312 | tf_op jit(solution)/shard_map/ppermute | solution.py:429
  89.2 0.1 slice_maximum_fusion
  89.3 2.4 %collective-permute-done.16 = f32[128,64]{1,0:T(8,128)S(1)} collective-permute-done((f32[128,64]{1,0:T(8,128)S(1)}, f32[128,64]{1,0:T(8,128)S(1)}, u32[]{:S(2)}, u32[]{:S(2)}) %collective-permute-start.16) | collective-permute-done | bytes 32800 | tf_op jit(solution)/shard_map/ppermute | solution.py:429
  91.7 0.8 pad_maximum_fusion
  (17 shorter events, 0.1 us)
Async XLA Ops:
  0.6 11.2 %copy-start.1 = (f32[1,128,512]{2,1,0:T(8,128)S(1)}, f32[1,128,512]{2,1,0:T(8,128)}, u32[]{:S(2)}) copy-start(f32[1,128,512]{2,1,0:T(8,128)} %param.13) | copy-start | bytes 786436
  0.6 13.3 %collective-permute-start.3 = (f32[4,128,128]{2,1,0:T(8,128)}, f32[4,128,128]{2,1,0:T(8,128)S(1)}, u32[]{:S(2)}, u32[]{:S(2)}) collective-permute-start(f32[4,128,128]{2,1,0:T(8,128)} %bitcast.3), channel_id=1, source_target_pairs={{0,16},{16,32},{32,48},{48,64},{64,80},{80,96},{96,112},{112,128},... | collective-permute-start | bytes 786440 | tf_op jit(solution)/shard_map/ppermute | solution.py:429
  3.2 17.2 %copy-start = (f32[2,8,128]{2,1,0:T(8,128)S(1)}, f32[2,8,128]{2,1,0:T(8,128)}, u32[]{:S(2)}) copy-start(f32[2,8,128]{2,1,0:T(8,128)} %constant.30.refs_13_.refs_16_) | copy-start | bytes 24580
  6.4 14.0 %collective-permute-start = (f32[320,128]{1,0:T(8,128)}, f32[320,128]{1,0:T(8,128)S(1)}, u32[]{:S(2)}, u32[]{:S(2)}) collective-permute-start(f32[320,128]{1,0:T(8,128)} %get-tuple-element.36), channel_id=1, source_target_pairs={{0,2},{2,4},{4,6},{6,8},{8,10},{10,12},{12,14},{14,0},{1,3},{3,5},... | collective-permute-start | bytes 491528 | tf_op jit(solution)/shard_map/ppermute | solution.py:429
  8.5 12.0 %collective-permute-start.2 = (f32[64,512]{1,0:T(8,128)}, f32[64,512]{1,0:T(8,128)S(1)}, u32[]{:S(2)}, u32[]{:S(2)}) collective-permute-start(f32[64,512]{1,0:T(8,128)} %get-tuple-element.38), channel_id=1, source_target_pairs={{0,16},{16,32},{32,48},{48,64},{64,80},{80,96},{96,112},{112,128},... | collective-permute-start | bytes 393224 | tf_op jit(solution)/shard_map/ppermute | solution.py:429
  10.1 10.3 %collective-permute-start.1 = (f32[192,128]{1,0:T(8,128)}, f32[192,128]{1,0:T(8,128)S(1)}, u32[]{:S(2)}, u32[]{:S(2)}) collective-permute-start(f32[192,128]{1,0:T(8,128)} %get-tuple-element.37), channel_id=1, source_target_pairs={{0,18},{2,20},{4,22},{6,24},{8,26},{10,28},{12,30},{14,16},{16,34}... | collective-permute-start | bytes 294920 | tf_op jit(solution)/shard_map/ppermute | solution.py:429
  11.8 16.4 %collective-permute-start.4 = (f32[128,512]{1,0:T(8,128)S(1)}, f32[128,512]{1,0:T(8,128)S(1)}, u32[]{:S(2)}, u32[]{:S(2)}) collective-permute-start(f32[128,512]{1,0:T(8,128)S(1)} %bitcast.7), channel_id=1, source_target_pairs={{0,16},{16,32},{32,48},{48,64},{64,80},{80,96},{96,112},{112,128},... | collective-permute-start | bytes 786440 | tf_op jit(solution)/shard_map/ppermute | solution.py:429
  13.9 14.3 %collective-permute-start.5 = (f32[128,128]{1,0:T(8,128)}, f32[128,128]{1,0:T(8,128)S(1)}, u32[]{:S(2)}, u32[]{:S(2)}) collective-permute-start(f32[128,128]{1,0:T(8,128)} %get-tuple-element.53), channel_id=1, source_target_pairs={{0,18},{2,20},{4,22},{6,24},{8,26},{10,28},{12,30},{14,16},{16,34}... | collective-permute-start | bytes 196616 | tf_op jit(solution)/shard_map/ppermute | solution.py:429
  28.2 7.2 %collective-permute-start.6 = (f32[256,128]{1,0:T(8,128)}, f32[256,128]{1,0:T(8,128)S(1)}, u32[]{:S(2)}, u32[]{:S(2)}) collective-permute-start(f32[256,128]{1,0:T(8,128)} %get-tuple-element.57.refs_4_), channel_id=1, source_target_pairs={{0,2},{2,4},{4,6},{6,8},{8,10},{10,12},{12,14},{14,0},{1,3},{3,5},... | collective-permute-start | bytes 393224 | tf_op jit(solution)/shard_map/ppermute | solution.py:429
  29.6 5.9 %collective-permute-start.7 = (f32[256,128]{1,0:T(8,128)}, f32[256,128]{1,0:T(8,128)S(1)}, u32[]{:S(2)}, u32[]{:S(2)}) collective-permute-start(f32[256,128]{1,0:T(8,128)} %get-tuple-element.56.refs_2_), channel_id=1, source_target_pairs={{0,14},{2,0},{4,2},{6,4},{8,6},{10,8},{12,10},{14,12},{1,15},{3,1}... | collective-permute-start | bytes 393224 | tf_op jit(solution)/shard_map/ppermute | solution.py:429
  30.6 4.3 %collective-permute-start.10 = (f32[8,128]{1,0:T(8,128)S(1)}, f32[8,128]{1,0:T(8,128)S(1)}, u32[]{:S(2)}, u32[]{:S(2)}) collective-permute-start(f32[8,128]{1,0:T(8,128)S(1)} %get-tuple-element.58.refs_6_), channel_id=1, source_target_pairs={{0,48},{16,32},{32,16},{48,0},{64,112},{80,96},{96,80},{112,64},{1... | collective-permute-start | bytes 12296 | tf_op jit(solution)/shard_map/ppermute | solution.py:434
  30.6 4.3 %collective-permute-start.8 = (f32[8,128]{1,0:T(8,128)S(1)}, f32[8,128]{1,0:T(8,128)S(1)}, u32[]{:S(2)}, u32[]{:S(2)}) collective-permute-start(f32[8,128]{1,0:T(8,128)S(1)} %get-tuple-element.58.refs_6_), channel_id=1, source_target_pairs={{0,16},{16,0},{32,48},{48,32},{64,80},{80,64},{96,112},{112,96},{1... | collective-permute-start | bytes 12296 | tf_op jit(solution)/shard_map/ppermute | solution.py:434
  30.6 4.9 %collective-permute-start.9 = (f32[8,128]{1,0:T(8,128)S(1)}, f32[8,128]{1,0:T(8,128)S(1)}, u32[]{:S(2)}, u32[]{:S(2)}) collective-permute-start(f32[8,128]{1,0:T(8,128)S(1)} %get-tuple-element.58.refs_6_), channel_id=1, source_target_pairs={{0,32},{16,48},{32,0},{48,16},{64,96},{80,112},{96,64},{112,80},{1... | collective-permute-start | bytes 12296 | tf_op jit(solution)/shard_map/ppermute | solution.py:434
  37.6 20.6 %collective-permute-start.11 = (f32[128,640]{1,0:T(8,128)}, f32[128,640]{1,0:T(8,128)S(1)}, u32[]{:S(2)}, u32[]{:S(2)}) collective-permute-start(f32[128,640]{1,0:T(8,128)} %get-tuple-element.60.refs_2_), channel_id=1, source_target_pairs={{0,16},{16,32},{32,48},{48,64},{64,80},{80,96},{96,112},{112,128},... | collective-permute-start | bytes 983048 | tf_op jit(solution)/shard_map/ppermute | solution.py:429
  37.9 20.3 %collective-permute-start.12 = (f32[128,640]{1,0:T(8,128)}, f32[128,640]{1,0:T(8,128)S(1)}, u32[]{:S(2)}, u32[]{:S(2)}) collective-permute-start(f32[128,640]{1,0:T(8,128)} %get-tuple-element.59.refs_0_), channel_id=1, source_target_pairs={{0,240},{16,0},{32,16},{48,32},{64,48},{80,64},{96,80},{112,96},{1... | collective-permute-start | bytes 983048 | tf_op jit(solution)/shard_map/ppermute | solution.py:429
  67.5 9.5 %collective-permute-start.13 = (f32[64,512]{1,0:T(8,128)}, f32[64,512]{1,0:T(8,128)S(1)}, u32[]{:S(2)}, u32[]{:S(2)}) collective-permute-start(f32[64,512]{1,0:T(8,128)} %get-tuple-element.67), channel_id=1, source_target_pairs={{0,1},{1,0},{2,3},{3,2},{4,5},{5,4},{6,7},{7,6},{8,9},{9,8},{10,11... | collective-permute-start | bytes 393224 | tf_op jit(solution)/shard_map/ppermute | solution.py:434
  73.2 8.9 %collective-permute-start.14 = (f32[64,512]{1,0:T(8,128)}, f32[64,512]{1,0:T(8,128)S(1)}, u32[]{:S(2)}, u32[]{:S(2)}) collective-permute-start(f32[64,512]{1,0:T(8,128)} %get-tuple-element.68), channel_id=1, source_target_pairs={{0,240},{16,0},{32,16},{48,32},{64,48},{80,64},{96,80},{112,96},{1... | collective-permute-start | bytes 393224 | tf_op jit(solution)/shard_map/ppermute | solution.py:429
  73.4 10.1 %collective-permute-start.15 = (f32[64,512]{1,0:T(8,128)}, f32[64,512]{1,0:T(8,128)S(1)}, u32[]{:S(2)}, u32[]{:S(2)}) collective-permute-start(f32[64,512]{1,0:T(8,128)} %get-tuple-element.68), channel_id=1, source_target_pairs={{0,241},{1,240},{16,1},{17,0},{32,17},{33,16},{48,33},{49,32},{64,... | collective-permute-start | bytes 393224 | tf_op jit(solution)/shard_map/ppermute | solution.py:429
  83.6 8.1 %collective-permute-start.16 = (f32[128,64]{1,0:T(8,128)S(1)}, f32[128,64]{1,0:T(8,128)S(1)}, u32[]{:S(2)}, u32[]{:S(2)}) collective-permute-start(f32[128,64]{1,0:T(8,128)S(1)} %pad_maximum_fusion.1), channel_id=1, source_target_pairs={{0,14},{2,0},{4,2},{6,4},{8,6},{10,8},{12,10},{14,12},{1,15},{3,1}... | collective-permute-start | bytes 98312 | tf_op jit(solution)/shard_map/ppermute | solution.py:429

commit v6 on v5

--- a/solution.py
+++ b/solution.py
@@ -206,14 +206,10 @@
     total = len(names)
     hbm, refs = refs[:total], refs[total:]
     t, refs = dict(zip(ready, refs)), refs[len(ready) :]
-    outs_hbm, flux_ref, refs = refs[:5], refs[5], refs[6:]
-    buffers, sems, (more_ref, mid_top, mid_bottom, first_ref, last_ref) = refs[:total], refs[total], refs[total + 1 : total + 6]
-    x_ref, x_parts, y_parts = refs[total + 6 :]
+    more_hbm, mid_top, mid_bottom, first_ref, last_ref, flux_ref = refs[:6]
+    buffers, sems, more_ref, x_ref, x_parts, y_parts = refs[6 : 6 + total], *refs[6 + total :]
     got = Copies(names, picked(names, hbm), buffers, sems)
-    outs = [
-        pltpu.make_async_copy(source, out, sems.at[total + n])
-        for n, (source, out) in enumerate(zip((more_ref, mid_top, mid_bottom, first_ref, last_ref), outs_hbm))
-    ]
+    out = pltpu.make_async_copy(more_ref, more_hbm, sems.at[total])
     row_edge, column_edge = edges()
     alpha, beta = 1.0 - row_edge.astype(F32), 1.0 - column_edge.astype(F32)
     right_ref, diagonal_ref, above_ref, own_ref = [got[n] for n in ("right", "diagonal", "above", "own")]
@@ -235,7 +231,7 @@
     for n in range(2 * count + 2):
         store_parts(x_parts, at(n), stacked(lanes[at(n)]))
     more_ref[...] = dot(t["near_left"][...], x_parts[:, 2 * count * S :])
-    outs[0].start()
+    out.start()
     spec_ref, spec_above = t["spec"], t["spec_above"]
     obj_left = t["obj_left"]
     sign = alternating()
@@ -269,12 +265,12 @@
                 store_parts(y_parts, at(count + 1 + slot), turned)
     rows = dot(t["near_inverse"][...], y_parts[...])
     blocks = jnp.concatenate([side_by_side(rows[:, at(n)]) for n in range(2 * count + 2)], axis=0)
-    out = dot(wide_parts(blocks), t["out_right"][...])
+    image = dot(wide_parts(blocks), t["out_right"][...])
     flux = 0.0
     for half in range(2):
         base = half * (count + 1)
-        lefts = [out[at(base), :S]] + [out[at(base + q + 1), :S] for q in range(1, count)]
-        rights = [out[at(base + q + 1), S:] for q in range(count)]
+        lefts = [image[at(base), :S]] + [image[at(base + q + 1), :S] for q in range(1, count)]
+        rights = [image[at(base + q + 1), S:] for q in range(count)]
         first_ref[at(half)] = lefts[0]
         last_ref[at(half)] = rights[-1]
         middle = mid_bottom if half else mid_top
@@ -284,27 +280,26 @@
             middle[:, at(q - 1)] = block
             together = together + block
         flux = flux + jnp.sum(together)
-    for copy in outs[1:]:
-        copy.start()
     lane = lax.broadcasted_iota(jnp.int32, flux_ref.shape, 1)
     flux_ref[...] = jnp.where(lane < H, flux, t["total"][...])
-    for copy in outs:
-        copy.wait()
-
-
-def join_kernel(names, parts, *refs):
+    out.wait()
+
+
+def join_kernel(names, ready, *refs):
     total = len(names)
-    hbm, fluxes, refs = refs[:total], refs[total : total + parts], refs[total + parts :]
+    hbm, refs = refs[:total], refs[total:]
+    here, refs = dict(zip(ready, refs)), refs[len(ready) :]
+    fluxes = [here[n] for n in ready if n not in ("mid_top", "mid_bottom", "first", "last")]
     top_hbm, bottom_hbm, totals_ref = refs[:3]
     buffers, sems, top_ref, bottom_ref = refs[3 : 3 + total], refs[3 + total], refs[4 + total], refs[5 + total]
     t = Copies(names, hbm, buffers, sems)
     outs = []
     for half, out, place in ((0, top_ref, top_hbm), (1, bottom_ref, bottom_hbm)):
-        mid = t["mid_bottom" if half else "mid_top"]
+        mid = here["mid_bottom" if half else "mid_top"]
         width = mid.shape[1]
         out[:, S : S + width] = mid[...]
-        out[:, :S] = t["first"][at(half)] + t["from_left"][at(half)]
-        out[:, S + width :] = t["last"][at(half)] + t["from_right"][at(half)]
+        out[:, :S] = here["first"][at(half)] + t["from_left"][at(half)]
+        out[:, S + width :] = here["last"][at(half)] + t["from_right"][at(half)]
         outs.append(pltpu.make_async_copy(out, place, sems.at[total + half]))
         outs[-1].start()
     flux = sum([f[...] for f in fluxes[1:]], fluxes[0][...])
@@ -316,14 +311,20 @@
 def gradient_kernel(names, *refs):
     total = len(names)
     hbm, flux_ref, refs = refs[:total], refs[total], refs[total + 1 :]
-    residual_hbm, top_hbm, bottom_hbm = refs[:3]
-    buffers, sems, (residual_ref, out_top, out_bottom) = refs[3 : 3 + total], refs[3 + total], refs[4 + total : 7 + total]
-    r_ref, r_parts, g_parts = refs[7 + total :]
+    residual_hbm, top_hbm, bottom_hbm, first_hbm, rest_hbm = refs[:5]
+    buffers, sems, (residual_ref, out_top, out_bottom) = refs[5 : 5 + total], refs[5 + total], refs[6 + total : 9 + total]
+    r_ref, r_parts, g_parts = refs[9 + total :]
     t = Copies(names, picked(names, hbm), buffers, sems)
     sent = [
         pltpu.make_async_copy(source, out, sems.at[total + n])
         for n, (source, out) in enumerate(
-            zip((residual_ref, out_top, out_bottom), (residual_hbm, top_hbm, bottom_hbm))
+            (
+                (residual_ref, residual_hbm),
+                (out_bottom, bottom_hbm),
+                (out_top, top_hbm),
+                (out_top.at[:, pl.ds(0, S)], first_hbm),
+                (out_top.at[:, pl.ds(S, rest_hbm.shape[1])], rest_hbm),
+            )
         )
     ]
     row_edge, column_edge = edges()
@@ -499,9 +500,8 @@
         functools.partial(model_kernel, tuple(named), tuple(ready)),
         named,
         ready,
-        [(pltpu.HBM, o) for o in outs] + [(pltpu.VMEM, f32(8, S))],
-        like(named) + [pltpu.SemaphoreType.DMA((len(named) + len(outs),))]
-        + [pltpu.VMEM(o.shape, F32) for o in outs]
+        [(pltpu.HBM, outs[0])] + [(pltpu.VMEM, o) for o in outs[1:] + [f32(8, S)]],
+        like(named) + [pltpu.SemaphoreType.DMA((len(named) + 1,)), pltpu.VMEM(outs[0].shape, F32)]
         + [pltpu.VMEM((2 * width, S), F32), pltpu.VMEM((6 * S, 2 * width + 2 * S), BF16),
            pltpu.VMEM((6 * L, 2 * width + 2 * S), BF16)],
         36,
@@ -514,13 +514,13 @@
     from_right = ring(first, ("sx",), (-1,))
     from_left = ring(last, ("sx",), (1,))
     fluxes = [flux] + [mirrored(flux, "sy", k) for k in range(1, runs())]
-    named = {"mid_top": mid_top, "mid_bottom": mid_bottom, "first": first, "from_left": from_left,
-             "last": last, "from_right": from_right}
+    named = {"from_left": from_left, "from_right": from_right}
+    ready = {"mid_top": mid_top, "mid_bottom": mid_bottom, "first": first, "last": last} | dict(enumerate(fluxes))
     outs = [f32(S, width + S)] * 2
     top, bottom, flux = call(
-        functools.partial(join_kernel, tuple(named), len(fluxes)),
+        functools.partial(join_kernel, tuple(named), tuple(ready)),
         named,
-        dict(enumerate(fluxes)),
+        ready,
         [(pltpu.HBM, o) for o in outs]
         + [(pltpu.VMEM, f32(lax.axis_size("sy") // runs() * lax.axis_size("sx"), 8, S))],
         like(named) + [pltpu.SemaphoreType.DMA((len(named) + len(outs),))] + [pltpu.VMEM(o.shape, F32) for o in outs],
@@ -538,14 +538,14 @@
              "res_right": t["res_right"], "near_left": t["near_left"], "spec": spec, "spec_above": spec_above, "more": more,
              "grad_left": t["grad_left"], "grad_right": t["grad_right"],
              "windows": t["windows"], "plain": t["windows"][0]}
-    outs = [f32(S, width), f32(H, width), f32(H, width)]
-    residual, g_top, g_bottom = call(
+    outs = [f32(S, width), f32(H, width), f32(H, width), f32(H, S), f32(H, width - S)]
+    residual, g_top, g_bottom, g_first, g_rest = call(
         functools.partial(gradient_kernel, tuple(named)),
         named,
         {"flux": flux},
         [(pltpu.HBM, o) for o in outs],
         like(named) + [pltpu.SemaphoreType.DMA((len(named) + len(outs),))]
-        + [pltpu.VMEM(o.shape, F32) for o in outs]
+        + [pltpu.VMEM(o.shape, F32) for o in outs[:3]]
         + [pltpu.VMEM((L, width + S), F32), pltpu.VMEM((6 * S, 2 * width + 2 * S), BF16),
            pltpu.VMEM((12 * L, 2 * width), BF16)],
         44,
@@ -553,11 +553,18 @@
         ("above", "below", "obs_above", "obs_diagonal", "obs_left"),
     )
     bottom_other = mirrored(g_bottom, "fr", 1)
-    top_other = ring(g_top, ("sy", "fr"), (-1, 1))
     top_same = up(g_top)
-    total = jnp.concatenate([g_bottom + bottom_other, top_same + top_other], axis=0)
-    side = ring(total[:, :H], ("sx",), (-1,))
-    gradient = jnp.concatenate([total[:, H:], side], axis=1)
+    first_other = ring(g_first, ("sy", "fr"), (-1, 1))
+    rest_other = ring(g_rest, ("sy", "fr"), (-1, 1))
+    side = jnp.concatenate([g_bottom[:, :H] + bottom_other[:, :H], top_same[:, :H] + first_other[:, :H]], axis=0)
+    side = ring(side, ("sx",), (-1,))
+    upper = g_bottom[:, H:] + bottom_other[:, H:]
+    lower_first = top_same[:, H:S] + first_other[:, H:]
+    upper, lower_first, top_same, rest_other, side = lax.optimization_barrier(
+        (upper, lower_first, top_same, rest_other, side)
+    )
+    lower = jnp.concatenate([lower_first, top_same[:, S:] + rest_other], axis=1)
+    gradient = jnp.concatenate([jnp.concatenate([upper, lower], axis=0), side], axis=1)
     return gradient, residual[None]
 
 

time: 92.7 us -> 89.5 us (0.965)
  waiting for transfers between devices: 18.8 us -> 17 us
  starting transfers between devices: 31.9 us -> 30.4 us
    ppermute x4, waiting for transfers between devices: 4.85 us -> 2.9 us  [mirrored(): return lax.ppermute(value, axis, [(s, s ^ bits) for s in range(count)])]
    ppermute x13 -> x14, starting transfers between devices: 22.6 us -> 21.1 us  [ring(): return lax.ppermute(value, axes, pairs)]
    add x2 -> x4, other arithmetic: 0.95 us -> 1.89 us  [the longest x1 1.04 us: per_device(): upper = g_bottom[:, H:] + bottom_other[:, H:]]
    ppermute x13 -> x14, waiting for transfers between devices: 13.9 us -> 14.1 us  [ring(): return lax.ppermute(value, axes, pairs)]
  transfers between devices with their start and end apart: 17 -> 18, of which waited for: 8 -> 9; matrix products, arithmetic and copies ran while one was open for 1% -> 2% of each run, Pallas kernels for 14% -> 14%
where the time goes in v6:
time: 89.5 us; the launch traced here: 89.3 us
  starting transfers between devices  30.4 us (34%)
  Pallas kernels  23.4 us (26%)
  waiting for transfers between devices  17 us (19%)
  blocking collectives  15 us (17%)
  other arithmetic  2.73 us (3%)
    pallas_call x5, Pallas kernels, call(): pl.pallas_call(kernel, out_shape=[place(o.shape, o.dtype) for place, o in...  23.4 us
    ppermute x14, starting transfers between devices, ring(): return lax.ppermute(value, axes, pairs)  21.1 us
    all_to_all x1, blocking collectives, exchanged(): return lax.all_to_all(value, ('sy', 'sx'), 0, 0, axis_index_groups=groups)  15 us
    ppermute x14, waiting for transfers between devices, ring(): return lax.ppermute(value, axes, pairs)  14.1 us
    ppermute x4, starting transfers between devices, mirrored(): return lax.ppermute(value, axis, [(s, s ^ bits) for s in range(count)])  9.31 us
    ppermute x4, waiting for transfers between devices, mirrored(): return lax.ppermute(value, axis, [(s, s ^ bits) for s in range(count)])  2.9 us
  transfers between devices with their start and end apart: 18, of which 9 were waited for; matrix products, arithmetic and copies ran while one was open for 2% of the time, Pallas kernels for 14%

profile of v6, /device:TPU:1, one launch (start us, length us, event | category | flops | bytes accessed | tf_op | source)
XLA Modules:
  0.0 89.3 jit_solution(15869137004566641365)
XLA Ops:
  0.6 2.5 %collective-permute-start.3 = (f32[4,128,128]{2,1,0:T(8,128)}, f32[4,128,128]{2,1,0:T(8,128)S(1)}, u32[]{:S(2)}, u32[]{:S(2)}) collective-permute-start(f32[4,128,128]{2,1,0:T(8,128)} %bitcast.3), channel_id=1, source_target_pairs={{0,16},{16,32},{32,48},{48,64},{64,80},{80,96},{96,112},{112,128},... | collective-permute-start | bytes 786440 | tf_op jit(solution)/shard_map/ppermute | solution.py:430
  3.2 3.2 %shard_map.131 = (f32[64,512]{1,0:T(8,128)}, f32[320,128]{1,0:T(8,128)}, f32[192,128]{1,0:T(8,128)}, f32[128,128]{1,0:T(8,128)}, f32[512,512]{1,0:T(8,128)}, /*i...) custom-call(f32[4,128,128]{2,1,0:T(8,128)} %bitcast.4, ...), custom_call_target="tpu_custom_call" | custom-call | flops 504000000 | bytes 6111232 | tf_op jit(solution)/shard_map/pallas_call | solution.py:407
  6.4 2.1 %collective-permute-start = (f32[320,128]{1,0:T(8,128)}, f32[320,128]{1,0:T(8,128)S(1)}, u32[]{:S(2)}, u32[]{:S(2)}) collective-permute-start(f32[320,128]{1,0:T(8,128)} %get-tuple-element.43), channel_id=1, source_target_pairs={{0,2},{2,4},{4,6},{6,8},{8,10},{10,12},{12,14},{14,0},{1,3},{3,5},... | collective-permute-start | bytes 491528 | tf_op jit(solution)/shard_map/ppermute | solution.py:430
  8.5 1.6 %collective-permute-start.2 = (f32[64,512]{1,0:T(8,128)}, f32[64,512]{1,0:T(8,128)S(1)}, u32[]{:S(2)}, u32[]{:S(2)}) collective-permute-start(f32[64,512]{1,0:T(8,128)} %get-tuple-element.45), channel_id=1, source_target_pairs={{0,16},{16,32},{32,48},{48,64},{64,80},{80,96},{96,112},{112,128},... | collective-permute-start | bytes 393224 | tf_op jit(solution)/shard_map/ppermute | solution.py:430
  10.1 1.7 %collective-permute-start.1 = (f32[192,128]{1,0:T(8,128)}, f32[192,128]{1,0:T(8,128)S(1)}, u32[]{:S(2)}, u32[]{:S(2)}) collective-permute-start(f32[192,128]{1,0:T(8,128)} %get-tuple-element.44), channel_id=1, source_target_pairs={{0,18},{2,20},{4,22},{6,24},{8,26},{10,28},{12,30},{14,16},{16,34}... | collective-permute-start | bytes 294920 | tf_op jit(solution)/shard_map/ppermute | solution.py:430
  11.8 2.1 %collective-permute-done.3.psf_hbm = f32[4,128,128]{2,1,0:T(8,128)S(1)} collective-permute-done((f32[4,128,128]{2,1,0:T(8,128)}, f32[4,128,128]{2,1,0:T(8,128)S(1)}, u32[]{:S(2)}, u32[]{:S(2)}) %collective-permute-start.3) | collective-permute-done | bytes 262176 | tf_op jit(solution)/shard_map/ppermute | solution.py:430
  13.9 0.9 collective-permute-start.5
  14.8 1.9 %shard_map.132 = (f32[512,512]{1,0:T(8,128)}, f32[512,512]{1,0:T(8,128)S(1)}) custom-call(f32[4,128,128]{2,1,0:T(8,128)S(1)} %collective-permute-done.3.psf_hbm, bf16[384,256]{1,0:T(8,128)(2,1)S(1)} %get-tuple-element.46.right.refs_4_, bf16[512,768]{1,0:T(8,128)(2,1)S(1)} %get-tuple-element.47.left.refs_5_), custom_call_target="tpu_custom_call" | custom-call | flops 504000000 | bytes 262144 | tf_op jit(solution)/shard_map/pallas_call | solution.py:407
  16.7 3.7 %collective-permute-done.1.refs_1_ = f32[192,128]{1,0:T(8,128)S(1)} collective-permute-done((f32[192,128]{1,0:T(8,128)}, f32[192,128]{1,0:T(8,128)S(1)}, u32[]{:S(2)}, u32[]{:S(2)}) %collective-permute-start.1) | collective-permute-done | bytes 98336 | tf_op jit(solution)/shard_map/ppermute | solution.py:430
  20.4 7.8 %shard_map.133 = (f32[512,256]{1,0:T(8,128)}, f32[128,384]{1,0:T(8,128)S(1)}, f32[128,384]{1,0:T(8,128)S(1)}, f32[256,128]{1,0:T(8,128)S(1)}, f32[256,128]{1,0:T(8,128)S(1)}, /*index=5*/f32[8,128]{1,0:T(8,128)S(1)}) custom-call(f32[320,128]{1,0:T(8,128)S(1)} %collective-permute-done.refs_0_.refs_7_, f32[192,128]{1,0:T(8,128)S(1)} %collective-permute-done.1.refs_1_, ...), custom_call_target="tpu_custom_call" | custom-call | flops 3600000000 | bytes 655360 | tf_op jit(solution)/shard_map/pallas_call | solution.py:407
  28.2 1.3 %collective-permute-start.6 = (f32[256,128]{1,0:T(8,128)S(1)}, f32[256,128]{1,0:T(8,128)S(1)}, u32[]{:S(2)}, u32[]{:S(2)}) collective-permute-start(f32[256,128]{1,0:T(8,128)S(1)} %get-tuple-element.61.refs_5_), channel_id=1, source_target_pairs={{0,2},{2,4},{4,6},{6,8},{8,10},{10,12},{12,14},{14,0},{1,3},{3,5},... | collective-permute-start | bytes 393224 | tf_op jit(solution)/shard_map/ppermute | solution.py:430
  29.6 1.0 %collective-permute-start.7 = (f32[256,128]{1,0:T(8,128)S(1)}, f32[256,128]{1,0:T(8,128)S(1)}, u32[]{:S(2)}, u32[]{:S(2)}) collective-permute-start(f32[256,128]{1,0:T(8,128)S(1)} %get-tuple-element.62.refs_4_), channel_id=1, source_target_pairs={{0,14},{2,0},{4,2},{6,4},{8,6},{10,8},{12,10},{14,12},{1,15},{3,1}... | collective-permute-start | bytes 393224 | tf_op jit(solution)/shard_map/ppermute | solution.py:430
  30.6 3.5 %collective-permute-start.9 = (f32[8,128]{1,0:T(8,128)S(1)}, f32[8,128]{1,0:T(8,128)S(1)}, u32[]{:S(2)}, u32[]{:S(2)}) collective-permute-start(f32[8,128]{1,0:T(8,128)S(1)} %get-tuple-element.65.refs_6_), channel_id=1, source_target_pairs={{0,32},{16,48},{32,0},{48,16},{64,96},{80,112},{96,64},{112,80},{1... | collective-permute-start | bytes 12296 | tf_op jit(solution)/shard_map/ppermute | solution.py:435
  34.1 0.7 collective-permute-done.10.refs_9_
  34.8 0.6 collective-permute-done.9.refs_8_
  35.5 1.2 %shard_map.134 = (f32[128,640]{1,0:T(8,128)}, f32[128,640]{1,0:T(8,128)}, f32[32,8,128]{2,1,0:T(8,128)S(1)}) custom-call(f32[256,128]{1,0:T(8,128)S(1)} %collective-permute-done.6.refs_0_, f32[256,128]{1,0:T(8,128)S(1)} %collective-permute-done.7.refs_1_, f32[128,384]{1,0:T(8,128)S(1)} %get-tuple-element.63.refs_2_, ...), custom_call_target="tpu_custom_call" | custom-call | flops 1000000 | bytes 262144 | tf_op jit(solution)/shard_map/pallas_call | solution.py:407
  36.7 0.3 collective-permute-start.11
  37.0 5.4 %collective-permute-start.12 = (f32[128,640]{1,0:T(8,128)}, f32[128,640]{1,0:T(8,128)S(1)}, u32[]{:S(2)}, u32[]{:S(2)}) collective-permute-start(f32[128,640]{1,0:T(8,128)} %get-tuple-element.66.refs_0_), channel_id=1, source_target_pairs={{0,240},{16,0},{32,16},{48,32},{64,48},{80,64},{96,80},{112,96},{1... | collective-permute-start | bytes 983048 | tf_op jit(solution)/shard_map/ppermute | solution.py:430
  42.3 15.0 %all_to_all.5.refs_17_ = f32[32,8,128]{2,1,0:T(8,128)S(1)} all-to-all(f32[32,8,128]{2,1,0:T(8,128)S(1)} %get-tuple-element.73), channel_id=1, replica_groups={{0,2,4,6,8,10,12,14,64,66,68,70,72,74,76,78,128,130,132,134,136,138,140..., dimensions={0} | all-to-all | bytes 262144 | tf_op jit(solution)/shard_map/all_to_all | solution.py:447
  57.3 9.3 %shard_map.135 = (f32[128,512]{1,0:T(8,128)}, f32[64,512]{1,0:T(8,128)}, f32[64,512]{1,0:T(8,128)}, f32[64,128]{1,0:T(8,128)}, f32[64,384]{1,0:T(8,128)}) custom-call(f32[128,640]{1,0:T(8,128)} %get-tuple-element.66.refs_0_, f32[128,640]{1,0:T(8,128)S(1)} %collective-permute-done.11.refs_1_, f32[128,640]{1,0:T(8,128)} %get-tuple-element.67.refs_2_, ...), custom_call_target="tpu_custom_call" | custom-call | flops 3000000000 | bytes 9232384 | tf_op jit(solution)/shard_map/pallas_call | solution.py:407
  66.7 5.8 %collective-permute-start.13 = (f32[64,512]{1,0:T(8,128)}, f32[64,512]{1,0:T(8,128)S(1)}, u32[]{:S(2)}, u32[]{:S(2)}) collective-permute-start(f32[64,512]{1,0:T(8,128)} %get-tuple-element.74), channel_id=1, source_target_pairs={{0,1},{1,0},{2,3},{3,2},{4,5},{5,4},{6,7},{7,6},{8,9},{9,8},{10,11... | collective-permute-start | bytes 393224 | tf_op jit(solution)/shard_map/ppermute | solution.py:435
  72.4 0.2 collective-permute-start.14
  72.7 1.9 %collective-permute-start.16 = (f32[64,384]{1,0:T(8,128)}, f32[64,384]{1,0:T(8,128)S(1)}, u32[]{:S(2)}, u32[]{:S(2)}) collective-permute-start(f32[64,384]{1,0:T(8,128)} %get-tuple-element.77), channel_id=1, source_target_pairs={{0,241},{1,240},{16,1},{17,0},{32,17},{33,16},{48,33},{49,32},{64,... | collective-permute-start | bytes 294920 | tf_op jit(solution)/shard_map/ppermute | solution.py:430
  74.6 1.6 %collective-permute-done.13 = f32[64,512]{1,0:T(8,128)S(1)} collective-permute-done((f32[64,512]{1,0:T(8,128)}, f32[64,512]{1,0:T(8,128)S(1)}, u32[]{:S(2)}, u32[]{:S(2)}) %collective-permute-start.13) | collective-permute-done | bytes 131104 | tf_op jit(solution)/shard_map/ppermute | solution.py:435
  76.2 0.8 slice_add_fusion.3
  77.0 4.2 %collective-permute-done.15 = f32[64,128]{1,0:T(8,128)S(1)} collective-permute-done((f32[64,128]{1,0:T(8,128)}, f32[64,128]{1,0:T(8,128)S(1)}, u32[]{:S(2)}, u32[]{:S(2)}) %collective-permute-start.15) | collective-permute-done | bytes 32800 | tf_op jit(solution)/shard_map/ppermute | solution.py:430
  81.2 0.5 collective-permute-done.14
  81.8 2.0 %collective-permute-start.17 = (f32[128,64]{1,0:T(8,128)S(1)}, f32[128,64]{1,0:T(8,128)S(1)}, u32[]{:S(2)}, u32[]{:S(2)}) collective-permute-start(f32[128,64]{1,0:T(8,128)S(1)} %pad_maximum_fusion.1), channel_id=1, source_target_pairs={{0,14},{2,0},{4,2},{6,4},{8,6},{10,8},{12,10},{14,12},{1,15},{3,1}... | collective-permute-start | bytes 98312 | tf_op jit(solution)/shard_map/ppermute | solution.py:430
  83.8 1.0 %slice_add_fusion = f32[64,448]{1,0:T(8,128)S(1)} fusion(f32[64,512]{1,0:T(8,128)S(1)} %collective-permute-done.13, f32[64,512]{1,0:T(8,128)} %get-tuple-element.74), kind=kLoop, calls=%fused_computation.1 | loop fusion | flops 28672 | bytes 344064 | tf_op jit(solution)/shard_map/add | solution.py:561
  84.9 2.6 %collective-permute-done.16 = f32[64,384]{1,0:T(8,128)S(1)} collective-permute-done((f32[64,384]{1,0:T(8,128)}, f32[64,384]{1,0:T(8,128)S(1)}, u32[]{:S(2)}, u32[]{:S(2)}) %collective-permute-start.16) | collective-permute-done | bytes 98336 | tf_op jit(solution)/shard_map/ppermute | solution.py:430
  87.5 0.9 %collective-permute-done.17 = f32[128,64]{1,0:T(8,128)S(1)} collective-permute-done((f32[128,64]{1,0:T(8,128)S(1)}, f32[128,64]{1,0:T(8,128)S(1)}, u32[]{:S(2)}, u32[]{:S(2)}) %collective-permute-start.17) | collective-permute-done | bytes 32800 | tf_op jit(solution)/shard_map/ppermute | solution.py:430
  88.4 0.8 pad_maximum_fusion
  (20 shorter events, 0.1 us)
Async XLA Ops:
  0.6 11.2 %copy-start.1 = (f32[1,128,512]{2,1,0:T(8,128)S(1)}, f32[1,128,512]{2,1,0:T(8,128)}, u32[]{:S(2)}) copy-start(f32[1,128,512]{2,1,0:T(8,128)} %param.13) | copy-start | bytes 786436
  0.6 13.3 %collective-permute-start.3 = (f32[4,128,128]{2,1,0:T(8,128)}, f32[4,128,128]{2,1,0:T(8,128)S(1)}, u32[]{:S(2)}, u32[]{:S(2)}) collective-permute-start(f32[4,128,128]{2,1,0:T(8,128)} %bitcast.3), channel_id=1, source_target_pairs={{0,16},{16,32},{32,48},{48,64},{64,80},{80,96},{96,112},{112,128},... | collective-permute-start | bytes 786440 | tf_op jit(solution)/shard_map/ppermute | solution.py:430
  3.2 17.2 %copy-start = (f32[2,8,128]{2,1,0:T(8,128)S(1)}, f32[2,8,128]{2,1,0:T(8,128)}, u32[]{:S(2)}) copy-start(f32[2,8,128]{2,1,0:T(8,128)} %constant.30.refs_13_.refs_16_) | copy-start | bytes 24580
  6.4 14.0 %collective-permute-start = (f32[320,128]{1,0:T(8,128)}, f32[320,128]{1,0:T(8,128)S(1)}, u32[]{:S(2)}, u32[]{:S(2)}) collective-permute-start(f32[320,128]{1,0:T(8,128)} %get-tuple-element.43), channel_id=1, source_target_pairs={{0,2},{2,4},{4,6},{6,8},{8,10},{10,12},{12,14},{14,0},{1,3},{3,5},... | collective-permute-start | bytes 491528 | tf_op jit(solution)/shard_map/ppermute | solution.py:430
  8.5 11.9 %collective-permute-start.2 = (f32[64,512]{1,0:T(8,128)}, f32[64,512]{1,0:T(8,128)S(1)}, u32[]{:S(2)}, u32[]{:S(2)}) collective-permute-start(f32[64,512]{1,0:T(8,128)} %get-tuple-element.45), channel_id=1, source_target_pairs={{0,16},{16,32},{32,48},{48,64},{64,80},{80,96},{96,112},{112,128},... | collective-permute-start | bytes 393224 | tf_op jit(solution)/shard_map/ppermute | solution.py:430
  10.1 10.3 %collective-permute-start.1 = (f32[192,128]{1,0:T(8,128)}, f32[192,128]{1,0:T(8,128)S(1)}, u32[]{:S(2)}, u32[]{:S(2)}) collective-permute-start(f32[192,128]{1,0:T(8,128)} %get-tuple-element.44), channel_id=1, source_target_pairs={{0,18},{2,20},{4,22},{6,24},{8,26},{10,28},{12,30},{14,16},{16,34}... | collective-permute-start | bytes 294920 | tf_op jit(solution)/shard_map/ppermute | solution.py:430
  11.8 16.4 %collective-permute-start.4 = (f32[128,512]{1,0:T(8,128)S(1)}, f32[128,512]{1,0:T(8,128)S(1)}, u32[]{:S(2)}, u32[]{:S(2)}) collective-permute-start(f32[128,512]{1,0:T(8,128)S(1)} %bitcast.7), channel_id=1, source_target_pairs={{0,16},{16,32},{32,48},{48,64},{64,80},{80,96},{96,112},{112,128},... | collective-permute-start | bytes 786440 | tf_op jit(solution)/shard_map/ppermute | solution.py:430
  13.9 14.3 %collective-permute-start.5 = (f32[128,128]{1,0:T(8,128)}, f32[128,128]{1,0:T(8,128)S(1)}, u32[]{:S(2)}, u32[]{:S(2)}) collective-permute-start(f32[128,128]{1,0:T(8,128)} %get-tuple-element.60), channel_id=1, source_target_pairs={{0,18},{2,20},{4,22},{6,24},{8,26},{10,28},{12,30},{14,16},{16,34}... | collective-permute-start | bytes 196616 | tf_op jit(solution)/shard_map/ppermute | solution.py:430
  28.2 7.2 %collective-permute-start.6 = (f32[256,128]{1,0:T(8,128)S(1)}, f32[256,128]{1,0:T(8,128)S(1)}, u32[]{:S(2)}, u32[]{:S(2)}) collective-permute-start(f32[256,128]{1,0:T(8,128)S(1)} %get-tuple-element.61.refs_5_), channel_id=1, source_target_pairs={{0,2},{2,4},{4,6},{6,8},{8,10},{10,12},{12,14},{14,0},{1,3},{3,5},... | collective-permute-start | bytes 393224 | tf_op jit(solution)/shard_map/ppermute | solution.py:430
  29.6 5.9 %collective-permute-start.7 = (f32[256,128]{1,0:T(8,128)S(1)}, f32[256,128]{1,0:T(8,128)S(1)}, u32[]{:S(2)}, u32[]{:S(2)}) collective-permute-start(f32[256,128]{1,0:T(8,128)S(1)} %get-tuple-element.62.refs_4_), channel_id=1, source_target_pairs={{0,14},{2,0},{4,2},{6,4},{8,6},{10,8},{12,10},{14,12},{1,15},{3,1}... | collective-permute-start | bytes 393224 | tf_op jit(solution)/shard_map/ppermute | solution.py:430
  30.6 4.3 %collective-permute-start.10 = (f32[8,128]{1,0:T(8,128)S(1)}, f32[8,128]{1,0:T(8,128)S(1)}, u32[]{:S(2)}, u32[]{:S(2)}) collective-permute-start(f32[8,128]{1,0:T(8,128)S(1)} %get-tuple-element.65.refs_6_), channel_id=1, source_target_pairs={{0,48},{16,32},{32,16},{48,0},{64,112},{80,96},{96,80},{112,64},{1... | collective-permute-start | bytes 12296 | tf_op jit(solution)/shard_map/ppermute | solution.py:435
  30.6 4.3 %collective-permute-start.8 = (f32[8,128]{1,0:T(8,128)S(1)}, f32[8,128]{1,0:T(8,128)S(1)}, u32[]{:S(2)}, u32[]{:S(2)}) collective-permute-start(f32[8,128]{1,0:T(8,128)S(1)} %get-tuple-element.65.refs_6_), channel_id=1, source_target_pairs={{0,16},{16,0},{32,48},{48,32},{64,80},{80,64},{96,112},{112,96},{1... | collective-permute-start | bytes 12296 | tf_op jit(solution)/shard_map/ppermute | solution.py:435
  30.6 4.9 %collective-permute-start.9 = (f32[8,128]{1,0:T(8,128)S(1)}, f32[8,128]{1,0:T(8,128)S(1)}, u32[]{:S(2)}, u32[]{:S(2)}) collective-permute-start(f32[8,128]{1,0:T(8,128)S(1)} %get-tuple-element.65.refs_6_), channel_id=1, source_target_pairs={{0,32},{16,48},{32,0},{48,16},{64,96},{80,112},{96,64},{112,80},{1... | collective-permute-start | bytes 12296 | tf_op jit(solution)/shard_map/ppermute | solution.py:435
  36.7 20.6 %collective-permute-start.11 = (f32[128,640]{1,0:T(8,128)}, f32[128,640]{1,0:T(8,128)S(1)}, u32[]{:S(2)}, u32[]{:S(2)}) collective-permute-start(f32[128,640]{1,0:T(8,128)} %get-tuple-element.67.refs_2_), channel_id=1, source_target_pairs={{0,16},{16,32},{32,48},{48,64},{64,80},{80,96},{96,112},{112,128},... | collective-permute-start | bytes 983048 | tf_op jit(solution)/shard_map/ppermute | solution.py:430
  37.0 20.3 %collective-permute-start.12 = (f32[128,640]{1,0:T(8,128)}, f32[128,640]{1,0:T(8,128)S(1)}, u32[]{:S(2)}, u32[]{:S(2)}) collective-permute-start(f32[128,640]{1,0:T(8,128)} %get-tuple-element.66.refs_0_), channel_id=1, source_target_pairs={{0,240},{16,0},{32,16},{48,32},{64,48},{80,64},{96,80},{112,96},{1... | collective-permute-start | bytes 983048 | tf_op jit(solution)/shard_map/ppermute | solution.py:430
  66.7 9.5 %collective-permute-start.13 = (f32[64,512]{1,0:T(8,128)}, f32[64,512]{1,0:T(8,128)S(1)}, u32[]{:S(2)}, u32[]{:S(2)}) collective-permute-start(f32[64,512]{1,0:T(8,128)} %get-tuple-element.74), channel_id=1, source_target_pairs={{0,1},{1,0},{2,3},{3,2},{4,5},{5,4},{6,7},{7,6},{8,9},{9,8},{10,11... | collective-permute-start | bytes 393224 | tf_op jit(solution)/shard_map/ppermute | solution.py:435
  72.4 9.2 %collective-permute-start.14 = (f32[64,512]{1,0:T(8,128)}, f32[64,512]{1,0:T(8,128)S(1)}, u32[]{:S(2)}, u32[]{:S(2)}) collective-permute-start(f32[64,512]{1,0:T(8,128)} %get-tuple-element.75), channel_id=1, source_target_pairs={{0,240},{16,0},{32,16},{48,32},{64,48},{80,64},{96,80},{112,96},{1... | collective-permute-start | bytes 393224 | tf_op jit(solution)/shard_map/ppermute | solution.py:430
  72.7 8.5 %collective-permute-start.15 = (f32[64,128]{1,0:T(8,128)}, f32[64,128]{1,0:T(8,128)S(1)}, u32[]{:S(2)}, u32[]{:S(2)}) collective-permute-start(f32[64,128]{1,0:T(8,128)} %get-tuple-element.76), channel_id=1, source_target_pairs={{0,241},{1,240},{16,1},{17,0},{32,17},{33,16},{48,33},{49,32},{64,... | collective-permute-start | bytes 98312 | tf_op jit(solution)/shard_map/ppermute | solution.py:430
  72.7 14.8 %collective-permute-start.16 = (f32[64,384]{1,0:T(8,128)}, f32[64,384]{1,0:T(8,128)S(1)}, u32[]{:S(2)}, u32[]{:S(2)}) collective-permute-start(f32[64,384]{1,0:T(8,128)} %get-tuple-element.77), channel_id=1, source_target_pairs={{0,241},{1,240},{16,1},{17,0},{32,17},{33,16},{48,33},{49,32},{64,... | collective-permute-start | bytes 294920 | tf_op jit(solution)/shard_map/ppermute | solution.py:430
  81.8 6.6 %collective-permute-start.17 = (f32[128,64]{1,0:T(8,128)S(1)}, f32[128,64]{1,0:T(8,128)S(1)}, u32[]{:S(2)}, u32[]{:S(2)}) collective-permute-start(f32[128,64]{1,0:T(8,128)S(1)} %pad_maximum_fusion.1), channel_id=1, source_target_pairs={{0,14},{2,0},{4,2},{6,4},{8,6},{10,8},{12,10},{14,12},{1,15},{3,1}... | collective-permute-start | bytes 98312 | tf_op jit(solution)/shard_map/ppermute | solution.py:430

commit v7 on v6

--- a/solution.py
+++ b/solution.py
@@ -155,23 +155,18 @@
 def psf_kernel(names, *refs):
     total = len(names)
     hbm, refs = refs[:total], refs[total:]
-    down_hbm, right_hbm, diagonal_hbm, frame_hbm, spec_hbm, spec_ref, total_ref, *buffers = refs[:-5]
+    down_ref, right_ref, diagonal_ref, frame_ref, spec_hbm, spec_ref, total_ref, *buffers = refs[:-5]
     psf, obj, frame, sems, parts = refs[-5:]
     t = Copies(names, picked(names, hbm), (psf, obj, frame) + tuple(buffers), sems)
     count, last = psf.shape[0], pl.ds(obj.shape[1] - S, S)
     psf, obj, frame = t["psf"], t["object"], t["frame"]
-    moves = [
-        (obj.at[pl.ds(H, H)], down_hbm),
-        (psf.at[count - 1], right_hbm.at[pl.ds(0, S)]),
-        (obj.at[pl.ds(0, H), last], right_hbm.at[pl.ds(S, H)]),
-        (frame.at[:, last], right_hbm.at[pl.ds(S + H, S)]),
-        (psf.at[count - 1], diagonal_hbm.at[pl.ds(0, S)]),
-        (obj.at[pl.ds(H, H), last], diagonal_hbm.at[pl.ds(S, H)]),
-        (frame.at[:, last], frame_hbm),
-    ]
-    moves = [pltpu.make_async_copy(*move, sems.at[total + 1 + n]) for n, move in enumerate(moves)]
-    for copy in moves:
-        copy.start()
+    down_ref[...] = obj[H:]
+    right_ref[:S] = psf[count - 1]
+    right_ref[S : S + H] = obj[:H, last]
+    right_ref[S + H :] = frame[:, last]
+    diagonal_ref[:S] = psf[count - 1]
+    diagonal_ref[S:] = obj[H:, last]
+    frame_ref[...] = frame[:, last]
     lanes = dot(wide_parts(jnp.concatenate([psf[j] for j in range(count)], axis=0)), t["near_right"][...])
     for j in range(count):
         store_parts(parts, at(j), stacked(lanes[at(j)]))
@@ -181,8 +176,7 @@
     total_ref[...] = jnp.full(total_ref.shape, jnp.sum(t["frame"][...]), F32)
     for name in names:
         t[name]
-    for copy in moves + [out]:
-        copy.wait()
+    out.wait()
 
 
 def above_kernel(psf_hbm, right, left, spec_hbm, spec_ref, psf, sems, parts):
@@ -311,22 +305,10 @@
 def gradient_kernel(names, *refs):
     total = len(names)
     hbm, flux_ref, refs = refs[:total], refs[total], refs[total + 1 :]
-    residual_hbm, top_hbm, bottom_hbm, first_hbm, rest_hbm = refs[:5]
-    buffers, sems, (residual_ref, out_top, out_bottom) = refs[5 : 5 + total], refs[5 + total], refs[6 + total : 9 + total]
-    r_ref, r_parts, g_parts = refs[9 + total :]
+    residual_hbm, out_top, out_bottom, first_ref, rest_ref = refs[:5]
+    buffers, sems, residual_ref, r_ref, r_parts, g_parts = refs[5 : 5 + total], *refs[5 + total :]
     t = Copies(names, picked(names, hbm), buffers, sems)
-    sent = [
-        pltpu.make_async_copy(source, out, sems.at[total + n])
-        for n, (source, out) in enumerate(
-            (
-                (residual_ref, residual_hbm),
-                (out_bottom, bottom_hbm),
-                (out_top, top_hbm),
-                (out_top.at[:, pl.ds(0, S)], first_hbm),
-                (out_top.at[:, pl.ds(S, rest_hbm.shape[1])], rest_hbm),
-            )
-        )
-    ]
+    sent = pltpu.make_async_copy(residual_ref, residual_hbm, sems.at[total])
     row_edge, column_edge = edges()
     alpha, beta = 1.0 - row_edge.astype(F32), 1.0 - column_edge.astype(F32)
     width = residual_ref.shape[1]
@@ -340,7 +322,7 @@
     r_ref[:S, :S] -= t["obs_diagonal"][...]
     r_ref[S:, :S] -= t["obs_left"][...]
     residual_ref[...] = r_ref[S:, S:]
-    sent[0].start()
+    sent.start()
     near, far = r_ref[:, :S], r_ref[:, S : 2 * S]
     blocks = [
         jnp.concatenate([beta * near, far], axis=1),
@@ -390,10 +372,9 @@
         grad = gain * (out[at(2 * q)] * windows[0, :1] + out[at(2 * q + 1)] * windows[1, :1])
         out_top[:, at(q)] = grad[:H]
         out_bottom[:, at(q)] = grad[H:]
-    for copy in sent[1:]:
-        copy.start()
-    for copy in sent:
-        copy.wait()
+    first_ref[...] = out_top[:, :S]
+    rest_ref[...] = out_top[:, S:]
+    sent.wait()
 
 
 def f32(*shape):
@@ -468,12 +449,11 @@
         functools.partial(psf_kernel, tuple(named)),
         named,
         {},
-        [(pltpu.HBM, f32(H, width)), (pltpu.HBM, f32(2 * S + H, S)), (pltpu.HBM, f32(S + H, S)),
-         (pltpu.HBM, f32(S, S)),
-         (pltpu.HBM, f32(2 * L, width)), (pltpu.VMEM, f32(2 * L, width)), (pltpu.VMEM, f32(8, S))]
+        [(pltpu.VMEM, f32(H, width)), (pltpu.VMEM, f32(2 * S + H, S)), (pltpu.VMEM, f32(S + H, S)),
+         (pltpu.VMEM, f32(S, S)), (pltpu.HBM, f32(2 * L, width)), (pltpu.VMEM, f32(2 * L, width)), (pltpu.VMEM, f32(8, S))]
         + [(pltpu.VMEM, x) for x in like(kept)],
         [pltpu.VMEM(psfs.shape, F32), pltpu.VMEM(object_field.shape, F32), pltpu.VMEM(observed.shape, F32),
-         pltpu.SemaphoreType.DMA((len(named) + 8,)), pltpu.VMEM((6 * S, width), BF16)],
+         pltpu.SemaphoreType.DMA((len(named) + 1,)), pltpu.VMEM((6 * S, width), BF16)],
         16,
         6 * 84 * 10**6,
     )
@@ -543,25 +523,24 @@
         functools.partial(gradient_kernel, tuple(named)),
         named,
         {"flux": flux},
-        [(pltpu.HBM, o) for o in outs],
-        like(named) + [pltpu.SemaphoreType.DMA((len(named) + len(outs),))]
-        + [pltpu.VMEM(o.shape, F32) for o in outs[:3]]
+        [(pltpu.HBM, outs[0])] + [(pltpu.VMEM, o) for o in outs[1:]],
+        like(named) + [pltpu.SemaphoreType.DMA((len(named) + 1,)), pltpu.VMEM(outs[0].shape, F32)]
         + [pltpu.VMEM((L, width + S), F32), pltpu.VMEM((6 * S, 2 * width + 2 * S), BF16),
            pltpu.VMEM((12 * L, 2 * width), BF16)],
         44,
         6 * 500 * 10**6,
         ("above", "below", "obs_above", "obs_diagonal", "obs_left"),
     )
+    top_same = up(g_top)
     bottom_other = mirrored(g_bottom, "fr", 1)
-    top_same = up(g_top)
     first_other = ring(g_first, ("sy", "fr"), (-1, 1))
     rest_other = ring(g_rest, ("sy", "fr"), (-1, 1))
     side = jnp.concatenate([g_bottom[:, :H] + bottom_other[:, :H], top_same[:, :H] + first_other[:, :H]], axis=0)
     side = ring(side, ("sx",), (-1,))
     upper = g_bottom[:, H:] + bottom_other[:, H:]
     lower_first = top_same[:, H:S] + first_other[:, H:]
-    upper, lower_first, top_same, rest_other, side = lax.optimization_barrier(
-        (upper, lower_first, top_same, rest_other, side)
+    top_same, upper, lower_first, rest_other, side = lax.optimization_barrier(
+        (top_same, upper, lower_first, rest_other, side)
     )
     lower = jnp.concatenate([lower_first, top_same[:, S:] + rest_other], axis=1)
     gradient = jnp.concatenate([jnp.concatenate([upper, lower], axis=0), side], axis=1)

time: 89.5 us -> 89.2 us (level)
  waiting for transfers between devices: 17 us -> 19.7 us
  other arithmetic: 2.73 us -> 1.07 us
    ppermute x14, waiting for transfers between devices: 14.1 us -> 17.3 us  [ring(): return lax.ppermute(value, axes, pairs)]
    add x1, other arithmetic: 1.04 us -> 0.14 us  [per_device(): upper = g_bottom[:, H:] + bottom_other[:, H:]]
  transfers between devices with their start and end apart: 18 -> 18, of which waited for: 9 -> 9; matrix products, arithmetic and copies ran while one was open for 2% -> 0% of each run, Pallas kernels for 14% -> 14%
where the time goes in v7:
time: 89.2 us; the launch traced here: 89 us
  starting transfers between devices  29.9 us (34%)
  Pallas kernels  22.6 us (25%)
  waiting for transfers between devices  19.7 us (22%)
  blocking collectives  15 us (17%)
  other arithmetic  1.07 us (1%)
    pallas_call x5, Pallas kernels, call(): pl.pallas_call(kernel, out_shape=[place(o.shape, o.dtype) for place, o in...  22.6 us
    ppermute x14, starting transfers between devices, ring(): return lax.ppermute(value, axes, pairs)  20.9 us
    ppermute x14, waiting for transfers between devices, ring(): return lax.ppermute(value, axes, pairs)  17.3 us
    all_to_all x1, blocking collectives, exchanged(): return lax.all_to_all(value, ('sy', 'sx'), 0, 0, axis_index_groups=groups)  15 us
    ppermute x4, starting transfers between devices, mirrored(): return lax.ppermute(value, axis, [(s, s ^ bits) for s in range(count)])  8.97 us
    ppermute x4, waiting for transfers between devices, mirrored(): return lax.ppermute(value, axis, [(s, s ^ bits) for s in range(count)])  2.41 us
  transfers between devices with their start and end apart: 18, of which 9 were waited for; matrix products, arithmetic and copies ran while one was open for 0% of the time, Pallas kernels for 14%

profile of v7, /device:TPU:1, one launch (start us, length us, event | category | flops | bytes accessed | tf_op | source)
XLA Modules:
  0.0 89.0 jit_solution(12660357185642205975)
XLA Ops:
  0.6 2.5 %collective-permute-start.3 = (f32[4,128,128]{2,1,0:T(8,128)}, f32[4,128,128]{2,1,0:T(8,128)S(1)}, u32[]{:S(2)}, u32[]{:S(2)}) collective-permute-start(f32[4,128,128]{2,1,0:T(8,128)} %bitcast.3), channel_id=1, source_target_pairs={{0,16},{16,32},{32,48},{48,64},{64,80},{80,96},{96,112},{112,128},... | collective-permute-start | bytes 786440 | tf_op jit(solution)/shard_map/ppermute | solution.py:411
  3.2 3.1 %shard_map.131 = (f32[64,512]{1,0:T(8,128)S(1)}, f32[320,128]{1,0:T(8,128)S(1)}, f32[192,128]{1,0:T(8,128)S(1)}, f32[128,128]{1,0:T(8,128)S(1)}, f32[512,512]{1,...) custom-call(f32[4,128,128]{2,1,0:T(8,128)} %bitcast.4, ...), custom_call_target="tpu_custom_call" | custom-call | flops 504000000 | bytes 6111232 | tf_op jit(solution)/shard_map/pallas_call | solution.py:388
  6.3 2.1 %collective-permute-start = (f32[320,128]{1,0:T(8,128)S(1)}, f32[320,128]{1,0:T(8,128)S(1)}, u32[]{:S(2)}, u32[]{:S(2)}) collective-permute-start(f32[320,128]{1,0:T(8,128)S(1)} %get-tuple-element.43), channel_id=1, source_target_pairs={{0,2},{2,4},{4,6},{6,8},{8,10},{10,12},{12,14},{14,0},{1,3},{3,5},... | collective-permute-start | bytes 491528 | tf_op jit(solution)/shard_map/ppermute | solution.py:411
  8.4 1.6 %collective-permute-start.2 = (f32[64,512]{1,0:T(8,128)S(1)}, f32[64,512]{1,0:T(8,128)S(1)}, u32[]{:S(2)}, u32[]{:S(2)}) collective-permute-start(f32[64,512]{1,0:T(8,128)S(1)} %get-tuple-element.45), channel_id=1, source_target_pairs={{0,16},{16,32},{32,48},{48,64},{64,80},{80,96},{96,112},{112,128},... | collective-permute-start | bytes 393224 | tf_op jit(solution)/shard_map/ppermute | solution.py:411
  10.0 1.7 %collective-permute-start.1 = (f32[192,128]{1,0:T(8,128)S(1)}, f32[192,128]{1,0:T(8,128)S(1)}, u32[]{:S(2)}, u32[]{:S(2)}) collective-permute-start(f32[192,128]{1,0:T(8,128)S(1)} %get-tuple-element.44), channel_id=1, source_target_pairs={{0,18},{2,20},{4,22},{6,24},{8,26},{10,28},{12,30},{14,16},{16,34}... | collective-permute-start | bytes 294920 | tf_op jit(solution)/shard_map/ppermute | solution.py:411
  11.8 2.1 %collective-permute-done.3.psf_hbm = f32[4,128,128]{2,1,0:T(8,128)S(1)} collective-permute-done((f32[4,128,128]{2,1,0:T(8,128)}, f32[4,128,128]{2,1,0:T(8,128)S(1)}, u32[]{:S(2)}, u32[]{:S(2)}) %collective-permute-start.3) | collective-permute-done | bytes 262176 | tf_op jit(solution)/shard_map/ppermute | solution.py:411
  13.9 0.8 collective-permute-start.5
  14.7 1.9 %shard_map.132 = (f32[512,512]{1,0:T(8,128)}, f32[512,512]{1,0:T(8,128)S(1)}) custom-call(f32[4,128,128]{2,1,0:T(8,128)S(1)} %collective-permute-done.3.psf_hbm, bf16[384,256]{1,0:T(8,128)(2,1)S(1)} %get-tuple-element.46.right.refs_4_, bf16[512,768]{1,0:T(8,128)(2,1)S(1)} %get-tuple-element.47.left.refs_5_), custom_call_target="tpu_custom_call" | custom-call | flops 504000000 | bytes 262144 | tf_op jit(solution)/shard_map/pallas_call | solution.py:388
  16.6 4.1 %collective-permute-done.1.refs_1_ = f32[192,128]{1,0:T(8,128)S(1)} collective-permute-done((f32[192,128]{1,0:T(8,128)S(1)}, f32[192,128]{1,0:T(8,128)S(1)}, u32[]{:S(2)}, u32[]{:S(2)}) %collective-permute-start.1) | collective-permute-done | bytes 98336 | tf_op jit(solution)/shard_map/ppermute | solution.py:411
  20.7 7.8 %shard_map.133 = (f32[512,256]{1,0:T(8,128)}, f32[128,384]{1,0:T(8,128)S(1)}, f32[128,384]{1,0:T(8,128)S(1)}, f32[256,128]{1,0:T(8,128)S(1)}, f32[256,128]{1,0:T(8,128)S(1)}, /*index=5*/f32[8,128]{1,0:T(8,128)S(1)}) custom-call(f32[320,128]{1,0:T(8,128)S(1)} %collective-permute-done.refs_0_.refs_7_, f32[192,128]{1,0:T(8,128)S(1)} %collective-permute-done.1.refs_1_, ...), custom_call_target="tpu_custom_call" | custom-call | flops 3600000000 | bytes 655360 | tf_op jit(solution)/shard_map/pallas_call | solution.py:388
  28.5 0.8 collective-permute-start.6
  29.3 1.4 %collective-permute-start.7 = (f32[256,128]{1,0:T(8,128)S(1)}, f32[256,128]{1,0:T(8,128)S(1)}, u32[]{:S(2)}, u32[]{:S(2)}) collective-permute-start(f32[256,128]{1,0:T(8,128)S(1)} %get-tuple-element.62.refs_4_), channel_id=1, source_target_pairs={{0,14},{2,0},{4,2},{6,4},{8,6},{10,8},{12,10},{14,12},{1,15},{3,1}... | collective-permute-start | bytes 393224 | tf_op jit(solution)/shard_map/ppermute | solution.py:411
  30.7 3.5 %collective-permute-start.9 = (f32[8,128]{1,0:T(8,128)S(1)}, f32[8,128]{1,0:T(8,128)S(1)}, u32[]{:S(2)}, u32[]{:S(2)}) collective-permute-start(f32[8,128]{1,0:T(8,128)S(1)} %get-tuple-element.65.refs_6_), channel_id=1, source_target_pairs={{0,32},{16,48},{32,0},{48,16},{64,96},{80,112},{96,64},{112,80},{1... | collective-permute-start | bytes 12296 | tf_op jit(solution)/shard_map/ppermute | solution.py:416
  34.2 0.7 collective-permute-done.10.refs_9_
  34.9 0.6 collective-permute-done.9.refs_8_
  35.5 1.2 %shard_map.134 = (f32[128,640]{1,0:T(8,128)}, f32[128,640]{1,0:T(8,128)}, f32[32,8,128]{2,1,0:T(8,128)S(1)}) custom-call(f32[256,128]{1,0:T(8,128)S(1)} %collective-permute-done.6.refs_0_, f32[256,128]{1,0:T(8,128)S(1)} %collective-permute-done.7.refs_1_, f32[128,384]{1,0:T(8,128)S(1)} %get-tuple-element.63.refs_2_, ...), custom_call_target="tpu_custom_call" | custom-call | flops 1000000 | bytes 262144 | tf_op jit(solution)/shard_map/pallas_call | solution.py:388
  36.8 0.3 collective-permute-start.11
  37.1 5.4 %collective-permute-start.12 = (f32[128,640]{1,0:T(8,128)}, f32[128,640]{1,0:T(8,128)S(1)}, u32[]{:S(2)}, u32[]{:S(2)}) collective-permute-start(f32[128,640]{1,0:T(8,128)} %get-tuple-element.66.refs_0_), channel_id=1, source_target_pairs={{0,240},{16,0},{32,16},{48,32},{64,48},{80,64},{96,80},{112,96},{1... | collective-permute-start | bytes 983048 | tf_op jit(solution)/shard_map/ppermute | solution.py:411
  42.4 15.0 %all_to_all.5.refs_17_ = f32[32,8,128]{2,1,0:T(8,128)S(1)} all-to-all(f32[32,8,128]{2,1,0:T(8,128)S(1)} %get-tuple-element.73), channel_id=1, replica_groups={{0,2,4,6,8,10,12,14,64,66,68,70,72,74,76,78,128,130,132,134,136,138,140..., dimensions={0} | all-to-all | bytes 262144 | tf_op jit(solution)/shard_map/all_to_all | solution.py:428
  57.4 8.6 %shard_map.135 = (f32[128,512]{1,0:T(8,128)}, f32[64,512]{1,0:T(8,128)S(1)}, f32[64,512]{1,0:T(8,128)S(1)}, f32[64,128]{1,0:T(8,128)S(1)}, f32[64,384]{1,0:T(8,128)S(1)}) custom-call(f32[128,640]{1,0:T(8,128)} %get-tuple-element.66.refs_0_, f32[128,640]{1,0:T(8,128)S(1)} %collective-permute-done.11.refs_1_, f32[128,640]{1,0:T(8,128)} %get-tuple-element.67.refs_2_, ...), custom_call_target="tpu_custom_call" | custom-call | flops 3000000000 | bytes 9232384 | tf_op jit(solution)/shard_map/pallas_call | solution.py:388
  66.0 5.4 %collective-permute-start.14 = (f32[64,512]{1,0:T(8,128)S(1)}, f32[64,512]{1,0:T(8,128)S(1)}, u32[]{:S(2)}, u32[]{:S(2)}) collective-permute-start(f32[64,512]{1,0:T(8,128)S(1)} %get-tuple-element.75), channel_id=1, source_target_pairs={{0,1},{1,0},{2,3},{3,2},{4,5},{5,4},{6,7},{7,6},{8,9},{9,8},{10,11... | collective-permute-start | bytes 393224 | tf_op jit(solution)/shard_map/ppermute | solution.py:416
  71.4 0.2 collective-permute-start.13
  71.7 1.9 %collective-permute-start.16 = (f32[64,384]{1,0:T(8,128)S(1)}, f32[64,384]{1,0:T(8,128)S(1)}, u32[]{:S(2)}, u32[]{:S(2)}) collective-permute-start(f32[64,384]{1,0:T(8,128)S(1)} %get-tuple-element.77), channel_id=1, source_target_pairs={{0,241},{1,240},{16,1},{17,0},{32,17},{33,16},{48,33},{49,32},{64,... | collective-permute-start | bytes 294920 | tf_op jit(solution)/shard_map/ppermute | solution.py:411
  73.6 1.1 %collective-permute-done.14 = f32[64,512]{1,0:T(8,128)S(1)} collective-permute-done((f32[64,512]{1,0:T(8,128)S(1)}, f32[64,512]{1,0:T(8,128)S(1)}, u32[]{:S(2)}, u32[]{:S(2)}) %collective-permute-start.14) | collective-permute-done | bytes 131104 | tf_op jit(solution)/shard_map/ppermute | solution.py:416
  74.7 3.4 %collective-permute-done.15 = f32[64,128]{1,0:T(8,128)S(1)} collective-permute-done((f32[64,128]{1,0:T(8,128)S(1)}, f32[64,128]{1,0:T(8,128)S(1)}, u32[]{:S(2)}, u32[]{:S(2)}) %collective-permute-start.15) | collective-permute-done | bytes 32800 | tf_op jit(solution)/shard_map/ppermute | solution.py:411
  78.1 2.3 %collective-permute-done.13 = f32[64,512]{1,0:T(8,128)S(1)} collective-permute-done((f32[64,512]{1,0:T(8,128)S(1)}, f32[64,512]{1,0:T(8,128)S(1)}, u32[]{:S(2)}, u32[]{:S(2)}) %collective-permute-start.13) | collective-permute-done | bytes 131104 | tf_op jit(solution)/shard_map/ppermute | solution.py:411
  80.4 0.1 slice_add_fusion.2
  80.5 2.2 %collective-permute-start.17 = (f32[128,64]{1,0:T(8,128)S(1)}, f32[128,64]{1,0:T(8,128)S(1)}, u32[]{:S(2)}, u32[]{:S(2)}) collective-permute-start(f32[128,64]{1,0:T(8,128)S(1)} %pad_maximum_fusion.1), channel_id=1, source_target_pairs={{0,14},{2,0},{4,2},{6,4},{8,6},{10,8},{12,10},{14,12},{1,15},{3,1}... | collective-permute-start | bytes 98312 | tf_op jit(solution)/shard_map/ppermute | solution.py:411
  82.6 0.1 slice_add_fusion
  82.8 3.5 %collective-permute-done.16 = f32[64,384]{1,0:T(8,128)S(1)} collective-permute-done((f32[64,384]{1,0:T(8,128)S(1)}, f32[64,384]{1,0:T(8,128)S(1)}, u32[]{:S(2)}, u32[]{:S(2)}) %collective-permute-start.16) | collective-permute-done | bytes 98336 | tf_op jit(solution)/shard_map/ppermute | solution.py:411
  86.3 1.9 %collective-permute-done.17 = f32[128,64]{1,0:T(8,128)S(1)} collective-permute-done((f32[128,64]{1,0:T(8,128)S(1)}, f32[128,64]{1,0:T(8,128)S(1)}, u32[]{:S(2)}, u32[]{:S(2)}) %collective-permute-start.17) | collective-permute-done | bytes 32800 | tf_op jit(solution)/shard_map/ppermute | solution.py:411
  88.2 0.8 pad_maximum_fusion
  (20 shorter events, 0.1 us)
Async XLA Ops:
  0.6 11.1 %copy-start.1 = (f32[1,128,512]{2,1,0:T(8,128)S(1)}, f32[1,128,512]{2,1,0:T(8,128)}, u32[]{:S(2)}) copy-start(f32[1,128,512]{2,1,0:T(8,128)} %param.13) | copy-start | bytes 786436
  0.6 13.3 %collective-permute-start.3 = (f32[4,128,128]{2,1,0:T(8,128)}, f32[4,128,128]{2,1,0:T(8,128)S(1)}, u32[]{:S(2)}, u32[]{:S(2)}) collective-permute-start(f32[4,128,128]{2,1,0:T(8,128)} %bitcast.3), channel_id=1, source_target_pairs={{0,16},{16,32},{32,48},{48,64},{64,80},{80,96},{96,112},{112,128},... | collective-permute-start | bytes 786440 | tf_op jit(solution)/shard_map/ppermute | solution.py:411
  3.2 17.5 %copy-start = (f32[2,8,128]{2,1,0:T(8,128)S(1)}, f32[2,8,128]{2,1,0:T(8,128)}, u32[]{:S(2)}) copy-start(f32[2,8,128]{2,1,0:T(8,128)} %constant.30.refs_13_.refs_16_) | copy-start | bytes 24580
  6.3 14.4 %collective-permute-start = (f32[320,128]{1,0:T(8,128)S(1)}, f32[320,128]{1,0:T(8,128)S(1)}, u32[]{:S(2)}, u32[]{:S(2)}) collective-permute-start(f32[320,128]{1,0:T(8,128)S(1)} %get-tuple-element.43), channel_id=1, source_target_pairs={{0,2},{2,4},{4,6},{6,8},{8,10},{10,12},{12,14},{14,0},{1,3},{3,5},... | collective-permute-start | bytes 491528 | tf_op jit(solution)/shard_map/ppermute | solution.py:411
  8.4 12.3 %collective-permute-start.2 = (f32[64,512]{1,0:T(8,128)S(1)}, f32[64,512]{1,0:T(8,128)S(1)}, u32[]{:S(2)}, u32[]{:S(2)}) collective-permute-start(f32[64,512]{1,0:T(8,128)S(1)} %get-tuple-element.45), channel_id=1, source_target_pairs={{0,16},{16,32},{32,48},{48,64},{64,80},{80,96},{96,112},{112,128},... | collective-permute-start | bytes 393224 | tf_op jit(solution)/shard_map/ppermute | solution.py:411
  10.0 10.7 %collective-permute-start.1 = (f32[192,128]{1,0:T(8,128)S(1)}, f32[192,128]{1,0:T(8,128)S(1)}, u32[]{:S(2)}, u32[]{:S(2)}) collective-permute-start(f32[192,128]{1,0:T(8,128)S(1)} %get-tuple-element.44), channel_id=1, source_target_pairs={{0,18},{2,20},{4,22},{6,24},{8,26},{10,28},{12,30},{14,16},{16,34}... | collective-permute-start | bytes 294920 | tf_op jit(solution)/shard_map/ppermute | solution.py:411
  11.8 16.7 %collective-permute-start.4 = (f32[128,512]{1,0:T(8,128)S(1)}, f32[128,512]{1,0:T(8,128)S(1)}, u32[]{:S(2)}, u32[]{:S(2)}) collective-permute-start(f32[128,512]{1,0:T(8,128)S(1)} %bitcast.7), channel_id=1, source_target_pairs={{0,16},{16,32},{32,48},{48,64},{64,80},{80,96},{96,112},{112,128},... | collective-permute-start | bytes 786440 | tf_op jit(solution)/shard_map/ppermute | solution.py:411
  13.9 14.6 %collective-permute-start.5 = (f32[128,128]{1,0:T(8,128)S(1)}, f32[128,128]{1,0:T(8,128)S(1)}, u32[]{:S(2)}, u32[]{:S(2)}) collective-permute-start(f32[128,128]{1,0:T(8,128)S(1)} %get-tuple-element.60), channel_id=1, source_target_pairs={{0,18},{2,20},{4,22},{6,24},{8,26},{10,28},{12,30},{14,16},{16,34}... | collective-permute-start | bytes 196616 | tf_op jit(solution)/shard_map/ppermute | solution.py:411
  28.5 7.0 %collective-permute-start.6 = (f32[256,128]{1,0:T(8,128)S(1)}, f32[256,128]{1,0:T(8,128)S(1)}, u32[]{:S(2)}, u32[]{:S(2)}) collective-permute-start(f32[256,128]{1,0:T(8,128)S(1)} %get-tuple-element.61.refs_5_), channel_id=1, source_target_pairs={{0,2},{2,4},{4,6},{6,8},{8,10},{10,12},{12,14},{14,0},{1,3},{3,5},... | collective-permute-start | bytes 393224 | tf_op jit(solution)/shard_map/ppermute | solution.py:411
  29.3 6.3 %collective-permute-start.7 = (f32[256,128]{1,0:T(8,128)S(1)}, f32[256,128]{1,0:T(8,128)S(1)}, u32[]{:S(2)}, u32[]{:S(2)}) collective-permute-start(f32[256,128]{1,0:T(8,128)S(1)} %get-tuple-element.62.refs_4_), channel_id=1, source_target_pairs={{0,14},{2,0},{4,2},{6,4},{8,6},{10,8},{12,10},{14,12},{1,15},{3,1}... | collective-permute-start | bytes 393224 | tf_op jit(solution)/shard_map/ppermute | solution.py:411
  30.7 4.3 %collective-permute-start.10 = (f32[8,128]{1,0:T(8,128)S(1)}, f32[8,128]{1,0:T(8,128)S(1)}, u32[]{:S(2)}, u32[]{:S(2)}) collective-permute-start(f32[8,128]{1,0:T(8,128)S(1)} %get-tuple-element.65.refs_6_), channel_id=1, source_target_pairs={{0,48},{16,32},{32,16},{48,0},{64,112},{80,96},{96,80},{112,64},{1... | collective-permute-start | bytes 12296 | tf_op jit(solution)/shard_map/ppermute | solution.py:416
  30.7 4.3 %collective-permute-start.8 = (f32[8,128]{1,0:T(8,128)S(1)}, f32[8,128]{1,0:T(8,128)S(1)}, u32[]{:S(2)}, u32[]{:S(2)}) collective-permute-start(f32[8,128]{1,0:T(8,128)S(1)} %get-tuple-element.65.refs_6_), channel_id=1, source_target_pairs={{0,16},{16,0},{32,48},{48,32},{64,80},{80,64},{96,112},{112,96},{1... | collective-permute-start | bytes 12296 | tf_op jit(solution)/shard_map/ppermute | solution.py:416
  30.7 4.9 %collective-permute-start.9 = (f32[8,128]{1,0:T(8,128)S(1)}, f32[8,128]{1,0:T(8,128)S(1)}, u32[]{:S(2)}, u32[]{:S(2)}) collective-permute-start(f32[8,128]{1,0:T(8,128)S(1)} %get-tuple-element.65.refs_6_), channel_id=1, source_target_pairs={{0,32},{16,48},{32,0},{48,16},{64,96},{80,112},{96,64},{112,80},{1... | collective-permute-start | bytes 12296 | tf_op jit(solution)/shard_map/ppermute | solution.py:416
  36.8 20.6 %collective-permute-start.11 = (f32[128,640]{1,0:T(8,128)}, f32[128,640]{1,0:T(8,128)S(1)}, u32[]{:S(2)}, u32[]{:S(2)}) collective-permute-start(f32[128,640]{1,0:T(8,128)} %get-tuple-element.67.refs_2_), channel_id=1, source_target_pairs={{0,16},{16,32},{32,48},{48,64},{64,80},{80,96},{96,112},{112,128},... | collective-permute-start | bytes 983048 | tf_op jit(solution)/shard_map/ppermute | solution.py:411
  37.1 20.3 %collective-permute-start.12 = (f32[128,640]{1,0:T(8,128)}, f32[128,640]{1,0:T(8,128)S(1)}, u32[]{:S(2)}, u32[]{:S(2)}) collective-permute-start(f32[128,640]{1,0:T(8,128)} %get-tuple-element.66.refs_0_), channel_id=1, source_target_pairs={{0,240},{16,0},{32,16},{48,32},{64,48},{80,64},{96,80},{112,96},{1... | collective-permute-start | bytes 983048 | tf_op jit(solution)/shard_map/ppermute | solution.py:411
  66.0 8.7 %collective-permute-start.14 = (f32[64,512]{1,0:T(8,128)S(1)}, f32[64,512]{1,0:T(8,128)S(1)}, u32[]{:S(2)}, u32[]{:S(2)}) collective-permute-start(f32[64,512]{1,0:T(8,128)S(1)} %get-tuple-element.75), channel_id=1, source_target_pairs={{0,1},{1,0},{2,3},{3,2},{4,5},{5,4},{6,7},{7,6},{8,9},{9,8},{10,11... | collective-permute-start | bytes 393224 | tf_op jit(solution)/shard_map/ppermute | solution.py:416
  71.4 8.9 %collective-permute-start.13 = (f32[64,512]{1,0:T(8,128)S(1)}, f32[64,512]{1,0:T(8,128)S(1)}, u32[]{:S(2)}, u32[]{:S(2)}) collective-permute-start(f32[64,512]{1,0:T(8,128)S(1)} %get-tuple-element.74), channel_id=1, source_target_pairs={{0,240},{16,0},{32,16},{48,32},{64,48},{80,64},{96,80},{112,96},{1... | collective-permute-start | bytes 393224 | tf_op jit(solution)/shard_map/ppermute | solution.py:411
  71.7 6.4 %collective-permute-start.15 = (f32[64,128]{1,0:T(8,128)S(1)}, f32[64,128]{1,0:T(8,128)S(1)}, u32[]{:S(2)}, u32[]{:S(2)}) collective-permute-start(f32[64,128]{1,0:T(8,128)S(1)} %get-tuple-element.76), channel_id=1, source_target_pairs={{0,241},{1,240},{16,1},{17,0},{32,17},{33,16},{48,33},{49,32},{64,... | collective-permute-start | bytes 98312 | tf_op jit(solution)/shard_map/ppermute | solution.py:411
  71.7 14.6 %collective-permute-start.16 = (f32[64,384]{1,0:T(8,128)S(1)}, f32[64,384]{1,0:T(8,128)S(1)}, u32[]{:S(2)}, u32[]{:S(2)}) collective-permute-start(f32[64,384]{1,0:T(8,128)S(1)} %get-tuple-element.77), channel_id=1, source_target_pairs={{0,241},{1,240},{16,1},{17,0},{32,17},{33,16},{48,33},{49,32},{64,... | collective-permute-start | bytes 294920 | tf_op jit(solution)/shard_map/ppermute | solution.py:411
  80.5 7.7 %collective-permute-start.17 = (f32[128,64]{1,0:T(8,128)S(1)}, f32[128,64]{1,0:T(8,128)S(1)}, u32[]{:S(2)}, u32[]{:S(2)}) collective-permute-start(f32[128,64]{1,0:T(8,128)S(1)} %pad_maximum_fusion.1), channel_id=1, source_target_pairs={{0,14},{2,0},{4,2},{6,4},{8,6},{10,8},{12,10},{14,12},{1,15},{3,1}... | collective-permute-start | bytes 98312 | tf_op jit(solution)/shard_map/ppermute | solution.py:411

commit v8 on v7

--- a/solution.py
+++ b/solution.py
@@ -297,7 +297,7 @@
         outs.append(pltpu.make_async_copy(out, place, sems.at[total + half]))
         outs[-1].start()
     flux = sum([f[...] for f in fluxes[1:]], fluxes[0][...])
-    totals_ref[...] = jnp.broadcast_to(flux[None], totals_ref.shape)
+    totals_ref[...] = jnp.broadcast_to(flux[None, :1], totals_ref.shape)
     for copy in outs:
         copy.wait()
 
@@ -502,7 +502,7 @@
         named,
         ready,
         [(pltpu.HBM, o) for o in outs]
-        + [(pltpu.VMEM, f32(lax.axis_size("sy") // runs() * lax.axis_size("sx"), 8, S))],
+        + [(pltpu.VMEM, f32(lax.axis_size("sy") // runs() * lax.axis_size("sx"), 1, S))],
         like(named) + [pltpu.SemaphoreType.DMA((len(named) + len(outs),))] + [pltpu.VMEM(o.shape, F32) for o in outs],
         16,
         10**6,

time: 89.2 us -> 86.3 us (0.967)
  waiting for transfers between devices: 19.7 us -> 16.2 us
    ppermute x14, waiting for transfers between devices: 17.3 us -> 14.5 us  [ring(): return lax.ppermute(value, axes, pairs)]
  transfers between devices with their start and end apart: 18 -> 18, of which waited for: 9 -> 9; matrix products, arithmetic and copies ran while one was open for 0% -> 0% of each run, Pallas kernels for 14% -> 15%
where the time goes in v8:
time: 86.3 us; the launch traced here: 85.5 us
  starting transfers between devices  30.5 us (35%)
  Pallas kernels  22.6 us (26%)
  waiting for transfers between devices  16.2 us (19%)
  blocking collectives  14.3 us (17%)
  other arithmetic  1.07 us (1%)
    pallas_call x5, Pallas kernels, call(): pl.pallas_call(kernel, out_shape=[place(o.shape, o.dtype) for place, o in...  22.6 us
    ppermute x14, starting transfers between devices, ring(): return lax.ppermute(value, axes, pairs)  21.5 us
    ppermute x14, waiting for transfers between devices, ring(): return lax.ppermute(value, axes, pairs)  14.5 us
    all_to_all x1, blocking collectives, exchanged(): return lax.all_to_all(value, ('sy', 'sx'), 0, 0, axis_index_groups=groups)  14.3 us
    ppermute x4, starting transfers between devices, mirrored(): return lax.ppermute(value, axis, [(s, s ^ bits) for s in range(count)])  8.97 us
    ppermute x4, waiting for transfers between devices, mirrored(): return lax.ppermute(value, axis, [(s, s ^ bits) for s in range(count)])  1.73 us
  transfers between devices with their start and end apart: 18, of which 9 were waited for; matrix products, arithmetic and copies ran while one was open for 0% of the time, Pallas kernels for 15%

profile of v8, /device:TPU:1, one launch (start us, length us, event | category | flops | bytes accessed | tf_op | source)
XLA Modules:
  0.0 85.5 jit_solution(2281799341823085858)
XLA Ops:
  0.6 0.0 copy-start.1
  0.6 2.5 %collective-permute-start.3 = (f32[4,128,128]{2,1,0:T(8,128)}, f32[4,128,128]{2,1,0:T(8,128)S(1)}, u32[]{:S(2)}, u32[]{:S(2)}) collective-permute-start(f32[4,128,128]{2,1,0:T(8,128)} %bitcast.3), channel_id=1, source_target_pairs={{0,16},{16,32},{32,48},{48,64},{64,80},{80,96},{96,112},{112,128},... | collective-permute-start | bytes 786440 | tf_op jit(solution)/shard_map/ppermute | solution.py:411
  3.2 3.1 %shard_map.131 = (f32[64,512]{1,0:T(8,128)S(1)}, f32[320,128]{1,0:T(8,128)S(1)}, f32[192,128]{1,0:T(8,128)S(1)}, f32[128,128]{1,0:T(8,128)S(1)}, f32[512,512]{1,...) custom-call(f32[4,128,128]{2,1,0:T(8,128)} %bitcast.4, ...), custom_call_target="tpu_custom_call" | custom-call | flops 504000000 | bytes 6111232 | tf_op jit(solution)/shard_map/pallas_call | solution.py:388
  6.3 2.1 %collective-permute-start = (f32[320,128]{1,0:T(8,128)S(1)}, f32[320,128]{1,0:T(8,128)S(1)}, u32[]{:S(2)}, u32[]{:S(2)}) collective-permute-start(f32[320,128]{1,0:T(8,128)S(1)} %get-tuple-element.43), channel_id=1, source_target_pairs={{0,2},{2,4},{4,6},{6,8},{8,10},{10,12},{12,14},{14,0},{1,3},{3,5},... | collective-permute-start | bytes 491528 | tf_op jit(solution)/shard_map/ppermute | solution.py:411
  8.4 1.6 %collective-permute-start.2 = (f32[64,512]{1,0:T(8,128)S(1)}, f32[64,512]{1,0:T(8,128)S(1)}, u32[]{:S(2)}, u32[]{:S(2)}) collective-permute-start(f32[64,512]{1,0:T(8,128)S(1)} %get-tuple-element.45), channel_id=1, source_target_pairs={{0,16},{16,32},{32,48},{48,64},{64,80},{80,96},{96,112},{112,128},... | collective-permute-start | bytes 393224 | tf_op jit(solution)/shard_map/ppermute | solution.py:411
  10.0 1.7 %collective-permute-start.1 = (f32[192,128]{1,0:T(8,128)S(1)}, f32[192,128]{1,0:T(8,128)S(1)}, u32[]{:S(2)}, u32[]{:S(2)}) collective-permute-start(f32[192,128]{1,0:T(8,128)S(1)} %get-tuple-element.44), channel_id=1, source_target_pairs={{0,18},{2,20},{4,22},{6,24},{8,26},{10,28},{12,30},{14,16},{16,34}... | collective-permute-start | bytes 294920 | tf_op jit(solution)/shard_map/ppermute | solution.py:411
  11.8 2.1 %collective-permute-done.3.psf_hbm = f32[4,128,128]{2,1,0:T(8,128)S(1)} collective-permute-done((f32[4,128,128]{2,1,0:T(8,128)}, f32[4,128,128]{2,1,0:T(8,128)S(1)}, u32[]{:S(2)}, u32[]{:S(2)}) %collective-permute-start.3) | collective-permute-done | bytes 262176 | tf_op jit(solution)/shard_map/ppermute | solution.py:411
  13.9 0.8 collective-permute-start.5
  14.7 1.9 %shard_map.132 = (f32[512,512]{1,0:T(8,128)}, f32[512,512]{1,0:T(8,128)S(1)}) custom-call(f32[4,128,128]{2,1,0:T(8,128)S(1)} %collective-permute-done.3.psf_hbm, bf16[384,256]{1,0:T(8,128)(2,1)S(1)} %get-tuple-element.46.right.refs_4_, bf16[512,768]{1,0:T(8,128)(2,1)S(1)} %get-tuple-element.47.left.refs_5_), custom_call_target="tpu_custom_call" | custom-call | flops 504000000 | bytes 262144 | tf_op jit(solution)/shard_map/pallas_call | solution.py:388
  16.6 4.1 %collective-permute-done.1.refs_1_ = f32[192,128]{1,0:T(8,128)S(1)} collective-permute-done((f32[192,128]{1,0:T(8,128)S(1)}, f32[192,128]{1,0:T(8,128)S(1)}, u32[]{:S(2)}, u32[]{:S(2)}) %collective-permute-start.1) | collective-permute-done | bytes 98336 | tf_op jit(solution)/shard_map/ppermute | solution.py:411
  20.7 7.8 %shard_map.133 = (f32[512,256]{1,0:T(8,128)}, f32[128,384]{1,0:T(8,128)S(1)}, f32[128,384]{1,0:T(8,128)S(1)}, f32[256,128]{1,0:T(8,128)S(1)}, f32[256,128]{1,0:T(8,128)S(1)}, /*index=5*/f32[8,128]{1,0:T(8,128)S(1)}) custom-call(f32[320,128]{1,0:T(8,128)S(1)} %collective-permute-done.refs_0_.refs_7_, f32[192,128]{1,0:T(8,128)S(1)} %collective-permute-done.1.refs_1_, ...), custom_call_target="tpu_custom_call" | custom-call | flops 3600000000 | bytes 655360 | tf_op jit(solution)/shard_map/pallas_call | solution.py:388
  28.5 0.8 collective-permute-start.6
  29.3 1.4 %collective-permute-start.7 = (f32[256,128]{1,0:T(8,128)S(1)}, f32[256,128]{1,0:T(8,128)S(1)}, u32[]{:S(2)}, u32[]{:S(2)}) collective-permute-start(f32[256,128]{1,0:T(8,128)S(1)} %get-tuple-element.62.refs_4_), channel_id=1, source_target_pairs={{0,14},{2,0},{4,2},{6,4},{8,6},{10,8},{12,10},{14,12},{1,15},{3,1}... | collective-permute-start | bytes 393224 | tf_op jit(solution)/shard_map/ppermute | solution.py:411
  30.7 3.5 %collective-permute-start.9 = (f32[8,128]{1,0:T(8,128)S(1)}, f32[8,128]{1,0:T(8,128)S(1)}, u32[]{:S(2)}, u32[]{:S(2)}) collective-permute-start(f32[8,128]{1,0:T(8,128)S(1)} %get-tuple-element.65.refs_6_), channel_id=1, source_target_pairs={{0,32},{16,48},{32,0},{48,16},{64,96},{80,112},{96,64},{112,80},{1... | collective-permute-start | bytes 12296 | tf_op jit(solution)/shard_map/ppermute | solution.py:416
  34.2 0.7 collective-permute-done.10.refs_9_
  34.9 0.6 collective-permute-done.9.refs_8_
  35.5 1.2 %shard_map.134 = (f32[128,640]{1,0:T(8,128)}, f32[128,640]{1,0:T(8,128)}, f32[32,1,128]{2,1,0:T(1,128)S(1)}) custom-call(f32[256,128]{1,0:T(8,128)S(1)} %collective-permute-done.6.refs_0_, f32[256,128]{1,0:T(8,128)S(1)} %collective-permute-done.7.refs_1_, f32[128,384]{1,0:T(8,128)S(1)} %get-tuple-element.63.refs_2_, ...), custom_call_target="tpu_custom_call" | custom-call | flops 1000000 | bytes 262144 | tf_op jit(solution)/shard_map/pallas_call | solution.py:388
  36.8 0.3 collective-permute-start.11
  37.1 5.4 %collective-permute-start.12 = (f32[128,640]{1,0:T(8,128)}, f32[128,640]{1,0:T(8,128)S(1)}, u32[]{:S(2)}, u32[]{:S(2)}) collective-permute-start(f32[128,640]{1,0:T(8,128)} %get-tuple-element.66.refs_0_), channel_id=1, source_target_pairs={{0,240},{16,0},{32,16},{48,32},{64,48},{80,64},{96,80},{112,96},{1... | collective-permute-start | bytes 983048 | tf_op jit(solution)/shard_map/ppermute | solution.py:411
  42.4 14.3 %all_to_all.5.refs_17_ = f32[32,1,128]{2,1,0:T(1,128)S(1)} all-to-all(f32[32,1,128]{2,1,0:T(1,128)S(1)} %get-tuple-element.73), channel_id=1, replica_groups={{0,2,4,6,8,10,12,14,64,66,68,70,72,74,76,78,128,130,132,134,136,138,140..., dimensions={0} | all-to-all | bytes 32768 | tf_op jit(solution)/shard_map/all_to_all | solution.py:428
  56.7 8.6 %shard_map.135 = (f32[128,512]{1,0:T(8,128)}, f32[64,512]{1,0:T(8,128)S(1)}, f32[64,512]{1,0:T(8,128)S(1)}, f32[64,128]{1,0:T(8,128)S(1)}, f32[64,384]{1,0:T(8,128)S(1)}) custom-call(f32[128,640]{1,0:T(8,128)} %get-tuple-element.66.refs_0_, f32[128,640]{1,0:T(8,128)S(1)} %collective-permute-done.11.refs_1_, f32[128,640]{1,0:T(8,128)} %get-tuple-element.67.refs_2_, ...), custom_call_target="tpu_custom_call" | custom-call | flops 3000000000 | bytes 9232384 | tf_op jit(solution)/shard_map/pallas_call | solution.py:388
  65.3 5.4 %collective-permute-start.14 = (f32[64,512]{1,0:T(8,128)S(1)}, f32[64,512]{1,0:T(8,128)S(1)}, u32[]{:S(2)}, u32[]{:S(2)}) collective-permute-start(f32[64,512]{1,0:T(8,128)S(1)} %get-tuple-element.75), channel_id=1, source_target_pairs={{0,1},{1,0},{2,3},{3,2},{4,5},{5,4},{6,7},{7,6},{8,9},{9,8},{10,11... | collective-permute-start | bytes 393224 | tf_op jit(solution)/shard_map/ppermute | solution.py:416
  70.8 2.6 %collective-permute-start.16 = (f32[64,384]{1,0:T(8,128)S(1)}, f32[64,384]{1,0:T(8,128)S(1)}, u32[]{:S(2)}, u32[]{:S(2)}) collective-permute-start(f32[64,384]{1,0:T(8,128)S(1)} %get-tuple-element.77), channel_id=1, source_target_pairs={{0,241},{1,240},{16,1},{17,0},{32,17},{33,16},{48,33},{49,32},{64,... | collective-permute-start | bytes 294920 | tf_op jit(solution)/shard_map/ppermute | solution.py:411
  73.3 0.4 collective-permute-done.14
  73.7 6.1 %collective-permute-done.15 = f32[64,128]{1,0:T(8,128)S(1)} collective-permute-done((f32[64,128]{1,0:T(8,128)S(1)}, f32[64,128]{1,0:T(8,128)S(1)}, u32[]{:S(2)}, u32[]{:S(2)}) %collective-permute-start.15) | collective-permute-done | bytes 32800 | tf_op jit(solution)/shard_map/ppermute | solution.py:411
  79.8 0.7 collective-permute-done.13
  80.5 0.1 slice_add_fusion.2
  80.6 2.4 %collective-permute-start.17 = (f32[128,64]{1,0:T(8,128)S(1)}, f32[128,64]{1,0:T(8,128)S(1)}, u32[]{:S(2)}, u32[]{:S(2)}) collective-permute-start(f32[128,64]{1,0:T(8,128)S(1)} %pad_maximum_fusion.1), channel_id=1, source_target_pairs={{0,14},{2,0},{4,2},{6,4},{8,6},{10,8},{12,10},{14,12},{1,15},{3,1}... | collective-permute-start | bytes 98312 | tf_op jit(solution)/shard_map/ppermute | solution.py:411
  83.0 0.1 slice_add_fusion
  83.1 1.4 %collective-permute-done.16 = f32[64,384]{1,0:T(8,128)S(1)} collective-permute-done((f32[64,384]{1,0:T(8,128)S(1)}, f32[64,384]{1,0:T(8,128)S(1)}, u32[]{:S(2)}, u32[]{:S(2)}) %collective-permute-start.16) | collective-permute-done | bytes 98336 | tf_op jit(solution)/shard_map/ppermute | solution.py:411
  84.5 0.1 collective-permute-done.17
  84.6 0.8 pad_maximum_fusion
  (20 shorter events, 0.1 us)
Async XLA Ops:
  0.6 11.1 %copy-start.1 = (f32[1,128,512]{2,1,0:T(8,128)S(1)}, f32[1,128,512]{2,1,0:T(8,128)}, u32[]{:S(2)}) copy-start(f32[1,128,512]{2,1,0:T(8,128)} %param.13) | copy-start | bytes 786436
  0.6 13.3 %collective-permute-start.3 = (f32[4,128,128]{2,1,0:T(8,128)}, f32[4,128,128]{2,1,0:T(8,128)S(1)}, u32[]{:S(2)}, u32[]{:S(2)}) collective-permute-start(f32[4,128,128]{2,1,0:T(8,128)} %bitcast.3), channel_id=1, source_target_pairs={{0,16},{16,32},{32,48},{48,64},{64,80},{80,96},{96,112},{112,128},... | collective-permute-start | bytes 786440 | tf_op jit(solution)/shard_map/ppermute | solution.py:411
  3.2 17.5 %copy-start = (f32[2,8,128]{2,1,0:T(8,128)S(1)}, f32[2,8,128]{2,1,0:T(8,128)}, u32[]{:S(2)}) copy-start(f32[2,8,128]{2,1,0:T(8,128)} %constant.30.refs_13_.refs_16_) | copy-start | bytes 24580
  6.3 14.4 %collective-permute-start = (f32[320,128]{1,0:T(8,128)S(1)}, f32[320,128]{1,0:T(8,128)S(1)}, u32[]{:S(2)}, u32[]{:S(2)}) collective-permute-start(f32[320,128]{1,0:T(8,128)S(1)} %get-tuple-element.43), channel_id=1, source_target_pairs={{0,2},{2,4},{4,6},{6,8},{8,10},{10,12},{12,14},{14,0},{1,3},{3,5},... | collective-permute-start | bytes 491528 | tf_op jit(solution)/shard_map/ppermute | solution.py:411
  8.4 12.3 %collective-permute-start.2 = (f32[64,512]{1,0:T(8,128)S(1)}, f32[64,512]{1,0:T(8,128)S(1)}, u32[]{:S(2)}, u32[]{:S(2)}) collective-permute-start(f32[64,512]{1,0:T(8,128)S(1)} %get-tuple-element.45), channel_id=1, source_target_pairs={{0,16},{16,32},{32,48},{48,64},{64,80},{80,96},{96,112},{112,128},... | collective-permute-start | bytes 393224 | tf_op jit(solution)/shard_map/ppermute | solution.py:411
  10.0 10.7 %collective-permute-start.1 = (f32[192,128]{1,0:T(8,128)S(1)}, f32[192,128]{1,0:T(8,128)S(1)}, u32[]{:S(2)}, u32[]{:S(2)}) collective-permute-start(f32[192,128]{1,0:T(8,128)S(1)} %get-tuple-element.44), channel_id=1, source_target_pairs={{0,18},{2,20},{4,22},{6,24},{8,26},{10,28},{12,30},{14,16},{16,34}... | collective-permute-start | bytes 294920 | tf_op jit(solution)/shard_map/ppermute | solution.py:411
  11.8 16.7 %collective-permute-start.4 = (f32[128,512]{1,0:T(8,128)S(1)}, f32[128,512]{1,0:T(8,128)S(1)}, u32[]{:S(2)}, u32[]{:S(2)}) collective-permute-start(f32[128,512]{1,0:T(8,128)S(1)} %bitcast.7), channel_id=1, source_target_pairs={{0,16},{16,32},{32,48},{48,64},{64,80},{80,96},{96,112},{112,128},... | collective-permute-start | bytes 786440 | tf_op jit(solution)/shard_map/ppermute | solution.py:411
  13.9 14.6 %collective-permute-start.5 = (f32[128,128]{1,0:T(8,128)S(1)}, f32[128,128]{1,0:T(8,128)S(1)}, u32[]{:S(2)}, u32[]{:S(2)}) collective-permute-start(f32[128,128]{1,0:T(8,128)S(1)} %get-tuple-element.60), channel_id=1, source_target_pairs={{0,18},{2,20},{4,22},{6,24},{8,26},{10,28},{12,30},{14,16},{16,34}... | collective-permute-start | bytes 196616 | tf_op jit(solution)/shard_map/ppermute | solution.py:411
  28.5 7.0 %collective-permute-start.6 = (f32[256,128]{1,0:T(8,128)S(1)}, f32[256,128]{1,0:T(8,128)S(1)}, u32[]{:S(2)}, u32[]{:S(2)}) collective-permute-start(f32[256,128]{1,0:T(8,128)S(1)} %get-tuple-element.61.refs_5_), channel_id=1, source_target_pairs={{0,2},{2,4},{4,6},{6,8},{8,10},{10,12},{12,14},{14,0},{1,3},{3,5},... | collective-permute-start | bytes 393224 | tf_op jit(solution)/shard_map/ppermute | solution.py:411
  29.3 6.3 %collective-permute-start.7 = (f32[256,128]{1,0:T(8,128)S(1)}, f32[256,128]{1,0:T(8,128)S(1)}, u32[]{:S(2)}, u32[]{:S(2)}) collective-permute-start(f32[256,128]{1,0:T(8,128)S(1)} %get-tuple-element.62.refs_4_), channel_id=1, source_target_pairs={{0,14},{2,0},{4,2},{6,4},{8,6},{10,8},{12,10},{14,12},{1,15},{3,1}... | collective-permute-start | bytes 393224 | tf_op jit(solution)/shard_map/ppermute | solution.py:411
  30.7 4.3 %collective-permute-start.10 = (f32[8,128]{1,0:T(8,128)S(1)}, f32[8,128]{1,0:T(8,128)S(1)}, u32[]{:S(2)}, u32[]{:S(2)}) collective-permute-start(f32[8,128]{1,0:T(8,128)S(1)} %get-tuple-element.65.refs_6_), channel_id=1, source_target_pairs={{0,48},{16,32},{32,16},{48,0},{64,112},{80,96},{96,80},{112,64},{1... | collective-permute-start | bytes 12296 | tf_op jit(solution)/shard_map/ppermute | solution.py:416
  30.7 4.3 %collective-permute-start.8 = (f32[8,128]{1,0:T(8,128)S(1)}, f32[8,128]{1,0:T(8,128)S(1)}, u32[]{:S(2)}, u32[]{:S(2)}) collective-permute-start(f32[8,128]{1,0:T(8,128)S(1)} %get-tuple-element.65.refs_6_), channel_id=1, source_target_pairs={{0,16},{16,0},{32,48},{48,32},{64,80},{80,64},{96,112},{112,96},{1... | collective-permute-start | bytes 12296 | tf_op jit(solution)/shard_map/ppermute | solution.py:416
  30.7 4.9 %collective-permute-start.9 = (f32[8,128]{1,0:T(8,128)S(1)}, f32[8,128]{1,0:T(8,128)S(1)}, u32[]{:S(2)}, u32[]{:S(2)}) collective-permute-start(f32[8,128]{1,0:T(8,128)S(1)} %get-tuple-element.65.refs_6_), channel_id=1, source_target_pairs={{0,32},{16,48},{32,0},{48,16},{64,96},{80,112},{96,64},{112,80},{1... | collective-permute-start | bytes 12296 | tf_op jit(solution)/shard_map/ppermute | solution.py:416
  36.8 19.9 %collective-permute-start.11 = (f32[128,640]{1,0:T(8,128)}, f32[128,640]{1,0:T(8,128)S(1)}, u32[]{:S(2)}, u32[]{:S(2)}) collective-permute-start(f32[128,640]{1,0:T(8,128)} %get-tuple-element.67.refs_2_), channel_id=1, source_target_pairs={{0,16},{16,32},{32,48},{48,64},{64,80},{80,96},{96,112},{112,128},... | collective-permute-start | bytes 983048 | tf_op jit(solution)/shard_map/ppermute | solution.py:411
  37.1 19.7 %collective-permute-start.12 = (f32[128,640]{1,0:T(8,128)}, f32[128,640]{1,0:T(8,128)S(1)}, u32[]{:S(2)}, u32[]{:S(2)}) collective-permute-start(f32[128,640]{1,0:T(8,128)} %get-tuple-element.66.refs_0_), channel_id=1, source_target_pairs={{0,240},{16,0},{32,16},{48,32},{64,48},{80,64},{96,80},{112,96},{1... | collective-permute-start | bytes 983048 | tf_op jit(solution)/shard_map/ppermute | solution.py:411
  65.3 8.4 %collective-permute-start.14 = (f32[64,512]{1,0:T(8,128)S(1)}, f32[64,512]{1,0:T(8,128)S(1)}, u32[]{:S(2)}, u32[]{:S(2)}) collective-permute-start(f32[64,512]{1,0:T(8,128)S(1)} %get-tuple-element.75), channel_id=1, source_target_pairs={{0,1},{1,0},{2,3},{3,2},{4,5},{5,4},{6,7},{7,6},{8,9},{9,8},{10,11... | collective-permute-start | bytes 393224 | tf_op jit(solution)/shard_map/ppermute | solution.py:416
  70.7 9.8 %collective-permute-start.13 = (f32[64,512]{1,0:T(8,128)S(1)}, f32[64,512]{1,0:T(8,128)S(1)}, u32[]{:S(2)}, u32[]{:S(2)}) collective-permute-start(f32[64,512]{1,0:T(8,128)S(1)} %get-tuple-element.74), channel_id=1, source_target_pairs={{0,240},{16,0},{32,16},{48,32},{64,48},{80,64},{96,80},{112,96},{1... | collective-permute-start | bytes 393224 | tf_op jit(solution)/shard_map/ppermute | solution.py:411
  70.8 9.1 %collective-permute-start.15 = (f32[64,128]{1,0:T(8,128)S(1)}, f32[64,128]{1,0:T(8,128)S(1)}, u32[]{:S(2)}, u32[]{:S(2)}) collective-permute-start(f32[64,128]{1,0:T(8,128)S(1)} %get-tuple-element.76), channel_id=1, source_target_pairs={{0,241},{1,240},{16,1},{17,0},{32,17},{33,16},{48,33},{49,32},{64,... | collective-permute-start | bytes 98312 | tf_op jit(solution)/shard_map/ppermute | solution.py:411
  70.8 13.8 %collective-permute-start.16 = (f32[64,384]{1,0:T(8,128)S(1)}, f32[64,384]{1,0:T(8,128)S(1)}, u32[]{:S(2)}, u32[]{:S(2)}) collective-permute-start(f32[64,384]{1,0:T(8,128)S(1)} %get-tuple-element.77), channel_id=1, source_target_pairs={{0,241},{1,240},{16,1},{17,0},{32,17},{33,16},{48,33},{49,32},{64,... | collective-permute-start | bytes 294920 | tf_op jit(solution)/shard_map/ppermute | solution.py:411
  80.6 4.0 %collective-permute-start.17 = (f32[128,64]{1,0:T(8,128)S(1)}, f32[128,64]{1,0:T(8,128)S(1)}, u32[]{:S(2)}, u32[]{:S(2)}) collective-permute-start(f32[128,64]{1,0:T(8,128)S(1)} %pad_maximum_fusion.1), channel_id=1, source_target_pairs={{0,14},{2,0},{4,2},{6,4},{8,6},{10,8},{12,10},{14,12},{1,15},{3,1}... | collective-permute-start | bytes 98312 | tf_op jit(solution)/shard_map/ppermute | solution.py:411

commit v9 on v8

--- a/solution.py
+++ b/solution.py
@@ -275,7 +275,7 @@
             together = together + block
         flux = flux + jnp.sum(together)
     lane = lax.broadcasted_iota(jnp.int32, flux_ref.shape, 1)
-    flux_ref[...] = jnp.where(lane < H, flux, t["total"][...])
+    flux_ref[...] = jnp.where(lane < H, flux, t["total"][:1])
     out.wait()
 
 
@@ -480,7 +480,7 @@
         functools.partial(model_kernel, tuple(named), tuple(ready)),
         named,
         ready,
-        [(pltpu.HBM, outs[0])] + [(pltpu.VMEM, o) for o in outs[1:] + [f32(8, S)]],
+        [(pltpu.HBM, outs[0])] + [(pltpu.VMEM, o) for o in outs[1:] + [f32(1, S)]],
         like(named) + [pltpu.SemaphoreType.DMA((len(named) + 1,)), pltpu.VMEM(outs[0].shape, F32)]
         + [pltpu.VMEM((2 * width, S), F32), pltpu.VMEM((6 * S, 2 * width + 2 * S), BF16),
            pltpu.VMEM((6 * L, 2 * width + 2 * S), BF16)],

time: 86.3 us -> 86.4 us (level)
  no operation moved by 1% of the time
where the time goes in v9:
time: 86.4 us; the launch traced here: 85.4 us
  starting transfers between devices  30.5 us (35%)
  Pallas kernels  22.6 us (26%)
  waiting for transfers between devices  16.2 us (19%)
  blocking collectives  14.3 us (17%)
  other arithmetic  1.07 us (1%)
    pallas_call x5, Pallas kernels, call(): pl.pallas_call(kernel, out_shape=[place(o.shape, o.dtype) for place, o in...  22.6 us
    ppermute x14, starting transfers between devices, ring(): return lax.ppermute(value, axes, pairs)  21.5 us
    ppermute x14, waiting for transfers between devices, ring(): return lax.ppermute(value, axes, pairs)  14.6 us
    all_to_all x1, blocking collectives, exchanged(): return lax.all_to_all(value, ('sy', 'sx'), 0, 0, axis_index_groups=groups)  14.3 us
    ppermute x4, starting transfers between devices, mirrored(): return lax.ppermute(value, axis, [(s, s ^ bits) for s in range(count)])  8.97 us
  transfers between devices with their start and end apart: 18, of which 9 were waited for; matrix products, arithmetic and copies ran while one was open for 0% of the time, Pallas kernels for 15%

profile of v9, /device:TPU:1, one launch (start us, length us, event | category | flops | bytes accessed | tf_op | source)
XLA Modules:
  0.0 85.4 jit_solution(1546369483655880942)
XLA Ops:
  0.6 0.0 copy-start.1
  0.6 2.5 %collective-permute-start.3 = (f32[4,128,128]{2,1,0:T(8,128)}, f32[4,128,128]{2,1,0:T(8,128)S(1)}, u32[]{:S(2)}, u32[]{:S(2)}) collective-permute-start(f32[4,128,128]{2,1,0:T(8,128)} %bitcast.3), channel_id=1, source_target_pairs={{0,16},{16,32},{32,48},{48,64},{64,80},{80,96},{96,112},{112,128},... | collective-permute-start | bytes 786440 | tf_op jit(solution)/shard_map/ppermute | solution.py:411
  3.2 3.1 %shard_map.131 = (f32[64,512]{1,0:T(8,128)S(1)}, f32[320,128]{1,0:T(8,128)S(1)}, f32[192,128]{1,0:T(8,128)S(1)}, f32[128,128]{1,0:T(8,128)S(1)}, f32[512,512]{1,...) custom-call(f32[4,128,128]{2,1,0:T(8,128)} %bitcast.4, ...), custom_call_target="tpu_custom_call" | custom-call | flops 504000000 | bytes 6111232 | tf_op jit(solution)/shard_map/pallas_call | solution.py:388
  6.3 2.1 %collective-permute-start = (f32[320,128]{1,0:T(8,128)S(1)}, f32[320,128]{1,0:T(8,128)S(1)}, u32[]{:S(2)}, u32[]{:S(2)}) collective-permute-start(f32[320,128]{1,0:T(8,128)S(1)} %get-tuple-element.43), channel_id=1, source_target_pairs={{0,2},{2,4},{4,6},{6,8},{8,10},{10,12},{12,14},{14,0},{1,3},{3,5},... | collective-permute-start | bytes 491528 | tf_op jit(solution)/shard_map/ppermute | solution.py:411
  8.4 1.6 %collective-permute-start.2 = (f32[64,512]{1,0:T(8,128)S(1)}, f32[64,512]{1,0:T(8,128)S(1)}, u32[]{:S(2)}, u32[]{:S(2)}) collective-permute-start(f32[64,512]{1,0:T(8,128)S(1)} %get-tuple-element.45), channel_id=1, source_target_pairs={{0,16},{16,32},{32,48},{48,64},{64,80},{80,96},{96,112},{112,128},... | collective-permute-start | bytes 393224 | tf_op jit(solution)/shard_map/ppermute | solution.py:411
  10.0 1.7 %collective-permute-start.1 = (f32[192,128]{1,0:T(8,128)S(1)}, f32[192,128]{1,0:T(8,128)S(1)}, u32[]{:S(2)}, u32[]{:S(2)}) collective-permute-start(f32[192,128]{1,0:T(8,128)S(1)} %get-tuple-element.44), channel_id=1, source_target_pairs={{0,18},{2,20},{4,22},{6,24},{8,26},{10,28},{12,30},{14,16},{16,34}... | collective-permute-start | bytes 294920 | tf_op jit(solution)/shard_map/ppermute | solution.py:411
  11.8 2.1 %collective-permute-done.3.psf_hbm = f32[4,128,128]{2,1,0:T(8,128)S(1)} collective-permute-done((f32[4,128,128]{2,1,0:T(8,128)}, f32[4,128,128]{2,1,0:T(8,128)S(1)}, u32[]{:S(2)}, u32[]{:S(2)}) %collective-permute-start.3) | collective-permute-done | bytes 262176 | tf_op jit(solution)/shard_map/ppermute | solution.py:411
  13.9 0.8 collective-permute-start.5
  14.7 1.9 %shard_map.132 = (f32[512,512]{1,0:T(8,128)}, f32[512,512]{1,0:T(8,128)S(1)}) custom-call(f32[4,128,128]{2,1,0:T(8,128)S(1)} %collective-permute-done.3.psf_hbm, bf16[384,256]{1,0:T(8,128)(2,1)S(1)} %get-tuple-element.46.right.refs_4_, bf16[512,768]{1,0:T(8,128)(2,1)S(1)} %get-tuple-element.47.left.refs_5_), custom_call_target="tpu_custom_call" | custom-call | flops 504000000 | bytes 262144 | tf_op jit(solution)/shard_map/pallas_call | solution.py:388
  16.6 4.1 %collective-permute-done.1.refs_1_ = f32[192,128]{1,0:T(8,128)S(1)} collective-permute-done((f32[192,128]{1,0:T(8,128)S(1)}, f32[192,128]{1,0:T(8,128)S(1)}, u32[]{:S(2)}, u32[]{:S(2)}) %collective-permute-start.1) | collective-permute-done | bytes 98336 | tf_op jit(solution)/shard_map/ppermute | solution.py:411
  20.7 7.8 %shard_map.133 = (f32[512,256]{1,0:T(8,128)}, f32[128,384]{1,0:T(8,128)S(1)}, f32[128,384]{1,0:T(8,128)S(1)}, f32[256,128]{1,0:T(8,128)S(1)}, f32[256,128]{1,0:T(8,128)S(1)}, /*index=5*/f32[1,128]{1,0:T(1,128)S(1)}) custom-call(f32[320,128]{1,0:T(8,128)S(1)} %collective-permute-done.refs_0_.refs_7_, f32[192,128]{1,0:T(8,128)S(1)} %collective-permute-done.1.refs_1_, ...), custom_call_target="tpu_custom_call" | custom-call | flops 3600000000 | bytes 655360 | tf_op jit(solution)/shard_map/pallas_call | solution.py:388
  28.5 0.8 collective-permute-start.6
  29.3 1.4 %collective-permute-start.7 = (f32[256,128]{1,0:T(8,128)S(1)}, f32[256,128]{1,0:T(8,128)S(1)}, u32[]{:S(2)}, u32[]{:S(2)}) collective-permute-start(f32[256,128]{1,0:T(8,128)S(1)} %get-tuple-element.62.refs_4_), channel_id=1, source_target_pairs={{0,14},{2,0},{4,2},{6,4},{8,6},{10,8},{12,10},{14,12},{1,15},{3,1}... | collective-permute-start | bytes 393224 | tf_op jit(solution)/shard_map/ppermute | solution.py:411
  30.7 3.5 %collective-permute-start.9 = (f32[1,128]{1,0:T(1,128)S(1)}, f32[1,128]{1,0:T(1,128)S(1)}, u32[]{:S(2)}, u32[]{:S(2)}) collective-permute-start(f32[1,128]{1,0:T(1,128)S(1)} %get-tuple-element.65.refs_6_), channel_id=1, source_target_pairs={{0,32},{16,48},{32,0},{48,16},{64,96},{80,112},{96,64},{112,80},{1... | collective-permute-start | bytes 1544 | tf_op jit(solution)/shard_map/ppermute | solution.py:416
  34.2 0.7 collective-permute-done.10.refs_9_
  34.9 0.6 collective-permute-done.9.refs_8_
  35.4 1.2 %shard_map.134 = (f32[128,640]{1,0:T(8,128)}, f32[128,640]{1,0:T(8,128)}, f32[32,1,128]{2,1,0:T(1,128)S(1)}) custom-call(f32[256,128]{1,0:T(8,128)S(1)} %collective-permute-done.6.refs_0_, f32[256,128]{1,0:T(8,128)S(1)} %collective-permute-done.7.refs_1_, f32[128,384]{1,0:T(8,128)S(1)} %get-tuple-element.63.refs_2_, ...), custom_call_target="tpu_custom_call" | custom-call | flops 1000000 | bytes 262144 | tf_op jit(solution)/shard_map/pallas_call | solution.py:388
  36.7 0.3 collective-permute-start.11
  37.0 5.4 %collective-permute-start.12 = (f32[128,640]{1,0:T(8,128)}, f32[128,640]{1,0:T(8,128)S(1)}, u32[]{:S(2)}, u32[]{:S(2)}) collective-permute-start(f32[128,640]{1,0:T(8,128)} %get-tuple-element.66.refs_0_), channel_id=1, source_target_pairs={{0,240},{16,0},{32,16},{48,32},{64,48},{80,64},{96,80},{112,96},{1... | collective-permute-start | bytes 983048 | tf_op jit(solution)/shard_map/ppermute | solution.py:411
  42.3 14.3 %all_to_all.5.refs_17_ = f32[32,1,128]{2,1,0:T(1,128)S(1)} all-to-all(f32[32,1,128]{2,1,0:T(1,128)S(1)} %get-tuple-element.73), channel_id=1, replica_groups={{0,2,4,6,8,10,12,14,64,66,68,70,72,74,76,78,128,130,132,134,136,138,140..., dimensions={0} | all-to-all | bytes 32768 | tf_op jit(solution)/shard_map/all_to_all | solution.py:428
  56.6 8.6 %shard_map.135 = (f32[128,512]{1,0:T(8,128)}, f32[64,512]{1,0:T(8,128)S(1)}, f32[64,512]{1,0:T(8,128)S(1)}, f32[64,128]{1,0:T(8,128)S(1)}, f32[64,384]{1,0:T(8,128)S(1)}) custom-call(f32[128,640]{1,0:T(8,128)} %get-tuple-element.66.refs_0_, f32[128,640]{1,0:T(8,128)S(1)} %collective-permute-done.11.refs_1_, f32[128,640]{1,0:T(8,128)} %get-tuple-element.67.refs_2_, ...), custom_call_target="tpu_custom_call" | custom-call | flops 3000000000 | bytes 9232384 | tf_op jit(solution)/shard_map/pallas_call | solution.py:388
  65.2 5.4 %collective-permute-start.14 = (f32[64,512]{1,0:T(8,128)S(1)}, f32[64,512]{1,0:T(8,128)S(1)}, u32[]{:S(2)}, u32[]{:S(2)}) collective-permute-start(f32[64,512]{1,0:T(8,128)S(1)} %get-tuple-element.75), channel_id=1, source_target_pairs={{0,1},{1,0},{2,3},{3,2},{4,5},{5,4},{6,7},{7,6},{8,9},{9,8},{10,11... | collective-permute-start | bytes 393224 | tf_op jit(solution)/shard_map/ppermute | solution.py:416
  70.6 2.6 %collective-permute-start.16 = (f32[64,384]{1,0:T(8,128)S(1)}, f32[64,384]{1,0:T(8,128)S(1)}, u32[]{:S(2)}, u32[]{:S(2)}) collective-permute-start(f32[64,384]{1,0:T(8,128)S(1)} %get-tuple-element.77), channel_id=1, source_target_pairs={{0,241},{1,240},{16,1},{17,0},{32,17},{33,16},{48,33},{49,32},{64,... | collective-permute-start | bytes 294920 | tf_op jit(solution)/shard_map/ppermute | solution.py:411
  73.3 0.3 collective-permute-done.14
  73.6 6.1 %collective-permute-done.15 = f32[64,128]{1,0:T(8,128)S(1)} collective-permute-done((f32[64,128]{1,0:T(8,128)S(1)}, f32[64,128]{1,0:T(8,128)S(1)}, u32[]{:S(2)}, u32[]{:S(2)}) %collective-permute-start.15) | collective-permute-done | bytes 32800 | tf_op jit(solution)/shard_map/ppermute | solution.py:411
  79.8 0.7 collective-permute-done.13
  80.4 0.1 slice_add_fusion.2
  80.5 2.3 %collective-permute-start.17 = (f32[128,64]{1,0:T(8,128)S(1)}, f32[128,64]{1,0:T(8,128)S(1)}, u32[]{:S(2)}, u32[]{:S(2)}) collective-permute-start(f32[128,64]{1,0:T(8,128)S(1)} %pad_maximum_fusion.1), channel_id=1, source_target_pairs={{0,14},{2,0},{4,2},{6,4},{8,6},{10,8},{12,10},{14,12},{1,15},{3,1}... | collective-permute-start | bytes 98312 | tf_op jit(solution)/shard_map/ppermute | solution.py:411
  82.9 0.1 slice_add_fusion
  83.0 1.4 %collective-permute-done.16 = f32[64,384]{1,0:T(8,128)S(1)} collective-permute-done((f32[64,384]{1,0:T(8,128)S(1)}, f32[64,384]{1,0:T(8,128)S(1)}, u32[]{:S(2)}, u32[]{:S(2)}) %collective-permute-start.16) | collective-permute-done | bytes 98336 | tf_op jit(solution)/shard_map/ppermute | solution.py:411
  84.4 0.1 collective-permute-done.17
  84.6 0.8 pad_maximum_fusion
  (20 shorter events, 0.1 us)
Async XLA Ops:
  0.6 11.1 %copy-start.1 = (f32[1,128,512]{2,1,0:T(8,128)S(1)}, f32[1,128,512]{2,1,0:T(8,128)}, u32[]{:S(2)}) copy-start(f32[1,128,512]{2,1,0:T(8,128)} %param.13) | copy-start | bytes 786436
  0.6 13.3 %collective-permute-start.3 = (f32[4,128,128]{2,1,0:T(8,128)}, f32[4,128,128]{2,1,0:T(8,128)S(1)}, u32[]{:S(2)}, u32[]{:S(2)}) collective-permute-start(f32[4,128,128]{2,1,0:T(8,128)} %bitcast.3), channel_id=1, source_target_pairs={{0,16},{16,32},{32,48},{48,64},{64,80},{80,96},{96,112},{112,128},... | collective-permute-start | bytes 786440 | tf_op jit(solution)/shard_map/ppermute | solution.py:411
  3.2 17.5 %copy-start = (f32[2,8,128]{2,1,0:T(8,128)S(1)}, f32[2,8,128]{2,1,0:T(8,128)}, u32[]{:S(2)}) copy-start(f32[2,8,128]{2,1,0:T(8,128)} %constant.30.refs_13_.refs_16_) | copy-start | bytes 24580
  6.3 14.4 %collective-permute-start = (f32[320,128]{1,0:T(8,128)S(1)}, f32[320,128]{1,0:T(8,128)S(1)}, u32[]{:S(2)}, u32[]{:S(2)}) collective-permute-start(f32[320,128]{1,0:T(8,128)S(1)} %get-tuple-element.43), channel_id=1, source_target_pairs={{0,2},{2,4},{4,6},{6,8},{8,10},{10,12},{12,14},{14,0},{1,3},{3,5},... | collective-permute-start | bytes 491528 | tf_op jit(solution)/shard_map/ppermute | solution.py:411
  8.4 12.3 %collective-permute-start.2 = (f32[64,512]{1,0:T(8,128)S(1)}, f32[64,512]{1,0:T(8,128)S(1)}, u32[]{:S(2)}, u32[]{:S(2)}) collective-permute-start(f32[64,512]{1,0:T(8,128)S(1)} %get-tuple-element.45), channel_id=1, source_target_pairs={{0,16},{16,32},{32,48},{48,64},{64,80},{80,96},{96,112},{112,128},... | collective-permute-start | bytes 393224 | tf_op jit(solution)/shard_map/ppermute | solution.py:411
  10.0 10.7 %collective-permute-start.1 = (f32[192,128]{1,0:T(8,128)S(1)}, f32[192,128]{1,0:T(8,128)S(1)}, u32[]{:S(2)}, u32[]{:S(2)}) collective-permute-start(f32[192,128]{1,0:T(8,128)S(1)} %get-tuple-element.44), channel_id=1, source_target_pairs={{0,18},{2,20},{4,22},{6,24},{8,26},{10,28},{12,30},{14,16},{16,34}... | collective-permute-start | bytes 294920 | tf_op jit(solution)/shard_map/ppermute | solution.py:411
  11.8 16.7 %collective-permute-start.4 = (f32[128,512]{1,0:T(8,128)S(1)}, f32[128,512]{1,0:T(8,128)S(1)}, u32[]{:S(2)}, u32[]{:S(2)}) collective-permute-start(f32[128,512]{1,0:T(8,128)S(1)} %bitcast.7), channel_id=1, source_target_pairs={{0,16},{16,32},{32,48},{48,64},{64,80},{80,96},{96,112},{112,128},... | collective-permute-start | bytes 786440 | tf_op jit(solution)/shard_map/ppermute | solution.py:411
  13.9 14.6 %collective-permute-start.5 = (f32[128,128]{1,0:T(8,128)S(1)}, f32[128,128]{1,0:T(8,128)S(1)}, u32[]{:S(2)}, u32[]{:S(2)}) collective-permute-start(f32[128,128]{1,0:T(8,128)S(1)} %get-tuple-element.60), channel_id=1, source_target_pairs={{0,18},{2,20},{4,22},{6,24},{8,26},{10,28},{12,30},{14,16},{16,34}... | collective-permute-start | bytes 196616 | tf_op jit(solution)/shard_map/ppermute | solution.py:411
  28.5 6.9 %collective-permute-start.6 = (f32[256,128]{1,0:T(8,128)S(1)}, f32[256,128]{1,0:T(8,128)S(1)}, u32[]{:S(2)}, u32[]{:S(2)}) collective-permute-start(f32[256,128]{1,0:T(8,128)S(1)} %get-tuple-element.61.refs_5_), channel_id=1, source_target_pairs={{0,2},{2,4},{4,6},{6,8},{8,10},{10,12},{12,14},{14,0},{1,3},{3,5},... | collective-permute-start | bytes 393224 | tf_op jit(solution)/shard_map/ppermute | solution.py:411
  29.3 6.2 %collective-permute-start.7 = (f32[256,128]{1,0:T(8,128)S(1)}, f32[256,128]{1,0:T(8,128)S(1)}, u32[]{:S(2)}, u32[]{:S(2)}) collective-permute-start(f32[256,128]{1,0:T(8,128)S(1)} %get-tuple-element.62.refs_4_), channel_id=1, source_target_pairs={{0,14},{2,0},{4,2},{6,4},{8,6},{10,8},{12,10},{14,12},{1,15},{3,1}... | collective-permute-start | bytes 393224 | tf_op jit(solution)/shard_map/ppermute | solution.py:411
  30.7 4.2 %collective-permute-start.10 = (f32[1,128]{1,0:T(1,128)S(1)}, f32[1,128]{1,0:T(1,128)S(1)}, u32[]{:S(2)}, u32[]{:S(2)}) collective-permute-start(f32[1,128]{1,0:T(1,128)S(1)} %get-tuple-element.65.refs_6_), channel_id=1, source_target_pairs={{0,48},{16,32},{32,16},{48,0},{64,112},{80,96},{96,80},{112,64},{1... | collective-permute-start | bytes 1544 | tf_op jit(solution)/shard_map/ppermute | solution.py:416
  30.7 4.2 %collective-permute-start.8 = (f32[1,128]{1,0:T(1,128)S(1)}, f32[1,128]{1,0:T(1,128)S(1)}, u32[]{:S(2)}, u32[]{:S(2)}) collective-permute-start(f32[1,128]{1,0:T(1,128)S(1)} %get-tuple-element.65.refs_6_), channel_id=1, source_target_pairs={{0,16},{16,0},{32,48},{48,32},{64,80},{80,64},{96,112},{112,96},{1... | collective-permute-start | bytes 1544 | tf_op jit(solution)/shard_map/ppermute | solution.py:416
  30.7 4.8 %collective-permute-start.9 = (f32[1,128]{1,0:T(1,128)S(1)}, f32[1,128]{1,0:T(1,128)S(1)}, u32[]{:S(2)}, u32[]{:S(2)}) collective-permute-start(f32[1,128]{1,0:T(1,128)S(1)} %get-tuple-element.65.refs_6_), channel_id=1, source_target_pairs={{0,32},{16,48},{32,0},{48,16},{64,96},{80,112},{96,64},{112,80},{1... | collective-permute-start | bytes 1544 | tf_op jit(solution)/shard_map/ppermute | solution.py:416
  36.7 19.9 %collective-permute-start.11 = (f32[128,640]{1,0:T(8,128)}, f32[128,640]{1,0:T(8,128)S(1)}, u32[]{:S(2)}, u32[]{:S(2)}) collective-permute-start(f32[128,640]{1,0:T(8,128)} %get-tuple-element.67.refs_2_), channel_id=1, source_target_pairs={{0,16},{16,32},{32,48},{48,64},{64,80},{80,96},{96,112},{112,128},... | collective-permute-start | bytes 983048 | tf_op jit(solution)/shard_map/ppermute | solution.py:411
  37.0 19.7 %collective-permute-start.12 = (f32[128,640]{1,0:T(8,128)}, f32[128,640]{1,0:T(8,128)S(1)}, u32[]{:S(2)}, u32[]{:S(2)}) collective-permute-start(f32[128,640]{1,0:T(8,128)} %get-tuple-element.66.refs_0_), channel_id=1, source_target_pairs={{0,240},{16,0},{32,16},{48,32},{64,48},{80,64},{96,80},{112,96},{1... | collective-permute-start | bytes 983048 | tf_op jit(solution)/shard_map/ppermute | solution.py:411
  65.2 8.4 %collective-permute-start.14 = (f32[64,512]{1,0:T(8,128)S(1)}, f32[64,512]{1,0:T(8,128)S(1)}, u32[]{:S(2)}, u32[]{:S(2)}) collective-permute-start(f32[64,512]{1,0:T(8,128)S(1)} %get-tuple-element.75), channel_id=1, source_target_pairs={{0,1},{1,0},{2,3},{3,2},{4,5},{5,4},{6,7},{7,6},{8,9},{9,8},{10,11... | collective-permute-start | bytes 393224 | tf_op jit(solution)/shard_map/ppermute | solution.py:416
  70.6 9.8 %collective-permute-start.13 = (f32[64,512]{1,0:T(8,128)S(1)}, f32[64,512]{1,0:T(8,128)S(1)}, u32[]{:S(2)}, u32[]{:S(2)}) collective-permute-start(f32[64,512]{1,0:T(8,128)S(1)} %get-tuple-element.74), channel_id=1, source_target_pairs={{0,240},{16,0},{32,16},{48,32},{64,48},{80,64},{96,80},{112,96},{1... | collective-permute-start | bytes 393224 | tf_op jit(solution)/shard_map/ppermute | solution.py:411
  70.6 9.1 %collective-permute-start.15 = (f32[64,128]{1,0:T(8,128)S(1)}, f32[64,128]{1,0:T(8,128)S(1)}, u32[]{:S(2)}, u32[]{:S(2)}) collective-permute-start(f32[64,128]{1,0:T(8,128)S(1)} %get-tuple-element.76), channel_id=1, source_target_pairs={{0,241},{1,240},{16,1},{17,0},{32,17},{33,16},{48,33},{49,32},{64,... | collective-permute-start | bytes 98312 | tf_op jit(solution)/shard_map/ppermute | solution.py:411
  70.6 13.8 %collective-permute-start.16 = (f32[64,384]{1,0:T(8,128)S(1)}, f32[64,384]{1,0:T(8,128)S(1)}, u32[]{:S(2)}, u32[]{:S(2)}) collective-permute-start(f32[64,384]{1,0:T(8,128)S(1)} %get-tuple-element.77), channel_id=1, source_target_pairs={{0,241},{1,240},{16,1},{17,0},{32,17},{33,16},{48,33},{49,32},{64,... | collective-permute-start | bytes 294920 | tf_op jit(solution)/shard_map/ppermute | solution.py:411
  80.5 4.0 %collective-permute-start.17 = (f32[128,64]{1,0:T(8,128)S(1)}, f32[128,64]{1,0:T(8,128)S(1)}, u32[]{:S(2)}, u32[]{:S(2)}) collective-permute-start(f32[128,64]{1,0:T(8,128)S(1)} %pad_maximum_fusion.1), channel_id=1, source_target_pairs={{0,14},{2,0},{4,2},{6,4},{8,6},{10,8},{12,10},{14,12},{1,15},{3,1}... | collective-permute-start | bytes 98312 | tf_op jit(solution)/shard_map/ppermute | solution.py:411
